TPU v7x, 32 devices: a whole 2x2x4 slice. The times are simulated.
32 devices in a mesh: grp: 2 (over core), gx: 8 (over z, y), gy: 2 (over x).
Axes of the slice: x: 2, y: 2, z: 4, core: 2. Of those that a mesh axis runs over, the one named last changes fastest.
Arguments:
- source: bfloat16 [4, 64, 128, 256], P(None, None, ('grp', 'gx'), 'gy'), may hold values from -6 to 6
- speed: bfloat16 [64, 128, 256], P(('grp', 'gx'), None, 'gy'), may hold values from 1 to 2.5
- impedance: bfloat16 [64, 128, 256], P(('grp', 'gx'), None, 'gy'), may hold values from 0.5 to 2
Outputs:
- pressure: float32 [64, 128, 256], P(('grp', 'gx'), None, 'gy')
- velocity: float32 [3, 64, 128, 256], P(None, ('grp', 'gx'), None, 'gy')
All inputs are finite; a program needn't handle non-finite values.
Results may differ from a plain program's by a relative error of at most 0.0017.
Values may be sent and summed in bfloat16 or wider, within the bound.
No kernel may reach another device: no remote copies, remote signals or barrier semaphores. Data moves between devices by JAX's collectives and lax.ppermute only.
A program may use at most 128 MiB of HBM per device.

v0:
```python
import jax
import jax.numpy as jnp
from jax import lax
from jax.sharding import PartitionSpec as P

courant = 0.15


def shortened(x):
    return jax.tree.map(lambda a: a.astype(jnp.bfloat16) if a.dtype == jnp.float32 else a, x)


def passed_along(block, axis, distance):
    devices = range(lax.axis_size(axis))
    route = [(i - distance, i) for i in devices if i - distance in devices]
    return lax.ppermute(block, axis, route)


def forward_diff(field, dim):
    widths = [(0, 0)] * field.ndim
    widths[dim] = (0, 1)
    padded = jnp.pad(field, widths)
    return lax.slice_in_dim(padded, 1, field.shape[dim] + 1, axis=dim) - field


def backward_diff(field, dim):
    widths = [(0, 0)] * field.ndim
    widths[dim] = (1, 0)
    padded = jnp.pad(field, widths)
    return field - lax.slice_in_dim(padded, 0, field.shape[dim], axis=dim)


def on_device(source, speed, impedance):
    count, whole_x, brick_y, depth = source.shape
    acoustic = lax.all_to_all(source, ("grp", "gx"), split_axis=1, concat_axis=2, tiled=True)
    sound = speed.astype(jnp.float32)
    imped = impedance.astype(jnp.float32)
    stiff = sound * imped
    buoy = sound / imped
    pressure = jnp.zeros(speed.shape, jnp.float32)
    vel_x = jnp.zeros(speed.shape, jnp.float32)
    vel_y = jnp.zeros(speed.shape, jnp.float32)
    vel_z = jnp.zeros(speed.shape, jnp.float32)
    for step in range(count):
        pressure = pressure + acoustic[count - 1 - step].astype(jnp.float32)
        loaded = stiff * pressure
        above_x = passed_along(shortened(loaded[0:1]), ("grp", "gx"), -1)
        above_z = passed_along(loaded[:, :, 0:1], "gy", -1)
        vel_x = vel_x + courant * (jnp.concatenate([loaded[1:], above_x], 0) - loaded)
        vel_y = vel_y + courant * forward_diff(loaded, 1)
        vel_z = vel_z + courant * (jnp.concatenate([loaded[:, :, 1:], above_z], 2) - loaded)
        flux_x = buoy * vel_x
        flux_y = buoy * vel_y
        flux_z = buoy * vel_z
        below_x = passed_along(shortened(flux_x[-1:]), ("grp", "gx"), 1)
        below_z = passed_along(flux_z[:, :, -1:], "gy", 1)
        spread = flux_x - jnp.concatenate([below_x, flux_x[:-1]], 0)
        spread = spread + backward_diff(flux_y, 1)
        spread = spread + flux_z - jnp.concatenate([below_z, flux_z[:, :, :-1]], 2)
        pressure = pressure + courant * spread
    return (pressure, jnp.stack([vel_x, vel_y, vel_z]))


def solution(mesh):
    in_specs = (
        P(None, None, ("grp", "gx"), "gy"),
        P(("grp", "gx"), None, "gy"),
        P(("grp", "gx"), None, "gy"),
    )
    out_specs = (P(("grp", "gx"), None, "gy"), P(None, ("grp", "gx"), None, "gy"))
    return jax.shard_map(
        on_device, mesh=mesh, in_specs=in_specs, out_specs=out_specs, check_vma=False
    )
```

profile of v0, /device:TPU:0, one launch (start us, length us, event | category | flops | bytes accessed | tf_op | source)
XLA Modules:
  0.0 115.2 jit_solution(3087344587487920677)
XLA Ops:
  0.6 1.1 copy.6
  1.8 23.0 %all_to_all.15 = bf16[4,64,8,128]{3,2,0,1:T(8,128)(2,1)S(1)} all-to-all(bf16[4,64,8,128]{3,2,0,1:T(8,128)(2,1)S(1)} %copy.6), channel_id=1, replica_groups=mesh['grp'=2,'gx'=8,'gy'=2] {'grp','gx'}, dimensions={1} | all-to-all | bytes 1048576 | tf_op jit(solution)/shard_map/all_to_all | solution.py:35
  24.9 0.8 copy-done
  25.8 1.3 %collective-permute-start = (bf16[1,128,128]{2,1,0:T(8,128)(2,1)S(1)}, bf16[1,128,128]{2,1,0:T(8,128)(2,1)S(1)}, u32[]{:S(2)}, u32[]{:S(2)}) collective-permute-start(bf16[1,128,128]{2,1,0:T(8,128)(2,1)S(1)} %slice.335), channel_id=1, source_target_pairs={{2,0},{4,2},{6,4},{8,6},{10,8},{12,10},{14,12},{16,14},{18,16},{20... | collective-permute-start | bytes 98312 | tf_op jit(solution)/shard_map/ppermute | solution.py:16
  27.1 1.3 %collective-permute-start.2 = (f32[4,128,1]{2,1,0:T(8,128)S(1)}, f32[4,128,1]{2,1,0:T(8,128)S(1)}, u32[]{:S(2)}, u32[]{:S(2)}) collective-permute-start(f32[4,128,1]{2,1,0:T(8,128)S(1)} %bitcast.29), channel_id=1, source_target_pairs={{1,0},{3,2},{5,4},{7,6},{9,8},{11,10},{13,12},{15,14},{17,16},{19,... | collective-permute-start | bytes 6152 | tf_op jit(solution)/shard_map/ppermute | solution.py:16
  28.4 0.1 slice.193
  28.5 3.1 %collective-permute-done = bf16[1,128,128]{2,1,0:T(8,128)(2,1)S(1)} collective-permute-done((bf16[1,128,128]{2,1,0:T(8,128)(2,1)S(1)}, bf16[1,128,128]{2,1,0:T(8,128)(2,1)S(1)}, u32[]{:S(2)}, u32[]{:S(2)}) %collective-permute-start) | collective-permute-done | bytes 32800 | tf_op jit(solution)/shard_map/ppermute | solution.py:16
  31.6 6.0 %collective-permute-done.2 = f32[4,128,1]{2,1,0:T(8,128)S(1)} collective-permute-done((f32[4,128,1]{2,1,0:T(8,128)S(1)}, f32[4,128,1]{2,1,0:T(8,128)S(1)}, u32[]{:S(2)}, u32[]{:S(2)}) %collective-permute-start.2) | collective-permute-done | bytes 2080 | tf_op jit(solution)/shard_map/ppermute | solution.py:16
  37.6 0.2 fusion.56
  37.8 2.9 %collective-permute-start.1 = (bf16[1,128,128]{2,1,0:T(8,128)(2,1)S(1)}, bf16[1,128,128]{2,1,0:T(8,128)(2,1)S(1)}, u32[]{:S(2)}, u32[]{:S(2)}) collective-permute-start(bf16[1,128,128]{2,1,0:T(8,128)(2,1)S(1)} %slice.334), channel_id=1, source_target_pairs={{0,2},{2,4},{4,6},{6,8},{8,10},{10,12},{12,14},{14,16},{16,18},{18... | collective-permute-start | bytes 98312 | tf_op jit(solution)/shard_map/ppermute | solution.py:16
  40.7 0.1 slice.195
  40.8 1.5 %collective-permute-start.3 = (f32[4,128,1]{2,1,0:T(8,128)S(1)}, f32[4,128,1]{2,1,0:T(8,128)S(1)}, u32[]{:S(2)}, u32[]{:S(2)}) collective-permute-start(f32[4,128,1]{2,1,0:T(8,128)S(1)} %slice.195), channel_id=1, source_target_pairs={{0,1},{2,3},{4,5},{6,7},{8,9},{10,11},{12,13},{14,15},{16,17},{18,... | collective-permute-start | bytes 6152 | tf_op jit(solution)/shard_map/ppermute | solution.py:16
  42.3 5.4 %collective-permute-done.3 = f32[4,128,1]{2,1,0:T(8,128)S(1)} collective-permute-done((f32[4,128,1]{2,1,0:T(8,128)S(1)}, f32[4,128,1]{2,1,0:T(8,128)S(1)}, u32[]{:S(2)}, u32[]{:S(2)}) %collective-permute-start.3) | collective-permute-done | bytes 2080 | tf_op jit(solution)/shard_map/ppermute | solution.py:16
  47.7 0.2 fusion.54
  47.9 1.3 %collective-permute-start.4 = (bf16[1,128,128]{2,1,0:T(8,128)(2,1)S(1)}, bf16[1,128,128]{2,1,0:T(8,128)(2,1)S(1)}, u32[]{:S(2)}, u32[]{:S(2)}) collective-permute-start(bf16[1,128,128]{2,1,0:T(8,128)(2,1)S(1)} %slice.333), channel_id=1, source_target_pairs={{2,0},{4,2},{6,4},{8,6},{10,8},{12,10},{14,12},{16,14},{18,16},{20... | collective-permute-start | bytes 98312 | tf_op jit(solution)/shard_map/ppermute | solution.py:16
  49.2 1.3 %collective-permute-start.6 = (f32[4,128,1]{2,1,0:T(8,128)S(1)}, f32[4,128,1]{2,1,0:T(8,128)S(1)}, u32[]{:S(2)}, u32[]{:S(2)}) collective-permute-start(f32[4,128,1]{2,1,0:T(8,128)S(1)} %bitcast.36), channel_id=1, source_target_pairs={{1,0},{3,2},{5,4},{7,6},{9,8},{11,10},{13,12},{15,14},{17,16},{19,... | collective-permute-start | bytes 6152 | tf_op jit(solution)/shard_map/ppermute | solution.py:16
  50.5 0.1 slice.202
  50.7 3.1 %collective-permute-done.4 = bf16[1,128,128]{2,1,0:T(8,128)(2,1)S(1)} collective-permute-done((bf16[1,128,128]{2,1,0:T(8,128)(2,1)S(1)}, bf16[1,128,128]{2,1,0:T(8,128)(2,1)S(1)}, u32[]{:S(2)}, u32[]{:S(2)}) %collective-permute-start.4) | collective-permute-done | bytes 32800 | tf_op jit(solution)/shard_map/ppermute | solution.py:16
  53.7 4.1 %collective-permute-done.6 = f32[4,128,1]{2,1,0:T(8,128)S(1)} collective-permute-done((f32[4,128,1]{2,1,0:T(8,128)S(1)}, f32[4,128,1]{2,1,0:T(8,128)S(1)}, u32[]{:S(2)}, u32[]{:S(2)}) %collective-permute-start.6) | collective-permute-done | bytes 2080 | tf_op jit(solution)/shard_map/ppermute | solution.py:16
  57.9 0.3 fusion.68
  58.2 4.7 %collective-permute-start.5 = (bf16[1,128,128]{2,1,0:T(8,128)(2,1)S(1)}, bf16[1,128,128]{2,1,0:T(8,128)(2,1)S(1)}, u32[]{:S(2)}, u32[]{:S(2)}) collective-permute-start(bf16[1,128,128]{2,1,0:T(8,128)(2,1)S(1)} %slice.332), channel_id=1, source_target_pairs={{0,2},{2,4},{4,6},{6,8},{8,10},{10,12},{12,14},{14,16},{16,18},{18... | collective-permute-start | bytes 98312 | tf_op jit(solution)/shard_map/ppermute | solution.py:16
  62.9 0.1 slice.204
  63.1 1.5 %collective-permute-start.7 = (f32[4,128,1]{2,1,0:T(8,128)S(1)}, f32[4,128,1]{2,1,0:T(8,128)S(1)}, u32[]{:S(2)}, u32[]{:S(2)}) collective-permute-start(f32[4,128,1]{2,1,0:T(8,128)S(1)} %slice.204), channel_id=1, source_target_pairs={{0,1},{2,3},{4,5},{6,7},{8,9},{10,11},{12,13},{14,15},{16,17},{18,... | collective-permute-start | bytes 6152 | tf_op jit(solution)/shard_map/ppermute | solution.py:16
  64.6 5.4 %collective-permute-done.7 = f32[4,128,1]{2,1,0:T(8,128)S(1)} collective-permute-done((f32[4,128,1]{2,1,0:T(8,128)S(1)}, f32[4,128,1]{2,1,0:T(8,128)S(1)}, u32[]{:S(2)}, u32[]{:S(2)}) %collective-permute-start.7) | collective-permute-done | bytes 2080 | tf_op jit(solution)/shard_map/ppermute | solution.py:16
  70.0 0.2 fusion.53
  70.2 1.3 %collective-permute-start.8 = (bf16[1,128,128]{2,1,0:T(8,128)(2,1)S(1)}, bf16[1,128,128]{2,1,0:T(8,128)(2,1)S(1)}, u32[]{:S(2)}, u32[]{:S(2)}) collective-permute-start(bf16[1,128,128]{2,1,0:T(8,128)(2,1)S(1)} %slice.331), channel_id=1, source_target_pairs={{2,0},{4,2},{6,4},{8,6},{10,8},{12,10},{14,12},{16,14},{18,16},{20... | collective-permute-start | bytes 98312 | tf_op jit(solution)/shard_map/ppermute | solution.py:16
  71.5 1.3 %collective-permute-start.10 = (f32[4,128,1]{2,1,0:T(8,128)S(1)}, f32[4,128,1]{2,1,0:T(8,128)S(1)}, u32[]{:S(2)}, u32[]{:S(2)}) collective-permute-start(f32[4,128,1]{2,1,0:T(8,128)S(1)} %bitcast.34), channel_id=1, source_target_pairs={{1,0},{3,2},{5,4},{7,6},{9,8},{11,10},{13,12},{15,14},{17,16},{19,... | collective-permute-start | bytes 6152 | tf_op jit(solution)/shard_map/ppermute | solution.py:16
  72.8 0.1 slice.211
  72.9 3.1 %collective-permute-done.8 = bf16[1,128,128]{2,1,0:T(8,128)(2,1)S(1)} collective-permute-done((bf16[1,128,128]{2,1,0:T(8,128)(2,1)S(1)}, bf16[1,128,128]{2,1,0:T(8,128)(2,1)S(1)}, u32[]{:S(2)}, u32[]{:S(2)}) %collective-permute-start.8) | collective-permute-done | bytes 32800 | tf_op jit(solution)/shard_map/ppermute | solution.py:16
  76.0 4.1 %collective-permute-done.10 = f32[4,128,1]{2,1,0:T(8,128)S(1)} collective-permute-done((f32[4,128,1]{2,1,0:T(8,128)S(1)}, f32[4,128,1]{2,1,0:T(8,128)S(1)}, u32[]{:S(2)}, u32[]{:S(2)}) %collective-permute-start.10) | collective-permute-done | bytes 2080 | tf_op jit(solution)/shard_map/ppermute | solution.py:16
  80.1 0.2 fusion.65
  80.4 4.7 %collective-permute-start.9 = (bf16[1,128,128]{2,1,0:T(8,128)(2,1)S(1)}, bf16[1,128,128]{2,1,0:T(8,128)(2,1)S(1)}, u32[]{:S(2)}, u32[]{:S(2)}) collective-permute-start(bf16[1,128,128]{2,1,0:T(8,128)(2,1)S(1)} %slice.330), channel_id=1, source_target_pairs={{0,2},{2,4},{4,6},{6,8},{8,10},{10,12},{12,14},{14,16},{16,18},{18... | collective-permute-start | bytes 98312 | tf_op jit(solution)/shard_map/ppermute | solution.py:16
  85.1 0.1 slice.213
  85.2 1.5 %collective-permute-start.11 = (f32[4,128,1]{2,1,0:T(8,128)S(1)}, f32[4,128,1]{2,1,0:T(8,128)S(1)}, u32[]{:S(2)}, u32[]{:S(2)}) collective-permute-start(f32[4,128,1]{2,1,0:T(8,128)S(1)} %slice.213), channel_id=1, source_target_pairs={{0,1},{2,3},{4,5},{6,7},{8,9},{10,11},{12,13},{14,15},{16,17},{18,... | collective-permute-start | bytes 6152 | tf_op jit(solution)/shard_map/ppermute | solution.py:16
  86.8 5.4 %collective-permute-done.11 = f32[4,128,1]{2,1,0:T(8,128)S(1)} collective-permute-done((f32[4,128,1]{2,1,0:T(8,128)S(1)}, f32[4,128,1]{2,1,0:T(8,128)S(1)}, u32[]{:S(2)}, u32[]{:S(2)}) %collective-permute-start.11) | collective-permute-done | bytes 2080 | tf_op jit(solution)/shard_map/ppermute | solution.py:16
  92.2 0.2 fusion.52
  92.4 1.3 %collective-permute-start.12 = (bf16[1,128,128]{2,1,0:T(8,128)(2,1)S(1)}, bf16[1,128,128]{2,1,0:T(8,128)(2,1)S(1)}, u32[]{:S(2)}, u32[]{:S(2)}) collective-permute-start(bf16[1,128,128]{2,1,0:T(8,128)(2,1)S(1)} %slice.329), channel_id=1, source_target_pairs={{2,0},{4,2},{6,4},{8,6},{10,8},{12,10},{14,12},{16,14},{18,16},{20... | collective-permute-start | bytes 98312 | tf_op jit(solution)/shard_map/ppermute | solution.py:16
  93.7 1.3 %collective-permute-start.14 = (f32[4,128,1]{2,1,0:T(8,128)S(1)}, f32[4,128,1]{2,1,0:T(8,128)S(1)}, u32[]{:S(2)}, u32[]{:S(2)}) collective-permute-start(f32[4,128,1]{2,1,0:T(8,128)S(1)} %bitcast.35), channel_id=1, source_target_pairs={{1,0},{3,2},{5,4},{7,6},{9,8},{11,10},{13,12},{15,14},{17,16},{19,... | collective-permute-start | bytes 6152 | tf_op jit(solution)/shard_map/ppermute | solution.py:16
  95.0 0.1 slice.220
  95.1 3.1 %collective-permute-done.12 = bf16[1,128,128]{2,1,0:T(8,128)(2,1)S(1)} collective-permute-done((bf16[1,128,128]{2,1,0:T(8,128)(2,1)S(1)}, bf16[1,128,128]{2,1,0:T(8,128)(2,1)S(1)}, u32[]{:S(2)}, u32[]{:S(2)}) %collective-permute-start.12) | collective-permute-done | bytes 32800 | tf_op jit(solution)/shard_map/ppermute | solution.py:16
  98.2 4.1 %collective-permute-done.14 = f32[4,128,1]{2,1,0:T(8,128)S(1)} collective-permute-done((f32[4,128,1]{2,1,0:T(8,128)S(1)}, f32[4,128,1]{2,1,0:T(8,128)S(1)}, u32[]{:S(2)}, u32[]{:S(2)}) %collective-permute-start.14) | collective-permute-done | bytes 2080 | tf_op jit(solution)/shard_map/ppermute | solution.py:16
  102.3 0.2 fusion.60
  102.6 4.7 %collective-permute-start.13 = (bf16[1,128,128]{2,1,0:T(8,128)(2,1)S(1)}, bf16[1,128,128]{2,1,0:T(8,128)(2,1)S(1)}, u32[]{:S(2)}, u32[]{:S(2)}) collective-permute-start(bf16[1,128,128]{2,1,0:T(8,128)(2,1)S(1)} %slice.328), channel_id=1, source_target_pairs={{0,2},{2,4},{4,6},{6,8},{8,10},{10,12},{12,14},{14,16},{16,18},{18... | collective-permute-start | bytes 98312 | tf_op jit(solution)/shard_map/ppermute | solution.py:16
  107.3 0.1 slice.222
  107.4 1.5 %collective-permute-start.15 = (f32[4,128,1]{2,1,0:T(8,128)S(1)}, f32[4,128,1]{2,1,0:T(8,128)S(1)}, u32[]{:S(2)}, u32[]{:S(2)}) collective-permute-start(f32[4,128,1]{2,1,0:T(8,128)S(1)} %slice.222), channel_id=1, source_target_pairs={{0,1},{2,3},{4,5},{6,7},{8,9},{10,11},{12,13},{14,15},{16,17},{18,... | collective-permute-start | bytes 6152 | tf_op jit(solution)/shard_map/ppermute | solution.py:16
  108.9 0.9 pad_maximum_fusion
  109.9 4.5 %collective-permute-done.15 = f32[4,128,1]{2,1,0:T(8,128)S(1)} collective-permute-done((f32[4,128,1]{2,1,0:T(8,128)S(1)}, f32[4,128,1]{2,1,0:T(8,128)S(1)}, u32[]{:S(2)}, u32[]{:S(2)}) %collective-permute-start.15) | collective-permute-done | bytes 2080 | tf_op jit(solution)/shard_map/ppermute | solution.py:16
  114.3 0.9 fusion.37
  (33 shorter events, 0.5 us)
Async XLA Ops:
  24.8 0.9 copy-start
  24.8 1.0 copy-start.1
  25.8 5.8 %collective-permute-start = (bf16[1,128,128]{2,1,0:T(8,128)(2,1)S(1)}, bf16[1,128,128]{2,1,0:T(8,128)(2,1)S(1)}, u32[]{:S(2)}, u32[]{:S(2)}) collective-permute-start(bf16[1,128,128]{2,1,0:T(8,128)(2,1)S(1)} %slice.335), channel_id=1, source_target_pairs={{2,0},{4,2},{6,4},{8,6},{10,8},{12,10},{14,12},{16,14},{18,16},{20... | collective-permute-start | bytes 98312 | tf_op jit(solution)/shard_map/ppermute | solution.py:16
  27.1 10.5 %collective-permute-start.2 = (f32[4,128,1]{2,1,0:T(8,128)S(1)}, f32[4,128,1]{2,1,0:T(8,128)S(1)}, u32[]{:S(2)}, u32[]{:S(2)}) collective-permute-start(f32[4,128,1]{2,1,0:T(8,128)S(1)} %bitcast.29), channel_id=1, source_target_pairs={{1,0},{3,2},{5,4},{7,6},{9,8},{11,10},{13,12},{15,14},{17,16},{19,... | collective-permute-start | bytes 6152 | tf_op jit(solution)/shard_map/ppermute | solution.py:16
  37.8 4.5 %collective-permute-start.1 = (bf16[1,128,128]{2,1,0:T(8,128)(2,1)S(1)}, bf16[1,128,128]{2,1,0:T(8,128)(2,1)S(1)}, u32[]{:S(2)}, u32[]{:S(2)}) collective-permute-start(bf16[1,128,128]{2,1,0:T(8,128)(2,1)S(1)} %slice.334), channel_id=1, source_target_pairs={{0,2},{2,4},{4,6},{6,8},{8,10},{10,12},{12,14},{14,16},{16,18},{18... | collective-permute-start | bytes 98312 | tf_op jit(solution)/shard_map/ppermute | solution.py:16
  40.8 6.9 %collective-permute-start.3 = (f32[4,128,1]{2,1,0:T(8,128)S(1)}, f32[4,128,1]{2,1,0:T(8,128)S(1)}, u32[]{:S(2)}, u32[]{:S(2)}) collective-permute-start(f32[4,128,1]{2,1,0:T(8,128)S(1)} %slice.195), channel_id=1, source_target_pairs={{0,1},{2,3},{4,5},{6,7},{8,9},{10,11},{12,13},{14,15},{16,17},{18,... | collective-permute-start | bytes 6152 | tf_op jit(solution)/shard_map/ppermute | solution.py:16
  47.9 5.8 %collective-permute-start.4 = (bf16[1,128,128]{2,1,0:T(8,128)(2,1)S(1)}, bf16[1,128,128]{2,1,0:T(8,128)(2,1)S(1)}, u32[]{:S(2)}, u32[]{:S(2)}) collective-permute-start(bf16[1,128,128]{2,1,0:T(8,128)(2,1)S(1)} %slice.333), channel_id=1, source_target_pairs={{2,0},{4,2},{6,4},{8,6},{10,8},{12,10},{14,12},{16,14},{18,16},{20... | collective-permute-start | bytes 98312 | tf_op jit(solution)/shard_map/ppermute | solution.py:16
  49.2 8.6 %collective-permute-start.6 = (f32[4,128,1]{2,1,0:T(8,128)S(1)}, f32[4,128,1]{2,1,0:T(8,128)S(1)}, u32[]{:S(2)}, u32[]{:S(2)}) collective-permute-start(f32[4,128,1]{2,1,0:T(8,128)S(1)} %bitcast.36), channel_id=1, source_target_pairs={{1,0},{3,2},{5,4},{7,6},{9,8},{11,10},{13,12},{15,14},{17,16},{19,... | collective-permute-start | bytes 6152 | tf_op jit(solution)/shard_map/ppermute | solution.py:16
  58.2 6.4 %collective-permute-start.5 = (bf16[1,128,128]{2,1,0:T(8,128)(2,1)S(1)}, bf16[1,128,128]{2,1,0:T(8,128)(2,1)S(1)}, u32[]{:S(2)}, u32[]{:S(2)}) collective-permute-start(bf16[1,128,128]{2,1,0:T(8,128)(2,1)S(1)} %slice.332), channel_id=1, source_target_pairs={{0,2},{2,4},{4,6},{6,8},{8,10},{10,12},{12,14},{14,16},{16,18},{18... | collective-permute-start | bytes 98312 | tf_op jit(solution)/shard_map/ppermute | solution.py:16
  63.1 6.9 %collective-permute-start.7 = (f32[4,128,1]{2,1,0:T(8,128)S(1)}, f32[4,128,1]{2,1,0:T(8,128)S(1)}, u32[]{:S(2)}, u32[]{:S(2)}) collective-permute-start(f32[4,128,1]{2,1,0:T(8,128)S(1)} %slice.204), channel_id=1, source_target_pairs={{0,1},{2,3},{4,5},{6,7},{8,9},{10,11},{12,13},{14,15},{16,17},{18,... | collective-permute-start | bytes 6152 | tf_op jit(solution)/shard_map/ppermute | solution.py:16
  70.2 5.8 %collective-permute-start.8 = (bf16[1,128,128]{2,1,0:T(8,128)(2,1)S(1)}, bf16[1,128,128]{2,1,0:T(8,128)(2,1)S(1)}, u32[]{:S(2)}, u32[]{:S(2)}) collective-permute-start(bf16[1,128,128]{2,1,0:T(8,128)(2,1)S(1)} %slice.331), channel_id=1, source_target_pairs={{2,0},{4,2},{6,4},{8,6},{10,8},{12,10},{14,12},{16,14},{18,16},{20... | collective-permute-start | bytes 98312 | tf_op jit(solution)/shard_map/ppermute | solution.py:16
  71.5 8.6 %collective-permute-start.10 = (f32[4,128,1]{2,1,0:T(8,128)S(1)}, f32[4,128,1]{2,1,0:T(8,128)S(1)}, u32[]{:S(2)}, u32[]{:S(2)}) collective-permute-start(f32[4,128,1]{2,1,0:T(8,128)S(1)} %bitcast.34), channel_id=1, source_target_pairs={{1,0},{3,2},{5,4},{7,6},{9,8},{11,10},{13,12},{15,14},{17,16},{19,... | collective-permute-start | bytes 6152 | tf_op jit(solution)/shard_map/ppermute | solution.py:16
  80.4 6.4 %collective-permute-start.9 = (bf16[1,128,128]{2,1,0:T(8,128)(2,1)S(1)}, bf16[1,128,128]{2,1,0:T(8,128)(2,1)S(1)}, u32[]{:S(2)}, u32[]{:S(2)}) collective-permute-start(bf16[1,128,128]{2,1,0:T(8,128)(2,1)S(1)} %slice.330), channel_id=1, source_target_pairs={{0,2},{2,4},{4,6},{6,8},{8,10},{10,12},{12,14},{14,16},{16,18},{18... | collective-permute-start | bytes 98312 | tf_op jit(solution)/shard_map/ppermute | solution.py:16
  85.2 6.9 %collective-permute-start.11 = (f32[4,128,1]{2,1,0:T(8,128)S(1)}, f32[4,128,1]{2,1,0:T(8,128)S(1)}, u32[]{:S(2)}, u32[]{:S(2)}) collective-permute-start(f32[4,128,1]{2,1,0:T(8,128)S(1)} %slice.213), channel_id=1, source_target_pairs={{0,1},{2,3},{4,5},{6,7},{8,9},{10,11},{12,13},{14,15},{16,17},{18,... | collective-permute-start | bytes 6152 | tf_op jit(solution)/shard_map/ppermute | solution.py:16
  92.4 5.8 %collective-permute-start.12 = (bf16[1,128,128]{2,1,0:T(8,128)(2,1)S(1)}, bf16[1,128,128]{2,1,0:T(8,128)(2,1)S(1)}, u32[]{:S(2)}, u32[]{:S(2)}) collective-permute-start(bf16[1,128,128]{2,1,0:T(8,128)(2,1)S(1)} %slice.329), channel_id=1, source_target_pairs={{2,0},{4,2},{6,4},{8,6},{10,8},{12,10},{14,12},{16,14},{18,16},{20... | collective-permute-start | bytes 98312 | tf_op jit(solution)/shard_map/ppermute | solution.py:16
  93.7 8.6 %collective-permute-start.14 = (f32[4,128,1]{2,1,0:T(8,128)S(1)}, f32[4,128,1]{2,1,0:T(8,128)S(1)}, u32[]{:S(2)}, u32[]{:S(2)}) collective-permute-start(f32[4,128,1]{2,1,0:T(8,128)S(1)} %bitcast.35), channel_id=1, source_target_pairs={{1,0},{3,2},{5,4},{7,6},{9,8},{11,10},{13,12},{15,14},{17,16},{19,... | collective-permute-start | bytes 6152 | tf_op jit(solution)/shard_map/ppermute | solution.py:16
  102.6 7.3 %collective-permute-start.13 = (bf16[1,128,128]{2,1,0:T(8,128)(2,1)S(1)}, bf16[1,128,128]{2,1,0:T(8,128)(2,1)S(1)}, u32[]{:S(2)}, u32[]{:S(2)}) collective-permute-start(bf16[1,128,128]{2,1,0:T(8,128)(2,1)S(1)} %slice.328), channel_id=1, source_target_pairs={{0,2},{2,4},{4,6},{6,8},{8,10},{10,12},{12,14},{14,16},{16,18},{18... | collective-permute-start | bytes 98312 | tf_op jit(solution)/shard_map/ppermute | solution.py:16
  107.4 6.9 %collective-permute-start.15 = (f32[4,128,1]{2,1,0:T(8,128)S(1)}, f32[4,128,1]{2,1,0:T(8,128)S(1)}, u32[]{:S(2)}, u32[]{:S(2)}) collective-permute-start(f32[4,128,1]{2,1,0:T(8,128)S(1)} %slice.222), channel_id=1, source_target_pairs={{0,1},{2,3},{4,5},{6,7},{8,9},{10,11},{12,13},{14,15},{16,17},{18,... | collective-permute-start | bytes 6152 | tf_op jit(solution)/shard_map/ppermute | solution.py:16
where the time goes:
time: 116 us; the launch traced here: 115 us
  waiting for transfers between devices  51.2 us (44%)
  starting transfers between devices  33.2 us (29%)
  blocking collectives  23 us (20%)
  other arithmetic  3.54 us (3%)
  local copies, waits for them, and re-layouts  3.13 us (3%)
    ppermute x16, waiting for transfers between devices, passed_along(): return lax.ppermute(block, axis, route)  51.2 us
    ppermute x16, starting transfers between devices, passed_along(): return lax.ppermute(block, axis, route)  33.2 us
    all_to_all x1, blocking collectives, on_device(): lax.all_to_all(source, ('grp', 'gx'), split_axis=1, concat_axis=2, tiled=...  23 us
  transfers between devices with their start and end apart: 16, of which 12 were waited for; matrix products, arithmetic and copies ran while one was open for 2% of the time, Pallas kernels for 0%

commit v1 on v0

v1 whole, which is shorter than its diff:
```python
import functools

import jax
import jax.numpy as jnp
from jax import lax
from jax.experimental import pallas as pl
from jax.experimental.pallas import tpu as pltpu
from jax.sharding import PartitionSpec as P

courant = 0.15
EDGE = 4
STRIP = 4 * EDGE
LOW, HIGH = EDGE - 1, 3 * EDGE


def f32(x):
    return x.astype(jnp.float32)


def iota(shape, dim):
    return lax.broadcasted_iota(jnp.int32, shape, dim)


def brick_block(src, step, layer):
    bricks = f32(src[:, layer, step])
    return bricks.reshape(bricks.shape[0] * bricks.shape[1], bricks.shape[2])


def coefficients(speed, imped):
    held = imped > 0.0
    stiff = courant * (speed * imped)
    buoy = jnp.where(held, courant * (speed / jnp.where(held, imped, 1.0)), 0.0)
    return stiff, buoy


class Block:
    def __init__(self, shape, series):
        self.row, self.lane = iota(shape, 0), iota(shape, 1)
        self.rows, self.lanes = shape
        self.series = series

    def fwd_y(self, a):
        return jnp.where(self.row == self.rows - 1, 0.0, pltpu.roll(a, self.rows - 1, 0)) - a

    def bwd_y(self, g):
        return g - jnp.where(self.row == 0, 0.0, pltpu.roll(g, 1, 0))

    def column(self, key):
        j = key
        return self.series[:, j : j + 1]

    def fwd_z(self, a, key):
        col = self.column(key)
        return jnp.where(self.lane == self.lanes - 1, col, pltpu.roll(a, self.lanes - 1, 1)) - a

    def bwd_z(self, g, key):
        col = self.column(key)
        return g - jnp.where(self.lane == 0, col, pltpu.roll(g, 1, 1))


class Strip:
    def __init__(self, shape, series):
        self.lane = iota(shape, 1)
        self.rows, self.lanes = shape
        self.series = series

    def fwd_y(self, a):
        return jnp.where(self.lane == self.lanes - 1, 0.0, pltpu.roll(a, self.lanes - 1, 1)) - a

    def bwd_y(self, g):
        return g - jnp.where(self.lane == 0, 0.0, pltpu.roll(g, 1, 1))

    def fwd_z(self, a, key):
        self.series[key : key + 1, :] = a[HIGH : HIGH + 1, :]
        return pltpu.roll(a, self.rows - 1, 0) - a

    def bwd_z(self, g, key):
        self.series[key : key + 1, :] = g[LOW : LOW + 1, :]
        return g - pltpu.roll(g, 1, 0)


def load_key(step, layer):
    return step * 16 + layer


def flux_key(step, layer):
    return step * 16 + 8 + layer


def run_cut(space, steps, layers, src, stiff, buoy, pressure, velocity, put_load, put_flux):
    ends = (0, layers - 1)
    everywhere = tuple(range(layers))
    for k in range(steps):
        load = []
        for i in everywhere if k < steps - 1 else ends:
            p = src(k, i) if k == 0 else pressure[i] + src(k, i)
            pressure[i] = p
            load.append(stiff(i) * p)
        put_load(k, load[0])
        if k == steps - 1:
            put_flux(k, buoy(layers - 1) * (velocity[0, layers - 1] - load[-1]))
            return
        wanted = everywhere if k < steps - 2 else ends
        below = None
        for i in everywhere:
            x = (load[i + 1] - load[i]) if i + 1 < layers else -load[i]
            if k > 0:
                x = velocity[0, i] + x
            velocity[0, i] = x
            fx = buoy(i) * x
            if i == layers - 1:
                put_flux(k, fx)
            if i in wanted:
                y = space.fwd_y(load[i])
                z = space.fwd_z(load[i], load_key(k, i))
                if k > 0:
                    y, z = velocity[1, i] + y, velocity[2, i] + z
                velocity[1, i], velocity[2, i] = y, z
                spread = fx if i == 0 else fx - below
                spread = spread + space.bwd_y(buoy(i) * y)
                spread = spread + space.bwd_z(buoy(i) * z, flux_key(k, i))
                pressure[i] = pressure[i] + spread
            below = fx


def run_joined(space, steps, layers, src, stiff, buoy, pressure, velocity, load_in, flux_in, up, down):
    everywhere = tuple(range(layers))
    above, under = layers, layers + 1
    pa = xa = ya = za = pa2 = None
    pb = xb = yb = zb = pb2 = xb2 = None
    for k in range(steps):
        inner = 0 < k < steps - 1
        load = []
        for i in everywhere:
            p = src(k, i) if k == 0 else pressure[i] + src(k, i)
            pressure[i] = p
            load.append(stiff(i) * p)
        beyond = load_in(k)
        if k > 0:
            la = up[0] * pa
            beyond = beyond + la
            lb = down[0] * pb
        if inner:
            xa = -la if xa is None else xa - la
            if pa2 is not None:
                xa = xa + up[1] * pa2
            y, z = space.fwd_y(la), space.fwd_z(la, load_key(k, above))
            ya, za = (y, z) if ya is None else (ya + y, za + z)
            y, z = space.fwd_y(lb), space.fwd_z(lb, load_key(k, under))
            yb, zb = (y, z) if yb is None else (yb + y, zb + z)
            xb2 = lb if xb2 is None else xb2 + lb
            if pb2 is not None:
                xb2 = xb2 - down[1] * pb2
        xb = load[0] if k == 0 else xb + load[0] - lb
        fb = down[2] * xb
        below = flux_in(k) + fb
        for i in everywhere:
            x = (load[i + 1] if i + 1 < layers else beyond) - load[i]
            y = space.fwd_y(load[i])
            z = space.fwd_z(load[i], load_key(k, i))
            if k > 0:
                x, y, z = velocity[0, i] + x, velocity[1, i] + y, velocity[2, i] + z
            velocity[0, i], velocity[1, i], velocity[2, i] = x, y, z
            fx = buoy(i) * x
            spread = fx - below
            spread = spread + space.bwd_y(buoy(i) * y)
            spread = spread + space.bwd_z(buoy(i) * z, flux_key(k, i))
            pressure[i] = pressure[i] + spread
            below = fx
        if k == steps - 1:
            return
        if k == 0:
            pa, pb = -below, fb
            continue
        fa = up[2] * xa
        pa = pa + fa - below
        pa = pa + space.bwd_y(up[2] * ya) + space.bwd_z(up[2] * za, flux_key(k, above))
        fb2 = down[3] * xb2
        pb = pb + fb - fb2
        pb = pb + space.bwd_y(down[2] * yb) + space.bwd_z(down[2] * zb, flux_key(k, under))
        if k < steps - 2:
            pa2, pb2 = -fa, fb2


class Layers:
    def __init__(self, ref):
        self.ref = ref

    def __getitem__(self, i):
        return self.ref[i]

    def __setitem__(self, i, value):
        self.ref[i] = value


def pack_kernel(steps, layers, src, speed, imped, low, high):
    lanes = src.shape[-1]
    shape = (layers * EDGE, lanes)
    row, lane = iota(shape, 0), iota(shape, 1)
    for f in range(steps + 2):
        total = None
        for i in range(layers):
            mine = (row >> 2) == i
            picks = [mine & (lane == base + (row & 3)) for base in (0, lanes - EDGE)]
            pick = jnp.concatenate([jnp.where(p, 1.0, 0.0) for p in picks], 0).astype(jnp.bfloat16)
            if f < steps:
                block = brick_block(src, f, i).astype(jnp.bfloat16)
            else:
                block = (speed, imped)[f - steps][i]
            part = lax.dot_general(pick, block, (((1,), (1,)), ((), ())), preferred_element_type=jnp.float32)
            total = part if total is None else total + part
        rows = layers * EDGE
        low[f * rows : (f + 1) * rows, :] = total[:rows].astype(jnp.bfloat16)
        high[f * rows : (f + 1) * rows, :] = total[rows:].astype(jnp.bfloat16)


def strip_rows(message, at, lanes):
    parts = [f32(message[at + j * STRIP : at + (j + 1) * STRIP, :]) for j in range(lanes // 128)]
    return parts[0] if len(parts) == 1 else jnp.concatenate(parts, 1)


def put_strip(message, at, strip):
    for j in range(strip.shape[1] // 128):
        message[at + j * STRIP : at + (j + 1) * STRIP, :] = strip[:, j * 128 : (j + 1) * 128].astype(jnp.bfloat16)


def is_even():
    return lax.axis_index("gx") % 2 == 0


class Faces:
    def __init__(self, far, near):
        self.far, self.near = far, near
        self.even = is_even()

    def put(self, write, below, above):
        write(self.far, jnp.where(self.even, below, above))
        write(self.near, jnp.where(self.even, above, below))

    def above(self, read):
        return jnp.where(self.even, read(self.near), read(self.far))

    def below(self, read):
        return jnp.where(self.even, read(self.far), read(self.near))


class Series:
    def __init__(self, faces, write):
        self.faces, self.write, self.loads = faces, write, {}

    def put_load(self, k, a):
        self.loads[k] = a

    def put_flux(self, k, a):
        self.faces.put(lambda ref, value: self.write(ref, k, value), self.loads[k], a)


def rows_writer(rows):
    def write(ref, k, a):
        ref[k * rows : (k + 1) * rows, :] = a.astype(jnp.bfloat16)
    return write


def rows_reader(rows):
    return lambda k: lambda ref: f32(ref[k * rows : (k + 1) * rows, :])


def strip_layout(steps, y):
    step = STRIP * (y // 128)
    return step, steps * y, steps * y + steps * step


def prepare_kernel(steps, source, speed, imped, bricks, far, near, sems):
    copies = [pltpu.make_async_copy(source.at[k], bricks.at[:, k], sems.at[k]) for k in range(steps)]
    for copy in copies:
        copy.start()
    faces = Faces(far, near)
    last = speed.shape[0] - 1
    for j, ref in enumerate((speed, imped)):
        for depth in range(2):
            def write(out, value, at=2 * j + depth):
                out[at] = value.astype(jnp.bfloat16)
            faces.put(write, f32(ref[depth]), f32(ref[last - depth]))
    for copy in copies:
        copy.wait()


def cut_kernel(
    steps, layers, gy_size, src, speed, imped, low, high, left, right, far, near, strips,
    pressure, velocity, stiff_ref, buoy_ref, series, columns,
):
    y, lanes = speed.shape[1:]
    rows = layers * EDGE
    me = lax.axis_index("gy")
    square = (layers * STRIP, layers * STRIP)
    r, c = iota(square, 0), iota(square, 1)
    group = (r >> 2) & 3
    wanted = c == group * rows + (r >> 4) * EDGE + (r & 3)
    wanted = wanted & jnp.logical_not((group == 0) & (me == 0))
    wanted = wanted & jnp.logical_not((group == 3) & (me == gy_size - 1))
    order = jnp.where(wanted, 1.0, 0.0).astype(jnp.bfloat16)
    for f in range(steps + 2):
        parts = jnp.concatenate([a[f * rows : (f + 1) * rows, :] for a in (left, low, high, right)], 0)
        strips[f] = jnp.dot(order, parts, preferred_element_type=jnp.float32)

    def strip(f, i):
        return strips[f, i * STRIP : (i + 1) * STRIP, :]

    faces = Faces(far, near)
    step, base, extra = strip_layout(steps, y)
    last = layers - 1
    for j, (f, depth) in enumerate(((steps, 0), (steps, 1), (steps + 1, 0), (steps + 1, 1))):
        faces.put(
            lambda ref, value, at=extra + j * step: put_strip(ref, at, value), strip(f, depth), strip(f, last - depth)
        )

    coef = [coefficients(strip(steps, i), strip(steps + 1, i)) for i in range(layers)]
    series[...] = jnp.zeros(series.shape, jnp.float32)
    out = Series(faces, lambda ref, k, a: put_strip(ref, base + k * step, a))
    run_cut(
        Strip((STRIP, y), series), steps, layers, lambda k, i: strip(steps - 1 - k, i),
        lambda i: coef[i][0], lambda i: coef[i][1], {}, {}, out.put_load, out.put_flux,
    )
    columns[...] = series[...].T

    for i in range(layers):
        stiff_ref[i], buoy_ref[i] = coefficients(f32(speed[i]), f32(imped[i]))
    out = Series(faces, rows_writer(y))
    run_cut(
        Block((y, lanes), columns), steps, layers, lambda k, i: brick_block(src, steps - 1 - k, i),
        lambda i: stiff_ref[i], lambda i: buoy_ref[i], Layers(pressure), Layers(velocity), out.put_load, out.put_flux,
    )


def joined_kernel(
    steps, layers, src, speed, imped, strips, far, near, coef_far, coef_near,
    pressure, velocity, stiff_ref, buoy_ref, series, columns,
):
    y, lanes = speed.shape[1:]

    def strip(f, i):
        return strips[f, i * STRIP : (i + 1) * STRIP, :]

    faces = Faces(far, near)
    step, base, extra = strip_layout(steps, y)

    def strip_at(at):
        return lambda ref: strip_rows(ref, at, y)

    def beside(side, at):
        s = [side(at(j)) for j in range(4)]
        (stiff, buoy), (stiff2, buoy2) = coefficients(s[0], s[2]), coefficients(s[1], s[3])
        return stiff, stiff2, buoy, buoy2

    coef = [coefficients(strip(steps, i), strip(steps + 1, i)) for i in range(layers)]
    series[...] = jnp.zeros(series.shape, jnp.float32)
    run_joined(
        Strip((STRIP, y), series), steps, layers, lambda k, i: strip(steps - 1 - k, i),
        lambda i: coef[i][0], lambda i: coef[i][1], {}, {},
        lambda k: faces.above(strip_at(base + k * step)), lambda k: faces.below(strip_at(base + k * step)),
        beside(faces.above, lambda j: strip_at(extra + j * step)),
        beside(faces.below, lambda j: strip_at(extra + j * step)),
    )
    columns[...] = series[...].T

    for i in range(layers):
        stiff_ref[i], buoy_ref[i] = coefficients(f32(speed[i]), f32(imped[i]))
    held = Faces(coef_far, coef_near)
    read = rows_reader(y)
    run_joined(
        Block((y, lanes), columns), steps, layers, lambda k, i: brick_block(src, steps - 1 - k, i),
        lambda i: stiff_ref[i], lambda i: buoy_ref[i], Layers(pressure), Layers(velocity),
        lambda k: faces.above(read(k)), lambda k: faces.below(read(k)),
        beside(held.above, lambda j: lambda ref: f32(ref[j])),
        beside(held.below, lambda j: lambda ref: f32(ref[j])),
    )


def shifted(block, axis, distance):
    devices = range(lax.axis_size(axis))
    return lax.ppermute(block, axis, [(i, i + distance) for i in devices if i + distance in devices])


def swapped(block, axis, first):
    pairs = [(i, i + 1) for i in range(first, lax.axis_size(axis) - 1, 2)]
    return lax.ppermute(block, axis, pairs + [(j, i) for i, j in pairs])


def on_device(source, speed, impedance):
    steps, whole_x, brick_y, lanes = source.shape
    layers, y, _ = speed.shape
    assert layers == steps == EDGE and lanes == 128 and y % 128 == 0
    gy_size = lax.axis_size("gy")
    xs = ("grp", "gx")
    bf16 = jnp.bfloat16
    params = pltpu.CompilerParams(vmem_limit_bytes=32 * 1024 * 1024)
    sds = jax.ShapeDtypeStruct

    assert lax.axis_size("gx") % 2 == 0
    coef = sds((4, y, lanes), bf16)
    bricks, coef_far, coef_near = pl.pallas_call(
        functools.partial(prepare_kernel, steps),
        in_specs=[pl.BlockSpec(memory_space=pl.ANY)] + [pl.BlockSpec(memory_space=pltpu.VMEM)] * 2,
        out_shape=(sds((whole_x, steps, brick_y, lanes), bf16), coef, coef),
        scratch_shapes=[pltpu.SemaphoreType.DMA((steps,))],
        compiler_params=params,
        name="prepare",
    )(source, speed, impedance)
    coef_far, coef_near = swapped(coef_far, xs, 1), swapped(coef_near, xs, 0)
    relaid = lax.all_to_all(bricks, xs, split_axis=0, concat_axis=0, tiled=True)
    relaid = relaid.reshape(whole_x // layers, layers, steps, brick_y, lanes)
    relaid, coef_far, coef_near = lax.optimization_barrier((relaid, coef_far, coef_near))

    edge = sds(((steps + 2) * layers * EDGE, y), bf16)
    low, high = pl.pallas_call(
        functools.partial(pack_kernel, steps, layers), out_shape=(edge, edge), compiler_params=params, name="pack"
    )(relaid, speed, impedance)
    if gy_size == 2:
        left = right = lax.ppermute(jnp.where(lax.axis_index("gy") == 0, high, low), "gy", [(0, 1), (1, 0)])
    else:
        left, right = shifted(high, "gy", 1), shifted(low, "gy", -1)

    whole = pltpu.VMEM((layers, y, lanes), jnp.float32)
    series = [pltpu.VMEM((128, y), jnp.float32), pltpu.VMEM((y, 128), jnp.float32)]
    message = sds((steps * y + (steps + 4) * STRIP * (y // 128), 128), bf16)
    far, near, strips = pl.pallas_call(
        functools.partial(cut_kernel, steps, layers, gy_size),
        out_shape=(message, message, sds((steps + 2, layers * STRIP, y), jnp.float32)),
        scratch_shapes=[whole, pltpu.VMEM((3, layers, y, lanes), jnp.float32), whole, whole] + series,
        compiler_params=params,
        name="cut",
    )(relaid, speed, impedance, low, high, left, right)

    far, near = swapped(far, xs, 1), swapped(near, xs, 0)

    return pl.pallas_call(
        functools.partial(joined_kernel, steps, layers),
        out_shape=(sds((layers, y, lanes), jnp.float32), sds((3, layers, y, lanes), jnp.float32)),
        scratch_shapes=[whole, whole] + series,
        compiler_params=params,
        name="joined",
    )(relaid, speed, impedance, strips, far, near, coef_far, coef_near)


def solution(mesh):
    in_specs = (
        P(None, None, ("grp", "gx"), "gy"),
        P(("grp", "gx"), None, "gy"),
        P(("grp", "gx"), None, "gy"),
    )
    out_specs = (P(("grp", "gx"), None, "gy"), P(None, ("grp", "gx"), None, "gy"))
    return jax.shard_map(
        on_device, mesh=mesh, in_specs=in_specs, out_specs=out_specs, check_vma=False
    )
```

time: 116 us -> 50.1 us (0.43)
  waiting for transfers between devices: 51.2 us -> 20.7 us
  blocking collectives: 23 us -> 0 us
  starting transfers between devices: 33.2 us -> 18.8 us
  Pallas kernels: 0 us -> 6.77 us
  other arithmetic: 3.54 us -> 0.03 us
    ppermute x16 -> x5, waiting for transfers between devices: 51.2 us -> 18.4 us  [the longest x4 16.1 us: swapped(): return lax.ppermute(block, axis, pairs + [(j, i) for i, j in pairs])]
    all_to_all x1 -> x0, blocking collectives: 23 us -> none  [on_device(): lax.all_to_all(source, ('grp', 'gx'), split_axis=1, concat_axis=2, tiled=...]
    ppermute x16 -> x5, starting transfers between devices: 33.2 us -> 11.3 us  [the longest x4 9.7 us: swapped(): return lax.ppermute(block, axis, pairs + [(j, i) for i, j in pairs])]
    all_to_all x0 -> x1, starting transfers between devices: none -> 7.53 us  [on_device(): relaid = lax.all_to_all(bricks, xs, split_axis=0, concat_axis=0, tiled=True)]
    pallas_call x0 -> x4, Pallas kernels: none -> 6.77 us  [the longest x1 3.71 us: on_device(): pl.pallas_call(functools.partial(joined_kernel, steps, layers), out_shape...]
    all_to_all x0 -> x1, waiting for transfers between devices: none -> 2.27 us  [on_device(): relaid = lax.all_to_all(bricks, xs, split_axis=0, concat_axis=0, tiled=True)]
    mul x7 -> x0, other arithmetic: 1.35 us -> none  [the longest x3 0.72 us: on_device(): flux_x = buoy * vel_x]
    unnamed x5 -> x10, local copies, waits for them, and re-layouts: 1.97 us -> 2.86 us
  transfers between devices with their start and end apart: 16 -> 6, of which waited for: 12 -> 4; matrix products, arithmetic and copies ran while one was open for 2% -> 0% of each run, Pallas kernels for 0% -> 0%
where the time goes in v1:
time: 50.1 us; the launch traced here: 49.8 us
  waiting for transfers between devices  20.7 us (41%)
  starting transfers between devices  18.8 us (38%)
  Pallas kernels  6.77 us (14%)
  local copies, waits for them, and re-layouts  2.86 us (6%)
  between operations  0.71 us (1%)
    ppermute x4, waiting for transfers between devices, swapped(): return lax.ppermute(block, axis, pairs + [(j, i) for i, j in pairs])  16.1 us
    ppermute x4, starting transfers between devices, swapped(): return lax.ppermute(block, axis, pairs + [(j, i) for i, j in pairs])  9.7 us
    all_to_all x1, starting transfers between devices, on_device(): relaid = lax.all_to_all(bricks, xs, split_axis=0, concat_axis=0, tiled=True)  7.53 us
    pallas_call x1, Pallas kernels, on_device(): pl.pallas_call(functools.partial(joined_kernel, steps, layers), out_shape...  3.71 us
    unnamed x10, local copies, waits for them, and re-layouts  2.86 us
    ppermute x1, waiting for transfers between devices, on_device(): lax.ppermute(jnp.where(lax.axis_index('gy') == 0, high, low), 'gy', [(0,...  2.34 us
    all_to_all x1, waiting for transfers between devices, on_device(): relaid = lax.all_to_all(bricks, xs, split_axis=0, concat_axis=0, tiled=True)  2.27 us
    pallas_call x1, Pallas kernels, on_device(): pl.pallas_call(functools.partial(cut_kernel, steps, layers, gy_size), out...  1.56 us
  transfers between devices with their start and end apart: 6, of which 4 were waited for; matrix products, arithmetic and copies ran while one was open for 0% of the time, Pallas kernels for 0%

profile of v1, /device:TPU:0, one launch (start us, length us, event | category | flops | bytes accessed | tf_op | source)
XLA Modules:
  0.0 49.8 jit_solution(8830674531561853340)
XLA Ops:
  0.6 0.0 copy-start
  0.6 0.9 %copy-done = bf16[4,128,128]{2,1,0:T(8,128)(2,1)S(1)} copy-done((bf16[4,128,128]{2,1,0:T(8,128)(2,1)S(1)}, bf16[4,128,128]{2,1,0:T(8,128)(2,1)}, u32[]{:S(2)}) %copy-start) | copy-done | bytes 131096
  1.5 0.0 copy-start.2
  1.5 0.9 %copy-done.2 = bf16[4,128,128]{2,1,0:T(8,128)(2,1)S(1)} copy-done((bf16[4,128,128]{2,1,0:T(8,128)(2,1)S(1)}, bf16[4,128,128]{2,1,0:T(8,128)(2,1)}, u32[]{:S(2)}) %copy-start.2) | copy-done | bytes 131096
  2.4 0.0 copy-start.4
  2.4 1.0 %copy-done.4 = bf16[4,64,8,128]{3,2,1,0:T(8,128)(2,1)S(1)} copy-done((bf16[4,64,8,128]{3,2,1,0:T(8,128)(2,1)S(1)}, bf16[4,64,8,128]{3,2,1,0:T(8,128)(2,1)}, u32[]{:S(2)}) %copy-start.4) | copy-done | bytes 524312
  3.5 1.0 %prepare.1 = (bf16[64,4,8,128]{3,2,1,0:T(8,128)(2,1)}, bf16[4,128,128]{2,1,0:T(8,128)(2,1)S(1)}, bf16[4,128,128]{2,1,0:T(8,128)(2,1)S(1)}) custom-call(bf16[4,64,8,128]{3,2,1,0:T(8,128)(2,1)S(1)} %copy-done.4, bf16[4,128,128]{2,1,0:T(8,128)(2,1)S(1)} %copy-done, bf16[4,128,128]{2,1,0:T(8,128)(2,1)S(1)} %copy-done.2), custom_call_target="tpu_custom_call" | custom-call | tf_op jit(solution)/shard_map/prepare/pallas_call | solution.py:401
  4.5 0.0 copy-start.1
  4.5 0.0 copy-start.3
  4.5 7.5 %all-to-all-start = ((bf16[64,4,8,128]{3,2,1,0:T(8,128)(2,1)}), bf16[64,4,8,128]{3,2,1,0:T(8,128)(2,1)S(1)}, u32[]{:S(2)}, u32[]{:S(2)}) async-start(bf16[64,4,8,128]{3,2,1,0:T(8,128)(2,1)} %get-tuple-element.13), calls=%async_computation | async-start | bytes 1048576 | tf_op jit(solution)/shard_map/all_to_all | solution.py:410
  12.1 0.7 %collective-permute-start = (bf16[4,128,128]{2,1,0:T(8,128)(2,1)S(1)}, bf16[4,128,128]{2,1,0:T(8,128)(2,1)S(1)}, u32[]{:S(2)}, u32[]{:S(2)}) collective-permute-start(bf16[4,128,128]{2,1,0:T(8,128)(2,1)S(1)} %get-tuple-element.14), channel_id=1, source_target_pairs={{2,4},{6,8},{10,12},{14,16},{18,20},{22,24},{26,28},{4,2},{8,6},{1... | collective-permute-start | bytes 393224 | tf_op jit(solution)/shard_map/ppermute | solution.py:386
  12.7 4.7 %collective-permute-start.1 = (bf16[4,128,128]{2,1,0:T(8,128)(2,1)S(1)}, bf16[4,128,128]{2,1,0:T(8,128)(2,1)S(1)}, u32[]{:S(2)}, u32[]{:S(2)}) collective-permute-start(bf16[4,128,128]{2,1,0:T(8,128)(2,1)S(1)} %get-tuple-element.15), channel_id=1, source_target_pairs={{0,2},{4,6},{8,10},{12,14},{16,18},{20,22},{24,26},{28,30},{2,0},{... | collective-permute-start | bytes 393224 | tf_op jit(solution)/shard_map/ppermute | solution.py:386
  17.4 0.0 collective-permute-done.coef_far
  17.4 9.6 %collective-permute-done.1.coef_near = bf16[4,128,128]{2,1,0:T(8,128)(2,1)S(1)} collective-permute-done((bf16[4,128,128]{2,1,0:T(8,128)(2,1)S(1)}, bf16[4,128,128]{2,1,0:T(8,128)(2,1)S(1)}, u32[]{:S(2)}, u32[]{:S(2)}) %collective-permute-start.1) | collective-permute-done | bytes 131104 | tf_op jit(solution)/shard_map/ppermute | solution.py:386
  27.0 2.3 %all-to-all-done = bf16[64,4,8,128]{3,2,1,0:T(8,128)(2,1)S(1)} async-done(((bf16[64,4,8,128]{3,2,1,0:T(8,128)(2,1)}), bf16[64,4,8,128]{3,2,1,0:T(8,128)(2,1)S(1)}, u32[]{:S(2)}, u32[]{:S(2)}) %all-to-all-start) | async-done | bytes 524320 | tf_op jit(solution)/shard_map/all_to_all | solution.py:410
  29.3 0.0 copy-done.1
  29.3 0.0 copy-done.3
  29.3 0.5 %pack.1 = (bf16[96,128]{1,0:T(8,128)(2,1)S(1)}, bf16[96,128]{1,0:T(8,128)(2,1)S(1)}) custom-call(bf16[16,4,4,8,128]{4,3,2,1,0:T(8,128)(2,1)S(1)} %bitcast.1, bf16[4,128,128]{2,1,0:T(8,128)(2,1)S(1)} %copy-done.1, bf16[4,128,128]{2,1,0:T(8,128)(2,1)S(1)} %copy-done.3), custom_call_target="tpu_custom_call" | custom-call | tf_op jit(solution)/shard_map/pack/pallas_call | solution.py:415
  29.8 1.6 %collective-permute-start.2 = (bf16[96,128]{1,0:T(8,128)(2,1)S(1)}, bf16[96,128]{1,0:T(8,128)(2,1)S(1)}, u32[]{:S(2)}, u32[]{:S(2)}) collective-permute-start(bf16[96,128]{1,0:T(8,128)(2,1)S(1)} %broadcast_select_fusion), channel_id=1, source_target_pairs={{0,1},{1,0},{2,3},{3,2},{4,5},{5,4},{6,7},{7,6},{8,9},{9,8},{10,11... | collective-permute-start | bytes 73736 | tf_op jit(solution)/shard_map/ppermute | solution.py:419
  31.4 2.3 %collective-permute-done.2.left.right = bf16[96,128]{1,0:T(8,128)(2,1)S(1)} collective-permute-done((bf16[96,128]{1,0:T(8,128)(2,1)S(1)}, bf16[96,128]{1,0:T(8,128)(2,1)S(1)}, u32[]{:S(2)}, u32[]{:S(2)}) %collective-permute-start.2) | collective-permute-done | bytes 24608 | tf_op jit(solution)/shard_map/ppermute | solution.py:419
  33.7 1.6 %cut.1 = (bf16[640,128]{1,0:T(8,128)(2,1)S(1)}, bf16[640,128]{1,0:T(8,128)(2,1)S(1)}, f32[6,64,128]{2,1,0:T(8,128)S(1)}) custom-call(bf16[16,4,4,8,128]{4,3,2,1,0:T(8,128)(2,1)S(1)} %bitcast.2, bf16[4,128,128]{2,1,0:T(8,128)(2,1)S(1)} %copy-done.1, bf16[4,128,128]{2,1,0:T(8,128)(2,1)S(1)} %copy-done.3, bf16[96,128]{1,0:T(8,128)(2,1)S(1)} %get-tuple-element.17.low, ...), custom_call_target="tpu_custom_call" | custom-call | tf_op jit(solution)/shard_map/cut/pallas_call | solution.py:426
  35.3 0.7 %collective-permute-start.3 = (bf16[640,128]{1,0:T(8,128)(2,1)S(1)}, bf16[640,128]{1,0:T(8,128)(2,1)S(1)}, u32[]{:S(2)}, u32[]{:S(2)}) collective-permute-start(bf16[640,128]{1,0:T(8,128)(2,1)S(1)} %get-tuple-element.20), channel_id=1, source_target_pairs={{2,4},{6,8},{10,12},{14,16},{18,20},{22,24},{26,28},{4,2},{8,6},{1... | collective-permute-start | bytes 491528 | tf_op jit(solution)/shard_map/ppermute | solution.py:386
  35.9 3.7 %collective-permute-start.4 = (bf16[640,128]{1,0:T(8,128)(2,1)S(1)}, bf16[640,128]{1,0:T(8,128)(2,1)S(1)}, u32[]{:S(2)}, u32[]{:S(2)}) collective-permute-start(bf16[640,128]{1,0:T(8,128)(2,1)S(1)} %get-tuple-element.21), channel_id=1, source_target_pairs={{0,2},{4,6},{8,10},{12,14},{16,18},{20,22},{24,26},{28,30},{2,0},{... | collective-permute-start | bytes 491528 | tf_op jit(solution)/shard_map/ppermute | solution.py:386
  39.6 0.0 collective-permute-done.3.far
  39.6 6.5 %collective-permute-done.4.near = bf16[640,128]{1,0:T(8,128)(2,1)S(1)} collective-permute-done((bf16[640,128]{1,0:T(8,128)(2,1)S(1)}, bf16[640,128]{1,0:T(8,128)(2,1)S(1)}, u32[]{:S(2)}, u32[]{:S(2)}) %collective-permute-start.4) | collective-permute-done | bytes 163872 | tf_op jit(solution)/shard_map/ppermute | solution.py:386
  46.1 3.7 %joined.1 = (f32[4,128,128]{2,1,0:T(8,128)}, f32[3,4,128,128]{3,2,1,0:T(8,128)}) custom-call(bf16[16,4,4,8,128]{4,3,2,1,0:T(8,128)(2,1)S(1)} %bitcast.3, bf16[4,128,128]{2,1,0:T(8,128)(2,1)S(1)} %copy-done.1, bf16[4,128,128]{2,1,0:T(8,128)(2,1)S(1)} %copy-done.3, f32[6,64,128]{2,1,0:T(8,128)S(1)} %get-tuple-element.19.strips, ...), custom_call_target="tpu_custom_call" | custom-call | tf_op jit(solution)/shard_map/joined/pallas_call | solution.py:436
  (1 shorter events, 0.0 us)
Async XLA Ops:
  0.6 0.9 %copy-start = (bf16[4,128,128]{2,1,0:T(8,128)(2,1)S(1)}, bf16[4,128,128]{2,1,0:T(8,128)(2,1)}, u32[]{:S(2)}) copy-start(bf16[4,128,128]{2,1,0:T(8,128)(2,1)} %speed.7) | copy-start | bytes 393220
  1.5 0.9 %copy-start.2 = (bf16[4,128,128]{2,1,0:T(8,128)(2,1)S(1)}, bf16[4,128,128]{2,1,0:T(8,128)(2,1)}, u32[]{:S(2)}) copy-start(bf16[4,128,128]{2,1,0:T(8,128)(2,1)} %imped.7) | copy-start | bytes 393220
  2.4 1.0 %copy-start.4 = (bf16[4,64,8,128]{3,2,1,0:T(8,128)(2,1)S(1)}, bf16[4,64,8,128]{3,2,1,0:T(8,128)(2,1)}, u32[]{:S(2)}) copy-start(bf16[4,64,8,128]{3,2,1,0:T(8,128)(2,1)} %source.1) | copy-start | bytes 1572868
  4.5 24.8 %copy-start.1 = (bf16[4,128,128]{2,1,0:T(8,128)(2,1)S(1)}, bf16[4,128,128]{2,1,0:T(8,128)(2,1)}, u32[]{:S(2)}) copy-start(bf16[4,128,128]{2,1,0:T(8,128)(2,1)} %speed.7) | copy-start | bytes 393220
  4.5 24.8 %copy-start.3 = (bf16[4,128,128]{2,1,0:T(8,128)(2,1)S(1)}, bf16[4,128,128]{2,1,0:T(8,128)(2,1)}, u32[]{:S(2)}) copy-start(bf16[4,128,128]{2,1,0:T(8,128)(2,1)} %imped.7) | copy-start | bytes 393220
  4.5 24.8 %all-to-all-start = ((bf16[64,4,8,128]{3,2,1,0:T(8,128)(2,1)}), bf16[64,4,8,128]{3,2,1,0:T(8,128)(2,1)S(1)}, u32[]{:S(2)}, u32[]{:S(2)}) async-start(bf16[64,4,8,128]{3,2,1,0:T(8,128)(2,1)} %get-tuple-element.13), calls=%async_computation | async-start | bytes 1048576 | tf_op jit(solution)/shard_map/all_to_all | solution.py:410
  12.1 5.4 %collective-permute-start = (bf16[4,128,128]{2,1,0:T(8,128)(2,1)S(1)}, bf16[4,128,128]{2,1,0:T(8,128)(2,1)S(1)}, u32[]{:S(2)}, u32[]{:S(2)}) collective-permute-start(bf16[4,128,128]{2,1,0:T(8,128)(2,1)S(1)} %get-tuple-element.14), channel_id=1, source_target_pairs={{2,4},{6,8},{10,12},{14,16},{18,20},{22,24},{26,28},{4,2},{8,6},{1... | collective-permute-start | bytes 393224 | tf_op jit(solution)/shard_map/ppermute | solution.py:386
  12.7 14.3 %collective-permute-start.1 = (bf16[4,128,128]{2,1,0:T(8,128)(2,1)S(1)}, bf16[4,128,128]{2,1,0:T(8,128)(2,1)S(1)}, u32[]{:S(2)}, u32[]{:S(2)}) collective-permute-start(bf16[4,128,128]{2,1,0:T(8,128)(2,1)S(1)} %get-tuple-element.15), channel_id=1, source_target_pairs={{0,2},{4,6},{8,10},{12,14},{16,18},{20,22},{24,26},{28,30},{2,0},{... | collective-permute-start | bytes 393224 | tf_op jit(solution)/shard_map/ppermute | solution.py:386
  29.8 3.9 %collective-permute-start.2 = (bf16[96,128]{1,0:T(8,128)(2,1)S(1)}, bf16[96,128]{1,0:T(8,128)(2,1)S(1)}, u32[]{:S(2)}, u32[]{:S(2)}) collective-permute-start(bf16[96,128]{1,0:T(8,128)(2,1)S(1)} %broadcast_select_fusion), channel_id=1, source_target_pairs={{0,1},{1,0},{2,3},{3,2},{4,5},{5,4},{6,7},{7,6},{8,9},{9,8},{10,11... | collective-permute-start | bytes 73736 | tf_op jit(solution)/shard_map/ppermute | solution.py:419
  35.3 4.4 %collective-permute-start.3 = (bf16[640,128]{1,0:T(8,128)(2,1)S(1)}, bf16[640,128]{1,0:T(8,128)(2,1)S(1)}, u32[]{:S(2)}, u32[]{:S(2)}) collective-permute-start(bf16[640,128]{1,0:T(8,128)(2,1)S(1)} %get-tuple-element.20), channel_id=1, source_target_pairs={{2,4},{6,8},{10,12},{14,16},{18,20},{22,24},{26,28},{4,2},{8,6},{1... | collective-permute-start | bytes 491528 | tf_op jit(solution)/shard_map/ppermute | solution.py:386
  35.9 10.2 %collective-permute-start.4 = (bf16[640,128]{1,0:T(8,128)(2,1)S(1)}, bf16[640,128]{1,0:T(8,128)(2,1)S(1)}, u32[]{:S(2)}, u32[]{:S(2)}) collective-permute-start(bf16[640,128]{1,0:T(8,128)(2,1)S(1)} %get-tuple-element.21), channel_id=1, source_target_pairs={{0,2},{4,6},{8,10},{12,14},{16,18},{20,22},{24,26},{28,30},{2,0},{... | collective-permute-start | bytes 491528 | tf_op jit(solution)/shard_map/ppermute | solution.py:386

commit v2 on v1

--- a/solution.py
+++ b/solution.py
@@ -270,26 +270,16 @@
     return step, steps * y, steps * y + steps * step
 
 
-def prepare_kernel(steps, source, speed, imped, bricks, far, near, sems):
-    copies = [pltpu.make_async_copy(source.at[k], bricks.at[:, k], sems.at[k]) for k in range(steps)]
-    for copy in copies:
-        copy.start()
-    faces = Faces(far, near)
-    last = speed.shape[0] - 1
-    for j, ref in enumerate((speed, imped)):
-        for depth in range(2):
-            def write(out, value, at=2 * j + depth):
-                out[at] = value.astype(jnp.bfloat16)
-            faces.put(write, f32(ref[depth]), f32(ref[last - depth]))
-    for copy in copies:
-        copy.wait()
+def coefficients_kernel(speed, imped, stiff, buoy):
+    for i in range(speed.shape[0]):
+        stiff[i], buoy[i] = coefficients(f32(speed[i]), f32(imped[i]))
 
 
 def cut_kernel(
-    steps, layers, gy_size, src, speed, imped, low, high, left, right, far, near, strips,
-    pressure, velocity, stiff_ref, buoy_ref, series, columns,
+    steps, layers, gy_size, src, stiff, buoy, low, high, left, right, far, near, strips,
+    pressure, velocity, series, columns,
 ):
-    y, lanes = speed.shape[1:]
+    y, lanes = stiff.shape[1:]
     rows = layers * EDGE
     me = lax.axis_index("gy")
     square = (layers * STRIP, layers * STRIP)
@@ -323,20 +313,18 @@
     )
     columns[...] = series[...].T
 
-    for i in range(layers):
-        stiff_ref[i], buoy_ref[i] = coefficients(f32(speed[i]), f32(imped[i]))
     out = Series(faces, rows_writer(y))
     run_cut(
         Block((y, lanes), columns), steps, layers, lambda k, i: brick_block(src, steps - 1 - k, i),
-        lambda i: stiff_ref[i], lambda i: buoy_ref[i], Layers(pressure), Layers(velocity), out.put_load, out.put_flux,
+        lambda i: stiff[i], lambda i: buoy[i], Layers(pressure), Layers(velocity), out.put_load, out.put_flux,
     )
 
 
 def joined_kernel(
-    steps, layers, src, speed, imped, strips, far, near, coef_far, coef_near,
-    pressure, velocity, stiff_ref, buoy_ref, series, columns,
+    steps, layers, src, stiff, buoy, strips, far, near, coef_far, coef_near,
+    pressure, velocity, series, columns,
 ):
-    y, lanes = speed.shape[1:]
+    y, lanes = stiff.shape[1:]
 
     def strip(f, i):
         return strips[f, i * STRIP : (i + 1) * STRIP, :]
@@ -363,13 +351,11 @@
     )
     columns[...] = series[...].T
 
-    for i in range(layers):
-        stiff_ref[i], buoy_ref[i] = coefficients(f32(speed[i]), f32(imped[i]))
     held = Faces(coef_far, coef_near)
     read = rows_reader(y)
     run_joined(
         Block((y, lanes), columns), steps, layers, lambda k, i: brick_block(src, steps - 1 - k, i),
-        lambda i: stiff_ref[i], lambda i: buoy_ref[i], Layers(pressure), Layers(velocity),
+        lambda i: stiff[i], lambda i: buoy[i], Layers(pressure), Layers(velocity),
         lambda k: faces.above(read(k)), lambda k: faces.below(read(k)),
         beside(held.above, lambda j: lambda ref: f32(ref[j])),
         beside(held.below, lambda j: lambda ref: f32(ref[j])),
@@ -397,19 +383,18 @@
     sds = jax.ShapeDtypeStruct
 
     assert lax.axis_size("gx") % 2 == 0
-    coef = sds((4, y, lanes), bf16)
-    bricks, coef_far, coef_near = pl.pallas_call(
-        functools.partial(prepare_kernel, steps),
-        in_specs=[pl.BlockSpec(memory_space=pl.ANY)] + [pl.BlockSpec(memory_space=pltpu.VMEM)] * 2,
-        out_shape=(sds((whole_x, steps, brick_y, lanes), bf16), coef, coef),
-        scratch_shapes=[pltpu.SemaphoreType.DMA((steps,))],
-        compiler_params=params,
-        name="prepare",
-    )(source, speed, impedance)
+    below = jnp.concatenate([speed[:2], impedance[:2]], 0)
+    above = jnp.concatenate([speed[-1:], speed[-2:-1], impedance[-1:], impedance[-2:-1]], 0)
+    even = is_even()
+    coef_far, coef_near = jnp.where(even, below, above), jnp.where(even, above, below)
     coef_far, coef_near = swapped(coef_far, xs, 1), swapped(coef_near, xs, 0)
-    relaid = lax.all_to_all(bricks, xs, split_axis=0, concat_axis=0, tiled=True)
+    relaid = lax.all_to_all(source.transpose(1, 0, 2, 3), xs, split_axis=0, concat_axis=0, tiled=True)
     relaid = relaid.reshape(whole_x // layers, layers, steps, brick_y, lanes)
-    relaid, coef_far, coef_near = lax.optimization_barrier((relaid, coef_far, coef_near))
+    field = sds((layers, y, lanes), jnp.float32)
+    stiff, buoy = pl.pallas_call(
+        coefficients_kernel, out_shape=(field, field), compiler_params=params, name="coefficients"
+    )(speed, impedance)
+    relaid, coef_far, coef_near, stiff, buoy = lax.optimization_barrier((relaid, coef_far, coef_near, stiff, buoy))
 
     edge = sds(((steps + 2) * layers * EDGE, y), bf16)
     low, high = pl.pallas_call(
@@ -420,26 +405,25 @@
     else:
         left, right = shifted(high, "gy", 1), shifted(low, "gy", -1)
 
-    whole = pltpu.VMEM((layers, y, lanes), jnp.float32)
     series = [pltpu.VMEM((128, y), jnp.float32), pltpu.VMEM((y, 128), jnp.float32)]
     message = sds((steps * y + (steps + 4) * STRIP * (y // 128), 128), bf16)
     far, near, strips = pl.pallas_call(
         functools.partial(cut_kernel, steps, layers, gy_size),
         out_shape=(message, message, sds((steps + 2, layers * STRIP, y), jnp.float32)),
-        scratch_shapes=[whole, pltpu.VMEM((3, layers, y, lanes), jnp.float32), whole, whole] + series,
+        scratch_shapes=[pltpu.VMEM((layers, y, lanes), jnp.float32), pltpu.VMEM((3, layers, y, lanes), jnp.float32)] + series,
         compiler_params=params,
         name="cut",
-    )(relaid, speed, impedance, low, high, left, right)
+    )(relaid, stiff, buoy, low, high, left, right)
 
     far, near = swapped(far, xs, 1), swapped(near, xs, 0)
 
     return pl.pallas_call(
         functools.partial(joined_kernel, steps, layers),
-        out_shape=(sds((layers, y, lanes), jnp.float32), sds((3, layers, y, lanes), jnp.float32)),
-        scratch_shapes=[whole, whole] + series,
+        out_shape=(field, sds((3, layers, y, lanes), jnp.float32)),
+        scratch_shapes=series,
         compiler_params=params,
         name="joined",
-    )(relaid, speed, impedance, strips, far, near, coef_far, coef_near)
+    )(relaid, stiff, buoy, strips, far, near, coef_far, coef_near)
 
 
 def solution(mesh):

time: 50.1 us -> 48 us (0.958)
  starting transfers between devices: 18.8 us -> 15.9 us
  Pallas kernels: 6.77 us -> 5.78 us
  local copies, waits for them, and re-layouts: 2.86 us -> 3.75 us
  waiting for transfers between devices: 20.7 us -> 21.4 us
    ppermute x4, starting transfers between devices: 9.7 us -> 6.98 us  [swapped(): return lax.ppermute(block, axis, pairs + [(j, i) for i, j in pairs])]
    all_to_all x1, waiting for transfers between devices: 2.27 us -> 4.3 us  [on_device(): lax.all_to_all(source.transpose(1, 0, 2, 3), xs, split_axis=0, concat_axi...]
    ppermute x4, waiting for transfers between devices: 16.1 us -> 14.8 us  [swapped(): return lax.ppermute(block, axis, pairs + [(j, i) for i, j in pairs])]
    pallas_call x1, Pallas kernels: 1 us -> 0.09 us  [on_device(): pl.pallas_call(coefficients_kernel, out_shape=(field, field), compiler_pa...]
    slice x0 -> x5, local copies, waits for them, and re-layouts: none -> 0.87 us  [the longest x4 0.86 us: on_device(): below = jnp.concatenate([speed[:2], impedance[:2]], 0)]
    unnamed x10 -> x5, local copies, waits for them, and re-layouts: 2.86 us -> 2.88 us
where the time goes in v2:
time: 48 us; the launch traced here: 47.6 us
  waiting for transfers between devices  21.4 us (45%)
  starting transfers between devices  15.9 us (33%)
  Pallas kernels  5.78 us (12%)
  local copies, waits for them, and re-layouts  3.75 us (8%)
  between operations  0.73 us (2%)
    ppermute x4, waiting for transfers between devices, swapped(): return lax.ppermute(block, axis, pairs + [(j, i) for i, j in pairs])  14.8 us
    all_to_all x1, starting transfers between devices, on_device(): lax.all_to_all(source.transpose(1, 0, 2, 3), xs, split_axis=0, concat_axi...  7.39 us
    ppermute x4, starting transfers between devices, swapped(): return lax.ppermute(block, axis, pairs + [(j, i) for i, j in pairs])  6.98 us
    all_to_all x1, waiting for transfers between devices, on_device(): lax.all_to_all(source.transpose(1, 0, 2, 3), xs, split_axis=0, concat_axi...  4.3 us
    pallas_call x1, Pallas kernels, on_device(): pl.pallas_call(functools.partial(joined_kernel, steps, layers), out_shape...  3.64 us
    unnamed x5, local copies, waits for them, and re-layouts  2.88 us
    ppermute x1, waiting for transfers between devices, on_device(): lax.ppermute(jnp.where(lax.axis_index('gy') == 0, high, low), 'gy', [(0,...  2.34 us
    ppermute x1, starting transfers between devices, on_device(): lax.ppermute(jnp.where(lax.axis_index('gy') == 0, high, low), 'gy', [(0,...  1.56 us
  transfers between devices with their start and end apart: 6, of which 4 were waited for; matrix products, arithmetic and copies ran while one was open for 0% of the time, Pallas kernels for 0%

profile of v2, /device:TPU:0, one launch (start us, length us, event | category | flops | bytes accessed | tf_op | source)
XLA Modules:
  0.0 47.6 jit_solution(12881394766250358853)
XLA Ops:
  0.6 1.9 %copy.8 = bf16[4,64,8,128]{3,2,0,1:T(8,128)(2,1)} copy(bf16[4,64,8,128]{3,2,1,0:T(8,128)(2,1)} %param.3) | data formatting | bytes 1048576 | tf_op args[0]
  2.6 7.4 %all-to-all-start = ((bf16[64,4,8,128]{3,2,1,0:T(8,128)(2,1)}), bf16[64,4,8,128]{3,2,1,0:T(8,128)(2,1)S(1)}, u32[]{:S(2)}, u32[]{:S(2)}) async-start(bf16[64,4,8,128]{3,2,1,0:T(8,128)(2,1)} %bitcast.3), calls=%async_computation | async-start | bytes 1048576 | tf_op jit(solution)/shard_map/all_to_all | solution.py:391
  10.0 0.0 copy-start
  10.0 0.0 copy-start.1
  10.0 0.9 %copy-done = bf16[4,128,128]{2,1,0:T(8,128)(2,1)S(1)} copy-done((bf16[4,128,128]{2,1,0:T(8,128)(2,1)S(1)}, bf16[4,128,128]{2,1,0:T(8,128)(2,1)}, u32[]{:S(2)}) %copy-start) | copy-done | bytes 131096
  10.9 0.1 copy-done.1
  10.9 0.0 slice-start
  10.9 0.0 slice-start.1
  11.0 0.8 %slice-done = bf16[2,128,128]{2,1,0:T(8,128)(2,1)S(1)} async-done(((bf16[4,128,128]{2,1,0:T(8,128)(2,1)}), bf16[2,128,128]{2,1,0:T(8,128)(2,1)S(1)}, s32[]{:S(2)}) %slice-start) | async-done | bytes 65560 | tf_op jit(solution)/shard_map/slice | solution.py:386
  11.8 0.0 slice-done.1
  11.8 2.0 %collective-permute-start.1 = (bf16[4,128,128]{2,1,0:T(8,128)(2,1)S(1)}, bf16[4,128,128]{2,1,0:T(8,128)(2,1)S(1)}, u32[]{:S(2)}, u32[]{:S(2)}) collective-permute-start(bf16[4,128,128]{2,1,0:T(8,128)(2,1)S(1)} %get-tuple-element.26), channel_id=1, source_target_pairs={{0,2},{4,6},{8,10},{12,14},{16,18},{20,22},{24,26},{28,30},{2,0},{... | collective-permute-start | bytes 393224 | tf_op jit(solution)/shard_map/ppermute | solution.py:372
  13.8 0.7 %collective-permute-start = (bf16[4,128,128]{2,1,0:T(8,128)(2,1)S(1)}, bf16[4,128,128]{2,1,0:T(8,128)(2,1)S(1)}, u32[]{:S(2)}, u32[]{:S(2)}) collective-permute-start(bf16[4,128,128]{2,1,0:T(8,128)(2,1)S(1)} %get-tuple-element.27), channel_id=1, source_target_pairs={{2,4},{6,8},{10,12},{14,16},{18,20},{22,24},{26,28},{4,2},{8,6},{1... | collective-permute-start | bytes 393224 | tf_op jit(solution)/shard_map/ppermute | solution.py:372
  14.5 0.1 coefficients.1
  14.6 8.3 %collective-permute-done.1.coef_near = bf16[4,128,128]{2,1,0:T(8,128)(2,1)S(1)} collective-permute-done((bf16[4,128,128]{2,1,0:T(8,128)(2,1)S(1)}, bf16[4,128,128]{2,1,0:T(8,128)(2,1)S(1)}, u32[]{:S(2)}, u32[]{:S(2)}) %collective-permute-start.1) | collective-permute-done | bytes 131104 | tf_op jit(solution)/shard_map/ppermute | solution.py:372
  22.9 0.0 collective-permute-done.coef_far
  22.9 4.3 %all-to-all-done = bf16[64,4,8,128]{3,2,1,0:T(8,128)(2,1)S(1)} async-done(((bf16[64,4,8,128]{3,2,1,0:T(8,128)(2,1)}), bf16[64,4,8,128]{3,2,1,0:T(8,128)(2,1)S(1)}, u32[]{:S(2)}, u32[]{:S(2)}) %all-to-all-start) | async-done | bytes 524320 | tf_op jit(solution)/shard_map/all_to_all | solution.py:391
  27.2 0.5 %pack.1 = (bf16[96,128]{1,0:T(8,128)(2,1)S(1)}, bf16[96,128]{1,0:T(8,128)(2,1)S(1)}) custom-call(bf16[16,4,4,8,128]{4,3,2,1,0:T(8,128)(2,1)S(1)} %bitcast.4, bf16[4,128,128]{2,1,0:T(8,128)(2,1)S(1)} %copy-done, bf16[4,128,128]{2,1,0:T(8,128)(2,1)S(1)} %copy-done.1), custom_call_target="tpu_custom_call" | custom-call | tf_op jit(solution)/shard_map/pack/pallas_call | solution.py:400
  27.7 1.6 %collective-permute-start.2 = (bf16[96,128]{1,0:T(8,128)(2,1)S(1)}, bf16[96,128]{1,0:T(8,128)(2,1)S(1)}, u32[]{:S(2)}, u32[]{:S(2)}) collective-permute-start(bf16[96,128]{1,0:T(8,128)(2,1)S(1)} %broadcast_select_fusion.2), channel_id=1, source_target_pairs={{0,1},{1,0},{2,3},{3,2},{4,5},{5,4},{6,7},{7,6},{8,9},{9,8},{10,11... | collective-permute-start | bytes 73736 | tf_op jit(solution)/shard_map/ppermute | solution.py:404
  29.3 2.3 %collective-permute-done.2.left.right = bf16[96,128]{1,0:T(8,128)(2,1)S(1)} collective-permute-done((bf16[96,128]{1,0:T(8,128)(2,1)S(1)}, bf16[96,128]{1,0:T(8,128)(2,1)S(1)}, u32[]{:S(2)}, u32[]{:S(2)}) %collective-permute-start.2) | collective-permute-done | bytes 24608 | tf_op jit(solution)/shard_map/ppermute | solution.py:404
  31.6 1.6 %cut.1 = (bf16[640,128]{1,0:T(8,128)(2,1)S(1)}, bf16[640,128]{1,0:T(8,128)(2,1)S(1)}, f32[6,64,128]{2,1,0:T(8,128)S(1)}) custom-call(bf16[16,4,4,8,128]{4,3,2,1,0:T(8,128)(2,1)S(1)} %bitcast.5, f32[4,128,128]{2,1,0:T(8,128)S(1)} %get-tuple-element.17.stiff, f32[4,128,128]{2,1,0:T(8,128)S(1)} %get-tuple-element.18.buoy, ...), custom_call_target="tpu_custom_call" | custom-call | tf_op jit(solution)/shard_map/cut/pallas_call | solution.py:410
  33.1 0.7 %collective-permute-start.3 = (bf16[640,128]{1,0:T(8,128)(2,1)S(1)}, bf16[640,128]{1,0:T(8,128)(2,1)S(1)}, u32[]{:S(2)}, u32[]{:S(2)}) collective-permute-start(bf16[640,128]{1,0:T(8,128)(2,1)S(1)} %get-tuple-element.22), channel_id=1, source_target_pairs={{2,4},{6,8},{10,12},{14,16},{18,20},{22,24},{26,28},{4,2},{8,6},{1... | collective-permute-start | bytes 491528 | tf_op jit(solution)/shard_map/ppermute | solution.py:372
  33.8 3.7 %collective-permute-start.4 = (bf16[640,128]{1,0:T(8,128)(2,1)S(1)}, bf16[640,128]{1,0:T(8,128)(2,1)S(1)}, u32[]{:S(2)}, u32[]{:S(2)}) collective-permute-start(bf16[640,128]{1,0:T(8,128)(2,1)S(1)} %get-tuple-element.23), channel_id=1, source_target_pairs={{0,2},{4,6},{8,10},{12,14},{16,18},{20,22},{24,26},{28,30},{2,0},{... | collective-permute-start | bytes 491528 | tf_op jit(solution)/shard_map/ppermute | solution.py:372
  37.5 0.0 collective-permute-done.3.far
  37.5 6.5 %collective-permute-done.4.near = bf16[640,128]{1,0:T(8,128)(2,1)S(1)} collective-permute-done((bf16[640,128]{1,0:T(8,128)(2,1)S(1)}, bf16[640,128]{1,0:T(8,128)(2,1)S(1)}, u32[]{:S(2)}, u32[]{:S(2)}) %collective-permute-start.4) | collective-permute-done | bytes 163872 | tf_op jit(solution)/shard_map/ppermute | solution.py:372
  44.0 3.6 %joined.1 = (f32[4,128,128]{2,1,0:T(8,128)}, f32[3,4,128,128]{3,2,1,0:T(8,128)}) custom-call(bf16[16,4,4,8,128]{4,3,2,1,0:T(8,128)(2,1)S(1)} %bitcast.6, f32[4,128,128]{2,1,0:T(8,128)S(1)} %get-tuple-element.17.stiff, f32[4,128,128]{2,1,0:T(8,128)S(1)} %get-tuple-element.18.buoy, f32[6,64,128]{2,1,0:T(8,128)S(1)} %get-tuple-element.21.strips, ...), custom_call_target="tpu_custom_call" | custom-call | tf_op jit(solution)/shard_map/joined/pallas_call | solution.py:420
  (3 shorter events, 0.1 us)
Async XLA Ops:
  2.6 24.6 %all-to-all-start = ((bf16[64,4,8,128]{3,2,1,0:T(8,128)(2,1)}), bf16[64,4,8,128]{3,2,1,0:T(8,128)(2,1)S(1)}, u32[]{:S(2)}, u32[]{:S(2)}) async-start(bf16[64,4,8,128]{3,2,1,0:T(8,128)(2,1)} %bitcast.3), calls=%async_computation | async-start | bytes 1048576 | tf_op jit(solution)/shard_map/all_to_all | solution.py:391
  10.0 0.9 %copy-start = (bf16[4,128,128]{2,1,0:T(8,128)(2,1)S(1)}, bf16[4,128,128]{2,1,0:T(8,128)(2,1)}, u32[]{:S(2)}) copy-start(bf16[4,128,128]{2,1,0:T(8,128)(2,1)} %speed.3) | copy-start | bytes 393220
  10.0 1.0 %copy-start.1 = (bf16[4,128,128]{2,1,0:T(8,128)(2,1)S(1)}, bf16[4,128,128]{2,1,0:T(8,128)(2,1)}, u32[]{:S(2)}) copy-start(bf16[4,128,128]{2,1,0:T(8,128)(2,1)} %imped.3) | copy-start | bytes 393220
  10.9 0.8 %slice-start = ((bf16[4,128,128]{2,1,0:T(8,128)(2,1)}), bf16[2,128,128]{2,1,0:T(8,128)(2,1)S(1)}, s32[]{:S(2)}) async-start(bf16[4,128,128]{2,1,0:T(8,128)(2,1)} %speed.3), calls=%async_computation.1 | async-start | bytes 131072 | tf_op jit(solution)/shard_map/slice | solution.py:386
  10.9 0.9 %slice-start.1 = ((bf16[4,128,128]{2,1,0:T(8,128)(2,1)}), bf16[2,128,128]{2,1,0:T(8,128)(2,1)S(1)}, s32[]{:S(2)}) async-start(bf16[4,128,128]{2,1,0:T(8,128)(2,1)} %imped.3), calls=%async_computation.2 | async-start | bytes 131072 | tf_op jit(solution)/shard_map/slice | solution.py:386
  11.8 11.0 %collective-permute-start.1 = (bf16[4,128,128]{2,1,0:T(8,128)(2,1)S(1)}, bf16[4,128,128]{2,1,0:T(8,128)(2,1)S(1)}, u32[]{:S(2)}, u32[]{:S(2)}) collective-permute-start(bf16[4,128,128]{2,1,0:T(8,128)(2,1)S(1)} %get-tuple-element.26), channel_id=1, source_target_pairs={{0,2},{4,6},{8,10},{12,14},{16,18},{20,22},{24,26},{28,30},{2,0},{... | collective-permute-start | bytes 393224 | tf_op jit(solution)/shard_map/ppermute | solution.py:372
  13.8 9.0 %collective-permute-start = (bf16[4,128,128]{2,1,0:T(8,128)(2,1)S(1)}, bf16[4,128,128]{2,1,0:T(8,128)(2,1)S(1)}, u32[]{:S(2)}, u32[]{:S(2)}) collective-permute-start(bf16[4,128,128]{2,1,0:T(8,128)(2,1)S(1)} %get-tuple-element.27), channel_id=1, source_target_pairs={{2,4},{6,8},{10,12},{14,16},{18,20},{22,24},{26,28},{4,2},{8,6},{1... | collective-permute-start | bytes 393224 | tf_op jit(solution)/shard_map/ppermute | solution.py:372
  27.7 3.9 %collective-permute-start.2 = (bf16[96,128]{1,0:T(8,128)(2,1)S(1)}, bf16[96,128]{1,0:T(8,128)(2,1)S(1)}, u32[]{:S(2)}, u32[]{:S(2)}) collective-permute-start(bf16[96,128]{1,0:T(8,128)(2,1)S(1)} %broadcast_select_fusion.2), channel_id=1, source_target_pairs={{0,1},{1,0},{2,3},{3,2},{4,5},{5,4},{6,7},{7,6},{8,9},{9,8},{10,11... | collective-permute-start | bytes 73736 | tf_op jit(solution)/shard_map/ppermute | solution.py:404
  33.1 4.4 %collective-permute-start.3 = (bf16[640,128]{1,0:T(8,128)(2,1)S(1)}, bf16[640,128]{1,0:T(8,128)(2,1)S(1)}, u32[]{:S(2)}, u32[]{:S(2)}) collective-permute-start(bf16[640,128]{1,0:T(8,128)(2,1)S(1)} %get-tuple-element.22), channel_id=1, source_target_pairs={{2,4},{6,8},{10,12},{14,16},{18,20},{22,24},{26,28},{4,2},{8,6},{1... | collective-permute-start | bytes 491528 | tf_op jit(solution)/shard_map/ppermute | solution.py:372
  33.8 10.2 %collective-permute-start.4 = (bf16[640,128]{1,0:T(8,128)(2,1)S(1)}, bf16[640,128]{1,0:T(8,128)(2,1)S(1)}, u32[]{:S(2)}, u32[]{:S(2)}) collective-permute-start(bf16[640,128]{1,0:T(8,128)(2,1)S(1)} %get-tuple-element.23), channel_id=1, source_target_pairs={{0,2},{4,6},{8,10},{12,14},{16,18},{20,22},{24,26},{28,30},{2,0},{... | collective-permute-start | bytes 491528 | tf_op jit(solution)/shard_map/ppermute | solution.py:372

commit v3 on v2

--- a/solution.py
+++ b/solution.py
@@ -10,6 +10,8 @@
 courant = 0.15
 EDGE = 4
 STRIP = 4 * EDGE
+OWN = 3 * EDGE
+WIDE = 2 * (OWN + EDGE)
 LOW, HIGH = EDGE - 1, 3 * EDGE
 
 
@@ -46,8 +48,7 @@
         return g - jnp.where(self.row == 0, 0.0, pltpu.roll(g, 1, 0))
 
     def column(self, key):
-        j = key
-        return self.series[:, j : j + 1]
+        return 0.0 if self.series is None else self.series[:, key : key + 1]
 
     def fwd_z(self, a, key):
         col = self.column(key)
@@ -71,11 +72,13 @@
         return g - jnp.where(self.lane == 0, 0.0, pltpu.roll(g, 1, 1))
 
     def fwd_z(self, a, key):
-        self.series[key : key + 1, :] = a[HIGH : HIGH + 1, :]
+        if self.series is not None:
+            self.series[key : key + 1, :] = a[HIGH : HIGH + 1, :]
         return pltpu.roll(a, self.rows - 1, 0) - a
 
     def bwd_z(self, g, key):
-        self.series[key : key + 1, :] = g[LOW : LOW + 1, :]
+        if self.series is not None:
+            self.series[key : key + 1, :] = g[LOW : LOW + 1, :]
         return g - pltpu.roll(g, 1, 0)
 
 
@@ -193,23 +196,28 @@
         self.ref[i] = value
 
 
-def pack_kernel(steps, layers, src, speed, imped, low, high):
+def pack_kernel(steps, layers, src, speed, imped, low, high, own):
     lanes = src.shape[-1]
-    shape = (layers * EDGE, lanes)
-    row, lane = iota(shape, 0), iota(shape, 1)
+    rows = layers * EDGE
+    row, lane = iota((rows, lanes), 0), iota((rows, lanes), 1)
+    wrow, wlane = iota((WIDE, lanes), 0), iota((WIDE, lanes), 1)
+    half = WIDE // 2
+    at_low = (wrow >= EDGE) & (wrow < half) & (wlane == wrow - EDGE)
+    at_high = (wrow >= half) & (wrow < half + OWN) & (wlane == wrow + (lanes - OWN - half))
+    wide = jnp.where(at_low | at_high, 1.0, 0.0)
     for f in range(steps + 2):
         total = None
         for i in range(layers):
             mine = (row >> 2) == i
             picks = [mine & (lane == base + (row & 3)) for base in (0, lanes - EDGE)]
-            pick = jnp.concatenate([jnp.where(p, 1.0, 0.0) for p in picks], 0).astype(jnp.bfloat16)
+            pick = jnp.concatenate([wide] + [jnp.where(p, 1.0, 0.0) for p in picks], 0).astype(jnp.bfloat16)
             if f < steps:
                 block = brick_block(src, f, i).astype(jnp.bfloat16)
             else:
                 block = (speed, imped)[f - steps][i]
             part = lax.dot_general(pick, block, (((1,), (1,)), ((), ())), preferred_element_type=jnp.float32)
-            total = part if total is None else total + part
-        rows = layers * EDGE
+            own[f, i * WIDE : (i + 1) * WIDE, :] = part[:WIDE]
+            total = part[WIDE:] if total is None else total + part[WIDE:]
         low[f * rows : (f + 1) * rows, :] = total[:rows].astype(jnp.bfloat16)
         high[f * rows : (f + 1) * rows, :] = total[rows:].astype(jnp.bfloat16)
 
@@ -267,7 +275,7 @@
 
 def strip_layout(steps, y):
     step = STRIP * (y // 128)
-    return step, steps * y, steps * y + steps * step
+    return step, steps * step
 
 
 def coefficients_kernel(speed, imped, stiff, buoy):
@@ -275,65 +283,86 @@
         stiff[i], buoy[i] = coefficients(f32(speed[i]), f32(imped[i]))
 
 
-def cut_kernel(
-    steps, layers, gy_size, src, stiff, buoy, low, high, left, right, far, near, strips,
+def cut_kernel(steps, layers, src, stiff, buoy, far, near, pressure, velocity):
+    y, lanes = stiff.shape[1:]
+    out = Series(Faces(far, near), rows_writer(y))
+    run_cut(
+        Block((y, lanes), None), steps, layers, lambda k, i: brick_block(src, steps - 1 - k, i),
+        lambda i: stiff[i], lambda i: buoy[i], Layers(pressure), Layers(velocity), out.put_load, out.put_flux,
+    )
+
+
+def edge_kernel(steps, layers, gy_size, own, left, right, far, near, strips, whole):
+    y = own.shape[2]
+    rows = layers * EDGE
+    me = lax.axis_index("gy")
+    shape = (layers * WIDE, 2 * rows)
+    r, c = iota(shape, 0), iota(shape, 1)
+    inside = r & (WIDE - 1)
+    at = (r >> 5) * EDGE + (r & 3)
+    wanted = (inside < EDGE) & (c == at) & (me > 0)
+    wanted = wanted | ((inside >= WIDE - EDGE) & (c == rows + at) & (me < gy_size - 1))
+    order = jnp.where(wanted, 1.0, 0.0).astype(jnp.bfloat16)
+
+    def narrow(a):
+        half = STRIP // 2
+        return jnp.concatenate([a[:half], a[WIDE - half :]], 0)
+
+    for f in range(steps + 2):
+        parts = jnp.concatenate([a[f * rows : (f + 1) * rows, :] for a in (left, right)], 0)
+        whole[f] = own[f] + jnp.dot(order, parts, preferred_element_type=jnp.float32)
+        for i in range(layers):
+            strips[f, i * STRIP : (i + 1) * STRIP, :] = narrow(whole[f, i * WIDE : (i + 1) * WIDE, :])
+
+    def strip(f, i):
+        return whole[f, i * WIDE : (i + 1) * WIDE, :]
+
+    faces = Faces(far, near)
+    step, extra = strip_layout(steps, y)
+    last = layers - 1
+    for j, (f, depth) in enumerate(((steps, 0), (steps, 1), (steps + 1, 0), (steps + 1, 1))):
+        faces.put(
+            lambda ref, value, at=extra + j * step: put_strip(ref, at, value),
+            narrow(strip(f, depth)), narrow(strip(f, last - depth)),
+        )
+    coef = [coefficients(strip(steps, i), strip(steps + 1, i)) for i in range(layers)]
+    out = Series(faces, lambda ref, k, a: put_strip(ref, k * step, narrow(a)))
+    run_cut(
+        Strip((WIDE, y), None), steps, layers, lambda k, i: strip(steps - 1 - k, i),
+        lambda i: coef[i][0], lambda i: coef[i][1], {}, {}, out.put_load, out.put_flux,
+    )
+
+
+def outer_key(step, side):
+    return 64 + ((step - 1) * 2 + side) * 8
+
+
+def joined_kernel(
+    steps, layers, src, stiff, buoy, strips, far, near, edge_far, edge_near, coef_far, coef_near,
     pressure, velocity, series, columns,
 ):
     y, lanes = stiff.shape[1:]
-    rows = layers * EDGE
-    me = lax.axis_index("gy")
-    square = (layers * STRIP, layers * STRIP)
-    r, c = iota(square, 0), iota(square, 1)
-    group = (r >> 2) & 3
-    wanted = c == group * rows + (r >> 4) * EDGE + (r & 3)
-    wanted = wanted & jnp.logical_not((group == 0) & (me == 0))
-    wanted = wanted & jnp.logical_not((group == 3) & (me == gy_size - 1))
-    order = jnp.where(wanted, 1.0, 0.0).astype(jnp.bfloat16)
-    for f in range(steps + 2):
-        parts = jnp.concatenate([a[f * rows : (f + 1) * rows, :] for a in (left, low, high, right)], 0)
-        strips[f] = jnp.dot(order, parts, preferred_element_type=jnp.float32)
 
     def strip(f, i):
         return strips[f, i * STRIP : (i + 1) * STRIP, :]
 
-    faces = Faces(far, near)
-    step, base, extra = strip_layout(steps, y)
-    last = layers - 1
-    for j, (f, depth) in enumerate(((steps, 0), (steps, 1), (steps + 1, 0), (steps + 1, 1))):
-        faces.put(
-            lambda ref, value, at=extra + j * step: put_strip(ref, at, value), strip(f, depth), strip(f, last - depth)
-        )
-
-    coef = [coefficients(strip(steps, i), strip(steps + 1, i)) for i in range(layers)]
+    faces = Faces(edge_far, edge_near)
+    step, extra = strip_layout(steps, y)
+    outer = EDGE - 1
     series[...] = jnp.zeros(series.shape, jnp.float32)
-    out = Series(faces, lambda ref, k, a: put_strip(ref, base + k * step, a))
-    run_cut(
-        Strip((STRIP, y), series), steps, layers, lambda k, i: strip(steps - 1 - k, i),
-        lambda i: coef[i][0], lambda i: coef[i][1], {}, {}, out.put_load, out.put_flux,
-    )
-    columns[...] = series[...].T
-
-    out = Series(faces, rows_writer(y))
-    run_cut(
-        Block((y, lanes), columns), steps, layers, lambda k, i: brick_block(src, steps - 1 - k, i),
-        lambda i: stiff[i], lambda i: buoy[i], Layers(pressure), Layers(velocity), out.put_load, out.put_flux,
-    )
-
-
-def joined_kernel(
-    steps, layers, src, stiff, buoy, strips, far, near, coef_far, coef_near,
-    pressure, velocity, series, columns,
-):
-    y, lanes = stiff.shape[1:]
-
-    def strip(f, i):
-        return strips[f, i * STRIP : (i + 1) * STRIP, :]
-
-    faces = Faces(far, near)
-    step, base, extra = strip_layout(steps, y)
 
     def strip_at(at):
         return lambda ref: strip_rows(ref, at, y)
+
+    def edge_face(side):
+        def read(k):
+            a = (faces.above, faces.below)[side](strip_at(k * step))
+            if k > 0:
+                at = outer_key(k, side)
+                series[at : at + outer, :] = a[HIGH - outer : HIGH, :]
+                series[at + outer : at + 2 * outer, :] = a[LOW + 1 : LOW + 1 + outer, :]
+            return a
+        return read
 
     def beside(side, at):
         s = [side(at(j)) for j in range(4)]
@@ -341,22 +370,31 @@
         return stiff, stiff2, buoy, buoy2
 
     coef = [coefficients(strip(steps, i), strip(steps + 1, i)) for i in range(layers)]
-    series[...] = jnp.zeros(series.shape, jnp.float32)
     run_joined(
         Strip((STRIP, y), series), steps, layers, lambda k, i: strip(steps - 1 - k, i),
-        lambda i: coef[i][0], lambda i: coef[i][1], {}, {},
-        lambda k: faces.above(strip_at(base + k * step)), lambda k: faces.below(strip_at(base + k * step)),
+        lambda i: coef[i][0], lambda i: coef[i][1], {}, {}, edge_face(0), edge_face(1),
         beside(faces.above, lambda j: strip_at(extra + j * step)),
         beside(faces.below, lambda j: strip_at(extra + j * step)),
     )
     columns[...] = series[...].T
 
     held = Faces(coef_far, coef_near)
+    main = Faces(far, near)
     read = rows_reader(y)
+    lane = iota((y, lanes), 1)
+
+    def face(side):
+        def get(k):
+            a = (main.above, main.below)[side](read(k))
+            if k == 0:
+                return a
+            placed = pltpu.roll(columns[...], (lanes - outer - outer_key(k, side)) % lanes, 1)
+            return jnp.where((lane < k) | (lane >= lanes - k), placed, a)
+        return get
+
     run_joined(
         Block((y, lanes), columns), steps, layers, lambda k, i: brick_block(src, steps - 1 - k, i),
-        lambda i: stiff[i], lambda i: buoy[i], Layers(pressure), Layers(velocity),
-        lambda k: faces.above(read(k)), lambda k: faces.below(read(k)),
+        lambda i: stiff[i], lambda i: buoy[i], Layers(pressure), Layers(velocity), face(0), face(1),
         beside(held.above, lambda j: lambda ref: f32(ref[j])),
         beside(held.below, lambda j: lambda ref: f32(ref[j])),
     )
@@ -396,34 +434,41 @@
     )(speed, impedance)
     relaid, coef_far, coef_near, stiff, buoy = lax.optimization_barrier((relaid, coef_far, coef_near, stiff, buoy))
 
+    def call(kernel, outs, scratch, *args, name):
+        return pl.pallas_call(kernel, out_shape=outs, scratch_shapes=scratch, compiler_params=params, name=name)(*args)
+
     edge = sds(((steps + 2) * layers * EDGE, y), bf16)
-    low, high = pl.pallas_call(
-        functools.partial(pack_kernel, steps, layers), out_shape=(edge, edge), compiler_params=params, name="pack"
-    )(relaid, speed, impedance)
+    low, high, own = call(
+        functools.partial(pack_kernel, steps, layers),
+        (edge, edge, sds((steps + 2, layers * WIDE, y), jnp.float32)), [], relaid, speed, impedance, name="pack",
+    )
     if gy_size == 2:
         left = right = lax.ppermute(jnp.where(lax.axis_index("gy") == 0, high, low), "gy", [(0, 1), (1, 0)])
     else:
         left, right = shifted(high, "gy", 1), shifted(low, "gy", -1)
 
-    series = [pltpu.VMEM((128, y), jnp.float32), pltpu.VMEM((y, 128), jnp.float32)]
-    message = sds((steps * y + (steps + 4) * STRIP * (y // 128), 128), bf16)
-    far, near, strips = pl.pallas_call(
-        functools.partial(cut_kernel, steps, layers, gy_size),
-        out_shape=(message, message, sds((steps + 2, layers * STRIP, y), jnp.float32)),
-        scratch_shapes=[pltpu.VMEM((layers, y, lanes), jnp.float32), pltpu.VMEM((3, layers, y, lanes), jnp.float32)] + series,
-        compiler_params=params,
-        name="cut",
-    )(relaid, stiff, buoy, low, high, left, right)
-
+    message = sds((steps * y, 128), bf16)
+    far, near = call(
+        functools.partial(cut_kernel, steps, layers), (message, message),
+        [pltpu.VMEM((layers, y, lanes), jnp.float32), pltpu.VMEM((3, layers, y, lanes), jnp.float32)],
+        relaid, stiff, buoy, name="cut",
+    )
+    far, near, left, right = lax.optimization_barrier((far, near, left, right))
     far, near = swapped(far, xs, 1), swapped(near, xs, 0)
 
-    return pl.pallas_call(
-        functools.partial(joined_kernel, steps, layers),
-        out_shape=(field, sds((3, layers, y, lanes), jnp.float32)),
-        scratch_shapes=series,
-        compiler_params=params,
-        name="joined",
-    )(relaid, stiff, buoy, strips, far, near, coef_far, coef_near)
+    message = sds(((steps + 4) * STRIP * (y // 128), 128), bf16)
+    edge_far, edge_near, strips = call(
+        functools.partial(edge_kernel, steps, layers, gy_size),
+        (message, message, sds((steps + 2, layers * STRIP, y), jnp.float32)),
+        [pltpu.VMEM((steps + 2, layers * WIDE, y), jnp.float32)], own, left, right, name="edge",
+    )
+    edge_far, edge_near = swapped(edge_far, xs, 1), swapped(edge_near, xs, 0)
+
+    return call(
+        functools.partial(joined_kernel, steps, layers), (field, sds((3, layers, y, lanes), jnp.float32)),
+        [pltpu.VMEM((128, y), jnp.float32), pltpu.VMEM((y, 128), jnp.float32)],
+        relaid, stiff, buoy, strips, far, near, edge_far, edge_near, coef_far, coef_near, name="joined",
+    )
 
 
 def solution(mesh):

time: 48 us -> 48.2 us (level)
  starting transfers between devices: 15.9 us -> 21.3 us
  waiting for transfers between devices: 21.4 us -> 16.1 us
    ppermute x4 -> x6, starting transfers between devices: 6.98 us -> 12.4 us  [swapped(): return lax.ppermute(block, axis, pairs + [(j, i) for i, j in pairs])]
    ppermute x4 -> x6, waiting for transfers between devices: 14.8 us -> 10.3 us  [swapped(): return lax.ppermute(block, axis, pairs + [(j, i) for i, j in pairs])]
    ppermute x1, waiting for transfers between devices: 2.34 us -> 1.57 us  [on_device(): lax.ppermute(jnp.where(lax.axis_index('gy') == 0, high, low), 'gy', [(0,...]
    pallas_call x3 -> x4, Pallas kernels: 5.69 us -> 5.78 us  [call(): pl.pallas_call(kernel, out_shape=outs, scratch_shapes=scratch, compiler_p...]
  transfers between devices with their start and end apart: 6 -> 8, of which waited for: 4 -> 4; matrix products, arithmetic and copies ran while one was open for 0% -> 0% of each run, Pallas kernels for 0% -> 3%
where the time goes in v3:
time: 48.2 us; the launch traced here: 47.9 us
  starting transfers between devices  21.3 us (44%)
  waiting for transfers between devices  16.1 us (33%)
  Pallas kernels  5.87 us (12%)
  local copies, waits for them, and re-layouts  3.75 us (8%)
  between operations  0.74 us (2%)
    ppermute x6, starting transfers between devices, swapped(): return lax.ppermute(block, axis, pairs + [(j, i) for i, j in pairs])  12.4 us
    ppermute x6, waiting for transfers between devices, swapped(): return lax.ppermute(block, axis, pairs + [(j, i) for i, j in pairs])  10.3 us
    all_to_all x1, starting transfers between devices, on_device(): lax.all_to_all(source.transpose(1, 0, 2, 3), xs, split_axis=0, concat_axi...  7.39 us
    pallas_call x4, Pallas kernels, call(): pl.pallas_call(kernel, out_shape=outs, scratch_shapes=scratch, compiler_p...  5.78 us
    all_to_all x1, waiting for transfers between devices, on_device(): lax.all_to_all(source.transpose(1, 0, 2, 3), xs, split_axis=0, concat_axi...  4.3 us
    unnamed x5, local copies, waits for them, and re-layouts  2.88 us
    ppermute x1, waiting for transfers between devices, on_device(): lax.ppermute(jnp.where(lax.axis_index('gy') == 0, high, low), 'gy', [(0,...  1.57 us
    ppermute x1, starting transfers between devices, on_device(): lax.ppermute(jnp.where(lax.axis_index('gy') == 0, high, low), 'gy', [(0,...  1.56 us
  transfers between devices with their start and end apart: 8, of which 4 were waited for; matrix products, arithmetic and copies ran while one was open for 0% of the time, Pallas kernels for 3%

profile of v3, /device:TPU:0, one launch (start us, length us, event | category | flops | bytes accessed | tf_op | source)
XLA Modules:
  0.0 47.9 jit_solution(9214978159045305472)
XLA Ops:
  0.6 1.9 %copy.8 = bf16[4,64,8,128]{3,2,0,1:T(8,128)(2,1)} copy(bf16[4,64,8,128]{3,2,1,0:T(8,128)(2,1)} %param.3) | data formatting | bytes 1048576 | tf_op args[0]
  2.6 7.4 %all-to-all-start = ((bf16[64,4,8,128]{3,2,1,0:T(8,128)(2,1)}), bf16[64,4,8,128]{3,2,1,0:T(8,128)(2,1)S(1)}, u32[]{:S(2)}, u32[]{:S(2)}) async-start(bf16[64,4,8,128]{3,2,1,0:T(8,128)(2,1)} %bitcast.3), calls=%async_computation | async-start | bytes 1048576 | tf_op jit(solution)/shard_map/all_to_all | solution.py:429
  10.0 0.0 copy-start
  10.0 0.0 copy-start.1
  10.0 0.9 %copy-done = bf16[4,128,128]{2,1,0:T(8,128)(2,1)S(1)} copy-done((bf16[4,128,128]{2,1,0:T(8,128)(2,1)S(1)}, bf16[4,128,128]{2,1,0:T(8,128)(2,1)}, u32[]{:S(2)}) %copy-start) | copy-done | bytes 131096
  10.9 0.1 copy-done.1
  10.9 0.0 slice-start
  10.9 0.0 slice-start.1
  11.0 0.8 %slice-done = bf16[2,128,128]{2,1,0:T(8,128)(2,1)S(1)} async-done(((bf16[4,128,128]{2,1,0:T(8,128)(2,1)}), bf16[2,128,128]{2,1,0:T(8,128)(2,1)S(1)}, s32[]{:S(2)}) %slice-start) | async-done | bytes 65560 | tf_op jit(solution)/shard_map/slice | solution.py:424
  11.8 0.0 slice-done.1
  11.8 2.0 %collective-permute-start.1 = (bf16[4,128,128]{2,1,0:T(8,128)(2,1)S(1)}, bf16[4,128,128]{2,1,0:T(8,128)(2,1)S(1)}, u32[]{:S(2)}, u32[]{:S(2)}) collective-permute-start(bf16[4,128,128]{2,1,0:T(8,128)(2,1)S(1)} %get-tuple-element.40), channel_id=1, source_target_pairs={{0,2},{4,6},{8,10},{12,14},{16,18},{20,22},{24,26},{28,30},{2,0},{... | collective-permute-start | bytes 393224 | tf_op jit(solution)/shard_map/ppermute | solution.py:410
  13.8 0.7 %collective-permute-start = (bf16[4,128,128]{2,1,0:T(8,128)(2,1)S(1)}, bf16[4,128,128]{2,1,0:T(8,128)(2,1)S(1)}, u32[]{:S(2)}, u32[]{:S(2)}) collective-permute-start(bf16[4,128,128]{2,1,0:T(8,128)(2,1)S(1)} %get-tuple-element.41), channel_id=1, source_target_pairs={{2,4},{6,8},{10,12},{14,16},{18,20},{22,24},{26,28},{4,2},{8,6},{1... | collective-permute-start | bytes 393224 | tf_op jit(solution)/shard_map/ppermute | solution.py:410
  14.5 0.1 coefficients.1
  14.6 8.3 %collective-permute-done.1.coef_near = bf16[4,128,128]{2,1,0:T(8,128)(2,1)S(1)} collective-permute-done((bf16[4,128,128]{2,1,0:T(8,128)(2,1)S(1)}, bf16[4,128,128]{2,1,0:T(8,128)(2,1)S(1)}, u32[]{:S(2)}, u32[]{:S(2)}) %collective-permute-start.1) | collective-permute-done | bytes 131104 | tf_op jit(solution)/shard_map/ppermute | solution.py:410
  22.9 0.0 collective-permute-done.coef_far
  22.9 4.3 %all-to-all-done = bf16[64,4,8,128]{3,2,1,0:T(8,128)(2,1)S(1)} async-done(((bf16[64,4,8,128]{3,2,1,0:T(8,128)(2,1)}), bf16[64,4,8,128]{3,2,1,0:T(8,128)(2,1)S(1)}, u32[]{:S(2)}, u32[]{:S(2)}) %all-to-all-start) | async-done | bytes 524320 | tf_op jit(solution)/shard_map/all_to_all | solution.py:429
  27.2 0.6 %pack.1 = (bf16[96,128]{1,0:T(8,128)(2,1)S(1)}, bf16[96,128]{1,0:T(8,128)(2,1)S(1)}, f32[6,128,128]{2,1,0:T(8,128)S(1)}) custom-call(bf16[16,4,4,8,128]{4,3,2,1,0:T(8,128)(2,1)S(1)} %bitcast.4, bf16[4,128,128]{2,1,0:T(8,128)(2,1)S(1)} %copy-done, bf16[4,128,128]{2,1,0:T(8,128)(2,1)S(1)} %copy-done.1), custom_call_target="tpu_custom_call" | custom-call | tf_op jit(solution)/shard_map/pack/pallas_call | solution.py:438
  27.8 1.6 %collective-permute-start.2 = (bf16[96,128]{1,0:T(8,128)(2,1)S(1)}, bf16[96,128]{1,0:T(8,128)(2,1)S(1)}, u32[]{:S(2)}, u32[]{:S(2)}) collective-permute-start(bf16[96,128]{1,0:T(8,128)(2,1)S(1)} %broadcast_select_fusion.2), channel_id=1, source_target_pairs={{0,1},{1,0},{2,3},{3,2},{4,5},{5,4},{6,7},{7,6},{8,9},{9,8},{10,11... | collective-permute-start | bytes 73736 | tf_op jit(solution)/shard_map/ppermute | solution.py:446
  29.4 0.8 %cut.1 = (bf16[512,128]{1,0:T(8,128)(2,1)S(1)}, bf16[512,128]{1,0:T(8,128)(2,1)S(1)}) custom-call(bf16[16,4,4,8,128]{4,3,2,1,0:T(8,128)(2,1)S(1)} %bitcast.5, f32[4,128,128]{2,1,0:T(8,128)S(1)} %get-tuple-element.24.stiff, f32[4,128,128]{2,1,0:T(8,128)S(1)} %get-tuple-element.25.buoy), custom_call_target="tpu_custom_call" | custom-call | tf_op jit(solution)/shard_map/cut/pallas_call | solution.py:438
  30.1 1.6 %collective-permute-done.2.left.right = bf16[96,128]{1,0:T(8,128)(2,1)S(1)} collective-permute-done((bf16[96,128]{1,0:T(8,128)(2,1)S(1)}, bf16[96,128]{1,0:T(8,128)(2,1)S(1)}, u32[]{:S(2)}, u32[]{:S(2)}) %collective-permute-start.2) | collective-permute-done | bytes 24608 | tf_op jit(solution)/shard_map/ppermute | solution.py:446
  31.7 0.7 %collective-permute-start.3 = (bf16[512,128]{1,0:T(8,128)(2,1)S(1)}, bf16[512,128]{1,0:T(8,128)(2,1)S(1)}, u32[]{:S(2)}, u32[]{:S(2)}) collective-permute-start(bf16[512,128]{1,0:T(8,128)(2,1)S(1)} %get-tuple-element.34), channel_id=1, source_target_pairs={{2,4},{6,8},{10,12},{14,16},{18,20},{22,24},{26,28},{4,2},{8,6},{1... | collective-permute-start | bytes 393224 | tf_op jit(solution)/shard_map/ppermute | solution.py:410
  32.4 3.7 %collective-permute-start.4 = (bf16[512,128]{1,0:T(8,128)(2,1)S(1)}, bf16[512,128]{1,0:T(8,128)(2,1)S(1)}, u32[]{:S(2)}, u32[]{:S(2)}) collective-permute-start(bf16[512,128]{1,0:T(8,128)(2,1)S(1)} %get-tuple-element.35), channel_id=1, source_target_pairs={{0,2},{4,6},{8,10},{12,14},{16,18},{20,22},{24,26},{28,30},{2,0},{... | collective-permute-start | bytes 393224 | tf_op jit(solution)/shard_map/ppermute | solution.py:410
  36.0 0.6 %edge.1 = (bf16[128,128]{1,0:T(8,128)(2,1)S(1)}, bf16[128,128]{1,0:T(8,128)(2,1)S(1)}, f32[6,64,128]{2,1,0:T(8,128)S(1)}) custom-call(f32[6,128,128]{2,1,0:T(8,128)S(1)} %get-tuple-element.26.own, bf16[96,128]{1,0:T(8,128)(2,1)S(1)} %collective-permute-done.2.left.right, bf16[96,128]{1,0:T(8,128)(2,1)S(1)} %collective-permute-done.2.left.right), custom_call_target="tpu_custom_call" | custom-call | tf_op jit(solution)/shard_map/edge/pallas_call | solution.py:438
  36.7 0.7 %collective-permute-start.5 = (bf16[128,128]{1,0:T(8,128)(2,1)S(1)}, bf16[128,128]{1,0:T(8,128)(2,1)S(1)}, u32[]{:S(2)}, u32[]{:S(2)}) collective-permute-start(bf16[128,128]{1,0:T(8,128)(2,1)S(1)} %get-tuple-element.36), channel_id=1, source_target_pairs={{2,4},{6,8},{10,12},{14,16},{18,20},{22,24},{26,28},{4,2},{8,6},{1... | collective-permute-start | bytes 98312 | tf_op jit(solution)/shard_map/ppermute | solution.py:410
  37.4 4.7 %collective-permute-start.6 = (bf16[128,128]{1,0:T(8,128)(2,1)S(1)}, bf16[128,128]{1,0:T(8,128)(2,1)S(1)}, u32[]{:S(2)}, u32[]{:S(2)}) collective-permute-start(bf16[128,128]{1,0:T(8,128)(2,1)S(1)} %get-tuple-element.37), channel_id=1, source_target_pairs={{0,2},{4,6},{8,10},{12,14},{16,18},{20,22},{24,26},{28,30},{2,0},{... | collective-permute-start | bytes 98312 | tf_op jit(solution)/shard_map/ppermute | solution.py:410
  42.1 0.0 collective-permute-done.5.edge_far
  42.1 2.0 %collective-permute-done.6.edge_near = bf16[128,128]{1,0:T(8,128)(2,1)S(1)} collective-permute-done((bf16[128,128]{1,0:T(8,128)(2,1)S(1)}, bf16[128,128]{1,0:T(8,128)(2,1)S(1)}, u32[]{:S(2)}, u32[]{:S(2)}) %collective-permute-start.6) | collective-permute-done | bytes 32800 | tf_op jit(solution)/shard_map/ppermute | solution.py:410
  44.1 0.0 collective-permute-done.3.far
  44.1 0.0 collective-permute-done.4.near
  44.1 3.8 %joined.1 = (f32[4,128,128]{2,1,0:T(8,128)}, f32[3,4,128,128]{3,2,1,0:T(8,128)}) custom-call(bf16[16,4,4,8,128]{4,3,2,1,0:T(8,128)(2,1)S(1)} %bitcast.6, f32[4,128,128]{2,1,0:T(8,128)S(1)} %get-tuple-element.24.stiff, f32[4,128,128]{2,1,0:T(8,128)S(1)} %get-tuple-element.25.buoy, f32[6,64,128]{2,1,0:T(8,128)S(1)} %get-tuple-element.33.strips, ...), custom_call_target="tpu_custom_call" | custom-call | tf_op jit(solution)/shard_map/joined/pallas_call | solution.py:438
  (3 shorter events, 0.1 us)
Async XLA Ops:
  2.6 24.6 %all-to-all-start = ((bf16[64,4,8,128]{3,2,1,0:T(8,128)(2,1)}), bf16[64,4,8,128]{3,2,1,0:T(8,128)(2,1)S(1)}, u32[]{:S(2)}, u32[]{:S(2)}) async-start(bf16[64,4,8,128]{3,2,1,0:T(8,128)(2,1)} %bitcast.3), calls=%async_computation | async-start | bytes 1048576 | tf_op jit(solution)/shard_map/all_to_all | solution.py:429
  10.0 0.9 %copy-start = (bf16[4,128,128]{2,1,0:T(8,128)(2,1)S(1)}, bf16[4,128,128]{2,1,0:T(8,128)(2,1)}, u32[]{:S(2)}) copy-start(bf16[4,128,128]{2,1,0:T(8,128)(2,1)} %speed.3) | copy-start | bytes 393220
  10.0 1.0 %copy-start.1 = (bf16[4,128,128]{2,1,0:T(8,128)(2,1)S(1)}, bf16[4,128,128]{2,1,0:T(8,128)(2,1)}, u32[]{:S(2)}) copy-start(bf16[4,128,128]{2,1,0:T(8,128)(2,1)} %imped.3) | copy-start | bytes 393220
  10.9 0.8 %slice-start = ((bf16[4,128,128]{2,1,0:T(8,128)(2,1)}), bf16[2,128,128]{2,1,0:T(8,128)(2,1)S(1)}, s32[]{:S(2)}) async-start(bf16[4,128,128]{2,1,0:T(8,128)(2,1)} %speed.3), calls=%async_computation.1 | async-start | bytes 131072 | tf_op jit(solution)/shard_map/slice | solution.py:424
  10.9 0.9 %slice-start.1 = ((bf16[4,128,128]{2,1,0:T(8,128)(2,1)}), bf16[2,128,128]{2,1,0:T(8,128)(2,1)S(1)}, s32[]{:S(2)}) async-start(bf16[4,128,128]{2,1,0:T(8,128)(2,1)} %imped.3), calls=%async_computation.2 | async-start | bytes 131072 | tf_op jit(solution)/shard_map/slice | solution.py:424
  11.8 11.0 %collective-permute-start.1 = (bf16[4,128,128]{2,1,0:T(8,128)(2,1)S(1)}, bf16[4,128,128]{2,1,0:T(8,128)(2,1)S(1)}, u32[]{:S(2)}, u32[]{:S(2)}) collective-permute-start(bf16[4,128,128]{2,1,0:T(8,128)(2,1)S(1)} %get-tuple-element.40), channel_id=1, source_target_pairs={{0,2},{4,6},{8,10},{12,14},{16,18},{20,22},{24,26},{28,30},{2,0},{... | collective-permute-start | bytes 393224 | tf_op jit(solution)/shard_map/ppermute | solution.py:410
  13.8 9.0 %collective-permute-start = (bf16[4,128,128]{2,1,0:T(8,128)(2,1)S(1)}, bf16[4,128,128]{2,1,0:T(8,128)(2,1)S(1)}, u32[]{:S(2)}, u32[]{:S(2)}) collective-permute-start(bf16[4,128,128]{2,1,0:T(8,128)(2,1)S(1)} %get-tuple-element.41), channel_id=1, source_target_pairs={{2,4},{6,8},{10,12},{14,16},{18,20},{22,24},{26,28},{4,2},{8,6},{1... | collective-permute-start | bytes 393224 | tf_op jit(solution)/shard_map/ppermute | solution.py:410
  27.8 3.9 %collective-permute-start.2 = (bf16[96,128]{1,0:T(8,128)(2,1)S(1)}, bf16[96,128]{1,0:T(8,128)(2,1)S(1)}, u32[]{:S(2)}, u32[]{:S(2)}) collective-permute-start(bf16[96,128]{1,0:T(8,128)(2,1)S(1)} %broadcast_select_fusion.2), channel_id=1, source_target_pairs={{0,1},{1,0},{2,3},{3,2},{4,5},{5,4},{6,7},{7,6},{8,9},{9,8},{10,11... | collective-permute-start | bytes 73736 | tf_op jit(solution)/shard_map/ppermute | solution.py:446
  31.7 12.4 %collective-permute-start.3 = (bf16[512,128]{1,0:T(8,128)(2,1)S(1)}, bf16[512,128]{1,0:T(8,128)(2,1)S(1)}, u32[]{:S(2)}, u32[]{:S(2)}) collective-permute-start(bf16[512,128]{1,0:T(8,128)(2,1)S(1)} %get-tuple-element.34), channel_id=1, source_target_pairs={{2,4},{6,8},{10,12},{14,16},{18,20},{22,24},{26,28},{4,2},{8,6},{1... | collective-permute-start | bytes 393224 | tf_op jit(solution)/shard_map/ppermute | solution.py:410
  32.4 11.7 %collective-permute-start.4 = (bf16[512,128]{1,0:T(8,128)(2,1)S(1)}, bf16[512,128]{1,0:T(8,128)(2,1)S(1)}, u32[]{:S(2)}, u32[]{:S(2)}) collective-permute-start(bf16[512,128]{1,0:T(8,128)(2,1)S(1)} %get-tuple-element.35), channel_id=1, source_target_pairs={{0,2},{4,6},{8,10},{12,14},{16,18},{20,22},{24,26},{28,30},{2,0},{... | collective-permute-start | bytes 393224 | tf_op jit(solution)/shard_map/ppermute | solution.py:410
  36.7 5.4 %collective-permute-start.5 = (bf16[128,128]{1,0:T(8,128)(2,1)S(1)}, bf16[128,128]{1,0:T(8,128)(2,1)S(1)}, u32[]{:S(2)}, u32[]{:S(2)}) collective-permute-start(bf16[128,128]{1,0:T(8,128)(2,1)S(1)} %get-tuple-element.36), channel_id=1, source_target_pairs={{2,4},{6,8},{10,12},{14,16},{18,20},{22,24},{26,28},{4,2},{8,6},{1... | collective-permute-start | bytes 98312 | tf_op jit(solution)/shard_map/ppermute | solution.py:410
  37.4 6.7 %collective-permute-start.6 = (bf16[128,128]{1,0:T(8,128)(2,1)S(1)}, bf16[128,128]{1,0:T(8,128)(2,1)S(1)}, u32[]{:S(2)}, u32[]{:S(2)}) collective-permute-start(bf16[128,128]{1,0:T(8,128)(2,1)S(1)} %get-tuple-element.37), channel_id=1, source_target_pairs={{0,2},{4,6},{8,10},{12,14},{16,18},{20,22},{24,26},{28,30},{2,0},{... | collective-permute-start | bytes 98312 | tf_op jit(solution)/shard_map/ppermute | solution.py:410

commit v4 on v3

--- a/solution.py
+++ b/solution.py
@@ -126,7 +126,7 @@
             below = fx
 
 
-def run_joined(space, steps, layers, src, stiff, buoy, pressure, velocity, load_in, flux_in, up, down):
+def run_joined(space, steps, layers, src, stiff, buoy, pressure, velocity, load_in, flux_in, up, down, finished=None):
     everywhere = tuple(range(layers))
     above, under = layers, layers + 1
     pa = xa = ya = za = pa2 = None
@@ -170,6 +170,8 @@
             spread = spread + space.bwd_z(buoy(i) * z, flux_key(k, i))
             pressure[i] = pressure[i] + spread
             below = fx
+            if k == steps - 1 and finished is not None:
+                finished(i)
         if k == steps - 1:
             return
         if k == 0:
@@ -252,17 +254,6 @@
         return jnp.where(self.even, read(self.far), read(self.near))
 
 
-class Series:
-    def __init__(self, faces, write):
-        self.faces, self.write, self.loads = faces, write, {}
-
-    def put_load(self, k, a):
-        self.loads[k] = a
-
-    def put_flux(self, k, a):
-        self.faces.put(lambda ref, value: self.write(ref, k, value), self.loads[k], a)
-
-
 def rows_writer(rows):
     def write(ref, k, a):
         ref[k * rows : (k + 1) * rows, :] = a.astype(jnp.bfloat16)
@@ -275,7 +266,12 @@
 
 def strip_layout(steps, y):
     step = STRIP * (y // 128)
-    return step, steps * step
+    return step, steps * y, steps * y + steps * step
+
+
+def bricks_kernel(source, bricks):
+    for k in range(source.shape[0]):
+        bricks[:, k] = source[k]
 
 
 def coefficients_kernel(speed, imped, stiff, buoy):
@@ -283,17 +279,20 @@
         stiff[i], buoy[i] = coefficients(f32(speed[i]), f32(imped[i]))
 
 
-def cut_kernel(steps, layers, src, stiff, buoy, far, near, pressure, velocity):
+def cut_kernel(steps, layers, src, stiff, buoy, loads, fluxes, pressure, velocity):
     y, lanes = stiff.shape[1:]
-    out = Series(Faces(far, near), rows_writer(y))
+    write = rows_writer(y)
     run_cut(
         Block((y, lanes), None), steps, layers, lambda k, i: brick_block(src, steps - 1 - k, i),
-        lambda i: stiff[i], lambda i: buoy[i], Layers(pressure), Layers(velocity), out.put_load, out.put_flux,
-    )
-
-
-def edge_kernel(steps, layers, gy_size, own, left, right, far, near, strips, whole):
-    y = own.shape[2]
+        lambda i: stiff[i], lambda i: buoy[i], Layers(pressure), Layers(velocity),
+        lambda k, a: write(loads, k, a), lambda k, a: write(fluxes, k, a),
+    )
+
+
+def edge_kernel(
+    steps, layers, gy_size, own, left, right, loads, fluxes, far, near, strips, whole, series, columns
+):
+    y, lanes = own.shape[2], loads.shape[1]
     rows = layers * EDGE
     me = lax.axis_index("gy")
     shape = (layers * WIDE, 2 * rows)
@@ -318,7 +317,7 @@
         return whole[f, i * WIDE : (i + 1) * WIDE, :]
 
     faces = Faces(far, near)
-    step, extra = strip_layout(steps, y)
+    step, base, extra = strip_layout(steps, y)
     last = layers - 1
     for j, (f, depth) in enumerate(((steps, 0), (steps, 1), (steps + 1, 0), (steps + 1, 1))):
         faces.put(
@@ -326,43 +325,55 @@
             narrow(strip(f, depth)), narrow(strip(f, last - depth)),
         )
     coef = [coefficients(strip(steps, i), strip(steps + 1, i)) for i in range(layers)]
-    out = Series(faces, lambda ref, k, a: put_strip(ref, k * step, narrow(a)))
+    strip_loads, strip_fluxes = {}, {}
     run_cut(
         Strip((WIDE, y), None), steps, layers, lambda k, i: strip(steps - 1 - k, i),
-        lambda i: coef[i][0], lambda i: coef[i][1], {}, {}, out.put_load, out.put_flux,
-    )
-
-
-def outer_key(step, side):
-    return 64 + ((step - 1) * 2 + side) * 8
-
-
-def joined_kernel(
-    steps, layers, src, stiff, buoy, strips, far, near, edge_far, edge_near, coef_far, coef_near,
-    pressure, velocity, series, columns,
-):
-    y, lanes = stiff.shape[1:]
-
-    def strip(f, i):
-        return strips[f, i * STRIP : (i + 1) * STRIP, :]
-
-    faces = Faces(edge_far, edge_near)
-    step, extra = strip_layout(steps, y)
+        lambda i: coef[i][0], lambda i: coef[i][1], {}, {}, strip_loads.__setitem__, strip_fluxes.__setitem__,
+    )
     outer = EDGE - 1
     series[...] = jnp.zeros(series.shape, jnp.float32)
-
-    def strip_at(at):
-        return lambda ref: strip_rows(ref, at, y)
-
-    def edge_face(side):
-        def read(k):
-            a = (faces.above, faces.below)[side](strip_at(k * step))
-            if k > 0:
+    for k in range(steps):
+        pair = narrow(strip_loads[k]), narrow(strip_fluxes[k])
+        faces.put(lambda ref, value: put_strip(ref, base + k * step, value), *pair)
+        if k > 0:
+            for side, a in enumerate(pair):
                 at = outer_key(k, side)
                 series[at : at + outer, :] = a[HIGH - outer : HIGH, :]
                 series[at + outer : at + 2 * outer, :] = a[LOW + 1 : LOW + 1 + outer, :]
+    columns[...] = series[...].T
+
+    lane = iota((y, lanes), 1)
+    read, write = rows_reader(y), rows_writer(y)
+
+    def merged(ref, k, side):
+        a = read(k)(ref)
+        if k == 0:
             return a
-        return read
+        placed = pltpu.roll(columns[...], (lanes - outer - outer_key(k, side)) % lanes, 1)
+        return jnp.where((lane < k) | (lane >= lanes - k), placed, a)
+
+    for k in range(steps):
+        faces.put(lambda ref, value: write(ref, k, value), merged(loads, k, 0), merged(fluxes, k, 1))
+
+
+def outer_key(step, side):
+    return ((step - 1) * 2 + side) * 8
+
+
+def joined_kernel(
+    steps, layers, src, stiff, buoy, strips, far, near, coef_far, coef_near, pressure_out, velocity_out,
+    pressure, velocity, series, columns, sems,
+):
+    y, lanes = stiff.shape[1:]
+
+    def strip(f, i):
+        return strips[f, i * STRIP : (i + 1) * STRIP, :]
+
+    faces = Faces(far, near)
+    step, base, extra = strip_layout(steps, y)
+
+    def strip_at(at):
+        return lambda ref: strip_rows(ref, at, y)
 
     def beside(side, at):
         s = [side(at(j)) for j in range(4)]
@@ -370,34 +381,39 @@
         return stiff, stiff2, buoy, buoy2
 
     coef = [coefficients(strip(steps, i), strip(steps + 1, i)) for i in range(layers)]
+    series[...] = jnp.zeros(series.shape, jnp.float32)
     run_joined(
         Strip((STRIP, y), series), steps, layers, lambda k, i: strip(steps - 1 - k, i),
-        lambda i: coef[i][0], lambda i: coef[i][1], {}, {}, edge_face(0), edge_face(1),
+        lambda i: coef[i][0], lambda i: coef[i][1], {}, {},
+        lambda k: faces.above(strip_at(base + k * step)), lambda k: faces.below(strip_at(base + k * step)),
         beside(faces.above, lambda j: strip_at(extra + j * step)),
         beside(faces.below, lambda j: strip_at(extra + j * step)),
     )
     columns[...] = series[...].T
 
+    def copies(i):
+        return (
+            pltpu.make_async_copy(velocity.at[:, i], velocity_out.at[:, i], sems.at[0, i]),
+            pltpu.make_async_copy(pressure.at[i], pressure_out.at[i], sems.at[1, i]),
+        )
+
+    def send(i):
+        for copy in copies(i):
+            copy.start()
+
     held = Faces(coef_far, coef_near)
-    main = Faces(far, near)
     read = rows_reader(y)
-    lane = iota((y, lanes), 1)
-
-    def face(side):
-        def get(k):
-            a = (main.above, main.below)[side](read(k))
-            if k == 0:
-                return a
-            placed = pltpu.roll(columns[...], (lanes - outer - outer_key(k, side)) % lanes, 1)
-            return jnp.where((lane < k) | (lane >= lanes - k), placed, a)
-        return get
-
     run_joined(
         Block((y, lanes), columns), steps, layers, lambda k, i: brick_block(src, steps - 1 - k, i),
-        lambda i: stiff[i], lambda i: buoy[i], Layers(pressure), Layers(velocity), face(0), face(1),
+        lambda i: stiff[i], lambda i: buoy[i], Layers(pressure), Layers(velocity),
+        lambda k: faces.above(read(k)), lambda k: faces.below(read(k)),
         beside(held.above, lambda j: lambda ref: f32(ref[j])),
         beside(held.below, lambda j: lambda ref: f32(ref[j])),
-    )
+        send,
+    )
+    for i in range(layers):
+        for copy in copies(i):
+            copy.wait()
 
 
 def shifted(block, axis, distance):
@@ -426,7 +442,17 @@
     even = is_even()
     coef_far, coef_near = jnp.where(even, below, above), jnp.where(even, above, below)
     coef_far, coef_near = swapped(coef_far, xs, 1), swapped(coef_near, xs, 0)
-    relaid = lax.all_to_all(source.transpose(1, 0, 2, 3), xs, split_axis=0, concat_axis=0, tiled=True)
+    chunk = whole_x // 4
+    bricks = pl.pallas_call(
+        bricks_kernel,
+        grid=(4,),
+        in_specs=[pl.BlockSpec((steps, chunk, brick_y, lanes), lambda j: (0, j, 0, 0))],
+        out_specs=pl.BlockSpec((chunk, steps, brick_y, lanes), lambda j: (j, 0, 0, 0)),
+        out_shape=sds((whole_x, steps, brick_y, lanes), bf16),
+        compiler_params=pltpu.CompilerParams(vmem_limit_bytes=60 * 1024 * 1024),
+        name="bricks",
+    )(source)
+    relaid = lax.all_to_all(bricks, xs, split_axis=0, concat_axis=0, tiled=True)
     relaid = relaid.reshape(whole_x // layers, layers, steps, brick_y, lanes)
     field = sds((layers, y, lanes), jnp.float32)
     stiff, buoy = pl.pallas_call(
@@ -447,28 +473,33 @@
     else:
         left, right = shifted(high, "gy", 1), shifted(low, "gy", -1)
 
-    message = sds((steps * y, 128), bf16)
-    far, near = call(
-        functools.partial(cut_kernel, steps, layers), (message, message),
-        [pltpu.VMEM((layers, y, lanes), jnp.float32), pltpu.VMEM((3, layers, y, lanes), jnp.float32)],
-        relaid, stiff, buoy, name="cut",
-    )
-    far, near, left, right = lax.optimization_barrier((far, near, left, right))
-    far, near = swapped(far, xs, 1), swapped(near, xs, 0)
-
-    message = sds(((steps + 4) * STRIP * (y // 128), 128), bf16)
-    edge_far, edge_near, strips = call(
+    whole = pltpu.VMEM((layers, y, lanes), jnp.float32)
+    whole_velocity = pltpu.VMEM((3, layers, y, lanes), jnp.float32)
+    series = [pltpu.VMEM((128, y), jnp.float32), pltpu.VMEM((y, 128), jnp.float32)]
+    face = sds((steps * y, 128), bf16)
+    loads, fluxes = call(
+        functools.partial(cut_kernel, steps, layers), (face, face), [whole, whole_velocity], relaid, stiff, buoy, name="cut"
+    )
+    _, _, extra = strip_layout(steps, y)
+    message = sds((extra + 4 * STRIP * (y // 128), 128), bf16)
+    far, near, strips = call(
         functools.partial(edge_kernel, steps, layers, gy_size),
         (message, message, sds((steps + 2, layers * STRIP, y), jnp.float32)),
-        [pltpu.VMEM((steps + 2, layers * WIDE, y), jnp.float32)], own, left, right, name="edge",
-    )
-    edge_far, edge_near = swapped(edge_far, xs, 1), swapped(edge_near, xs, 0)
-
-    return call(
-        functools.partial(joined_kernel, steps, layers), (field, sds((3, layers, y, lanes), jnp.float32)),
-        [pltpu.VMEM((128, y), jnp.float32), pltpu.VMEM((y, 128), jnp.float32)],
-        relaid, stiff, buoy, strips, far, near, edge_far, edge_near, coef_far, coef_near, name="joined",
-    )
+        [pltpu.VMEM((steps + 2, layers * WIDE, y), jnp.float32)] + series,
+        own, left, right, loads, fluxes, name="edge",
+    )
+    far, near = swapped(far, xs, 1), swapped(near, xs, 0)
+
+    args = relaid, stiff, buoy, strips, far, near, coef_far, coef_near
+    return pl.pallas_call(
+        functools.partial(joined_kernel, steps, layers),
+        in_specs=[pl.BlockSpec(memory_space=pltpu.VMEM)] * len(args),
+        out_specs=(pl.BlockSpec(memory_space=pl.ANY), pl.BlockSpec(memory_space=pl.ANY)),
+        out_shape=(field, sds((3, layers, y, lanes), jnp.float32)),
+        scratch_shapes=[whole, whole_velocity] + series + [pltpu.SemaphoreType.DMA((2, layers))],
+        compiler_params=params,
+        name="joined",
+    )(*args)
 
 
 def solution(mesh):

time: 48.2 us -> 48.5 us (level)
  starting transfers between devices: 21.3 us -> 15.9 us
  waiting for transfers between devices: 16.1 us -> 20.6 us
  Pallas kernels: 5.87 us -> 8.99 us
  local copies, waits for them, and re-layouts: 3.75 us -> 1.82 us
    pallas_call x0 -> x2, Pallas kernels: none -> 6.66 us  [the longest x1 3.47 us: on_device(): pl.pallas_call(functools.partial(joined_kernel, steps, layers), in_specs=...]
    ppermute x6 -> x4, starting transfers between devices: 12.4 us -> 6.97 us  [swapped(): return lax.ppermute(block, axis, pairs + [(j, i) for i, j in pairs])]
    ppermute x6 -> x4, waiting for transfers between devices: 10.3 us -> 14.8 us  [swapped(): return lax.ppermute(block, axis, pairs + [(j, i) for i, j in pairs])]
    pallas_call x4 -> x3, Pallas kernels: 5.78 us -> 2.24 us  [call(): pl.pallas_call(kernel, out_shape=outs, scratch_shapes=scratch, compiler_p...]
    unnamed x5 -> x4, local copies, waits for them, and re-layouts: 2.88 us -> 0.96 us
  transfers between devices with their start and end apart: 8 -> 6, of which waited for: 4 -> 4; matrix products, arithmetic and copies ran while one was open for 0% -> 0% of each run, Pallas kernels for 3% -> 2%
where the time goes in v4:
time: 48.5 us; the launch traced here: 48.2 us
  waiting for transfers between devices  20.6 us (42%)
  starting transfers between devices  15.9 us (33%)
  Pallas kernels  8.99 us (19%)
  local copies, waits for them, and re-layouts  1.82 us (4%)
  between operations  0.73 us (2%)
    ppermute x4, waiting for transfers between devices, swapped(): return lax.ppermute(block, axis, pairs + [(j, i) for i, j in pairs])  14.8 us
    all_to_all x1, starting transfers between devices, on_device(): relaid = lax.all_to_all(bricks, xs, split_axis=0, concat_axis=0, tiled=True)  7.39 us
    ppermute x4, starting transfers between devices, swapped(): return lax.ppermute(block, axis, pairs + [(j, i) for i, j in pairs])  6.97 us
    all_to_all x1, waiting for transfers between devices, on_device(): relaid = lax.all_to_all(bricks, xs, split_axis=0, concat_axis=0, tiled=True)  4.3 us
    pallas_call x1, Pallas kernels, on_device(): pl.pallas_call(functools.partial(joined_kernel, steps, layers), in_specs=...  3.47 us
    pallas_call x1, Pallas kernels, on_device(): pl.pallas_call(bricks_kernel, grid=(4,), in_specs=[pl.BlockSpec((steps, c...  3.19 us
    pallas_call x3, Pallas kernels, call(): pl.pallas_call(kernel, out_shape=outs, scratch_shapes=scratch, compiler_p...  2.24 us
    ppermute x1, waiting for transfers between devices, on_device(): lax.ppermute(jnp.where(lax.axis_index('gy') == 0, high, low), 'gy', [(0,...  1.57 us
  transfers between devices with their start and end apart: 6, of which 4 were waited for; matrix products, arithmetic and copies ran while one was open for 0% of the time, Pallas kernels for 2%

profile of v4, /device:TPU:0, one launch (start us, length us, event | category | flops | bytes accessed | tf_op | source)
XLA Modules:
  0.0 48.2 jit_solution(168733711961734996)
XLA Ops:
  0.6 3.2 %bricks.1 = bf16[64,4,8,128]{3,2,1,0:T(8,128)(2,1)} custom-call(bf16[4,64,8,128]{3,2,1,0:T(8,128)(2,1)} %source.1), custom_call_target="tpu_custom_call" | custom-call | tf_op jit(solution)/shard_map/bricks/pallas_call | solution.py:446
  3.8 7.4 %all-to-all-start = ((bf16[64,4,8,128]{3,2,1,0:T(8,128)(2,1)}), bf16[64,4,8,128]{3,2,1,0:T(8,128)(2,1)S(1)}, u32[]{:S(2)}, u32[]{:S(2)}) async-start(bf16[64,4,8,128]{3,2,1,0:T(8,128)(2,1)} %bricks.1), calls=%async_computation | async-start | bytes 1048576 | tf_op jit(solution)/shard_map/all_to_all | solution.py:455
  11.2 0.0 copy-start
  11.2 0.0 copy-start.1
  11.3 0.9 %copy-done = bf16[4,128,128]{2,1,0:T(8,128)(2,1)S(1)} copy-done((bf16[4,128,128]{2,1,0:T(8,128)(2,1)S(1)}, bf16[4,128,128]{2,1,0:T(8,128)(2,1)}, u32[]{:S(2)}) %copy-start) | copy-done | bytes 131096
  12.1 0.1 copy-done.1
  12.2 0.0 slice-start
  12.2 0.0 slice-start.1
  12.2 0.8 %slice-done = bf16[2,128,128]{2,1,0:T(8,128)(2,1)S(1)} async-done(((bf16[4,128,128]{2,1,0:T(8,128)(2,1)}), bf16[2,128,128]{2,1,0:T(8,128)(2,1)S(1)}, s32[]{:S(2)}) %slice-start) | async-done | bytes 65560 | tf_op jit(solution)/shard_map/slice | solution.py:440
  13.0 0.0 slice-done.1
  13.1 2.0 %collective-permute-start.1 = (bf16[4,128,128]{2,1,0:T(8,128)(2,1)S(1)}, bf16[4,128,128]{2,1,0:T(8,128)(2,1)S(1)}, u32[]{:S(2)}, u32[]{:S(2)}) collective-permute-start(bf16[4,128,128]{2,1,0:T(8,128)(2,1)S(1)} %get-tuple-element.32), channel_id=1, source_target_pairs={{0,2},{4,6},{8,10},{12,14},{16,18},{20,22},{24,26},{28,30},{2,0},{... | collective-permute-start | bytes 393224 | tf_op jit(solution)/shard_map/ppermute | solution.py:426
  15.1 0.7 %collective-permute-start = (bf16[4,128,128]{2,1,0:T(8,128)(2,1)S(1)}, bf16[4,128,128]{2,1,0:T(8,128)(2,1)S(1)}, u32[]{:S(2)}, u32[]{:S(2)}) collective-permute-start(bf16[4,128,128]{2,1,0:T(8,128)(2,1)S(1)} %get-tuple-element.33), channel_id=1, source_target_pairs={{2,4},{6,8},{10,12},{14,16},{18,20},{22,24},{26,28},{4,2},{8,6},{1... | collective-permute-start | bytes 393224 | tf_op jit(solution)/shard_map/ppermute | solution.py:426
  15.7 0.1 coefficients.1
  15.8 8.3 %collective-permute-done.1.coef_near = bf16[4,128,128]{2,1,0:T(8,128)(2,1)S(1)} collective-permute-done((bf16[4,128,128]{2,1,0:T(8,128)(2,1)S(1)}, bf16[4,128,128]{2,1,0:T(8,128)(2,1)S(1)}, u32[]{:S(2)}, u32[]{:S(2)}) %collective-permute-start.1) | collective-permute-done | bytes 131104 | tf_op jit(solution)/shard_map/ppermute | solution.py:426
  24.1 0.0 collective-permute-done.coef_far
  24.1 4.3 %all-to-all-done = bf16[64,4,8,128]{3,2,1,0:T(8,128)(2,1)S(1)} async-done(((bf16[64,4,8,128]{3,2,1,0:T(8,128)(2,1)}), bf16[64,4,8,128]{3,2,1,0:T(8,128)(2,1)S(1)}, u32[]{:S(2)}, u32[]{:S(2)}) %all-to-all-start) | async-done | bytes 524320 | tf_op jit(solution)/shard_map/all_to_all | solution.py:455
  28.4 0.6 %pack.1 = (bf16[96,128]{1,0:T(8,128)(2,1)S(1)}, bf16[96,128]{1,0:T(8,128)(2,1)S(1)}, f32[6,128,128]{2,1,0:T(8,128)S(1)}) custom-call(bf16[16,4,4,8,128]{4,3,2,1,0:T(8,128)(2,1)S(1)} %bitcast.1, bf16[4,128,128]{2,1,0:T(8,128)(2,1)S(1)} %copy-done, bf16[4,128,128]{2,1,0:T(8,128)(2,1)S(1)} %copy-done.1), custom_call_target="tpu_custom_call" | custom-call | tf_op jit(solution)/shard_map/pack/pallas_call | solution.py:464
  29.1 1.6 %collective-permute-start.2 = (bf16[96,128]{1,0:T(8,128)(2,1)S(1)}, bf16[96,128]{1,0:T(8,128)(2,1)S(1)}, u32[]{:S(2)}, u32[]{:S(2)}) collective-permute-start(bf16[96,128]{1,0:T(8,128)(2,1)S(1)} %broadcast_select_fusion.2), channel_id=1, source_target_pairs={{0,1},{1,0},{2,3},{3,2},{4,5},{5,4},{6,7},{7,6},{8,9},{9,8},{10,11... | collective-permute-start | bytes 73736 | tf_op jit(solution)/shard_map/ppermute | solution.py:472
  30.6 0.8 %cut.1 = (bf16[512,128]{1,0:T(8,128)(2,1)S(1)}, bf16[512,128]{1,0:T(8,128)(2,1)S(1)}) custom-call(bf16[16,4,4,8,128]{4,3,2,1,0:T(8,128)(2,1)S(1)} %bitcast.2, f32[4,128,128]{2,1,0:T(8,128)S(1)} %get-tuple-element.20.stiff, f32[4,128,128]{2,1,0:T(8,128)S(1)} %get-tuple-element.21.buoy), custom_call_target="tpu_custom_call" | custom-call | tf_op jit(solution)/shard_map/cut/pallas_call | solution.py:464
  31.4 1.6 %collective-permute-done.2.left.right = bf16[96,128]{1,0:T(8,128)(2,1)S(1)} collective-permute-done((bf16[96,128]{1,0:T(8,128)(2,1)S(1)}, bf16[96,128]{1,0:T(8,128)(2,1)S(1)}, u32[]{:S(2)}, u32[]{:S(2)}) %collective-permute-start.2) | collective-permute-done | bytes 24608 | tf_op jit(solution)/shard_map/ppermute | solution.py:472
  33.0 0.9 %edge.1 = (bf16[640,128]{1,0:T(8,128)(2,1)S(1)}, bf16[640,128]{1,0:T(8,128)(2,1)S(1)}, f32[6,64,128]{2,1,0:T(8,128)S(1)}) custom-call(f32[6,128,128]{2,1,0:T(8,128)S(1)} %get-tuple-element.22.own, bf16[96,128]{1,0:T(8,128)(2,1)S(1)} %collective-permute-done.2.left.right, bf16[96,128]{1,0:T(8,128)(2,1)S(1)} %collective-permute-done.2.left.right, ...), custom_call_target="tpu_custom_call" | custom-call | tf_op jit(solution)/shard_map/edge/pallas_call | solution.py:464
  33.8 0.7 %collective-permute-start.3 = (bf16[640,128]{1,0:T(8,128)(2,1)S(1)}, bf16[640,128]{1,0:T(8,128)(2,1)S(1)}, u32[]{:S(2)}, u32[]{:S(2)}) collective-permute-start(bf16[640,128]{1,0:T(8,128)(2,1)S(1)} %get-tuple-element.28), channel_id=1, source_target_pairs={{2,4},{6,8},{10,12},{14,16},{18,20},{22,24},{26,28},{4,2},{8,6},{1... | collective-permute-start | bytes 491528 | tf_op jit(solution)/shard_map/ppermute | solution.py:426
  34.5 3.7 %collective-permute-start.4 = (bf16[640,128]{1,0:T(8,128)(2,1)S(1)}, bf16[640,128]{1,0:T(8,128)(2,1)S(1)}, u32[]{:S(2)}, u32[]{:S(2)}) collective-permute-start(bf16[640,128]{1,0:T(8,128)(2,1)S(1)} %get-tuple-element.29), channel_id=1, source_target_pairs={{0,2},{4,6},{8,10},{12,14},{16,18},{20,22},{24,26},{28,30},{2,0},{... | collective-permute-start | bytes 491528 | tf_op jit(solution)/shard_map/ppermute | solution.py:426
  38.2 0.0 collective-permute-done.3.far
  38.2 6.5 %collective-permute-done.4.near = bf16[640,128]{1,0:T(8,128)(2,1)S(1)} collective-permute-done((bf16[640,128]{1,0:T(8,128)(2,1)S(1)}, bf16[640,128]{1,0:T(8,128)(2,1)S(1)}, u32[]{:S(2)}, u32[]{:S(2)}) %collective-permute-start.4) | collective-permute-done | bytes 163872 | tf_op jit(solution)/shard_map/ppermute | solution.py:426
  44.7 3.5 %joined.1 = (f32[4,128,128]{2,1,0:T(8,128)}, f32[3,4,128,128]{3,2,1,0:T(8,128)}) custom-call(bf16[16,4,4,8,128]{4,3,2,1,0:T(8,128)(2,1)S(1)} %bitcast.3, f32[4,128,128]{2,1,0:T(8,128)S(1)} %get-tuple-element.20.stiff, f32[4,128,128]{2,1,0:T(8,128)S(1)} %get-tuple-element.21.buoy, f32[6,64,128]{2,1,0:T(8,128)S(1)} %get-tuple-element.27.strips, ...), custom_call_target="tpu_custom_call" | custom-call | tf_op jit(solution)/shard_map/joined/pallas_call | solution.py:494
  (3 shorter events, 0.1 us)
Async XLA Ops:
  3.8 24.6 %all-to-all-start = ((bf16[64,4,8,128]{3,2,1,0:T(8,128)(2,1)}), bf16[64,4,8,128]{3,2,1,0:T(8,128)(2,1)S(1)}, u32[]{:S(2)}, u32[]{:S(2)}) async-start(bf16[64,4,8,128]{3,2,1,0:T(8,128)(2,1)} %bricks.1), calls=%async_computation | async-start | bytes 1048576 | tf_op jit(solution)/shard_map/all_to_all | solution.py:455
  11.2 0.9 %copy-start = (bf16[4,128,128]{2,1,0:T(8,128)(2,1)S(1)}, bf16[4,128,128]{2,1,0:T(8,128)(2,1)}, u32[]{:S(2)}) copy-start(bf16[4,128,128]{2,1,0:T(8,128)(2,1)} %speed.3) | copy-start | bytes 393220
  11.2 1.0 %copy-start.1 = (bf16[4,128,128]{2,1,0:T(8,128)(2,1)S(1)}, bf16[4,128,128]{2,1,0:T(8,128)(2,1)}, u32[]{:S(2)}) copy-start(bf16[4,128,128]{2,1,0:T(8,128)(2,1)} %imped.3) | copy-start | bytes 393220
  12.2 0.8 %slice-start = ((bf16[4,128,128]{2,1,0:T(8,128)(2,1)}), bf16[2,128,128]{2,1,0:T(8,128)(2,1)S(1)}, s32[]{:S(2)}) async-start(bf16[4,128,128]{2,1,0:T(8,128)(2,1)} %speed.3), calls=%async_computation.1 | async-start | bytes 131072 | tf_op jit(solution)/shard_map/slice | solution.py:440
  12.2 0.9 %slice-start.1 = ((bf16[4,128,128]{2,1,0:T(8,128)(2,1)}), bf16[2,128,128]{2,1,0:T(8,128)(2,1)S(1)}, s32[]{:S(2)}) async-start(bf16[4,128,128]{2,1,0:T(8,128)(2,1)} %imped.3), calls=%async_computation.2 | async-start | bytes 131072 | tf_op jit(solution)/shard_map/slice | solution.py:440
  13.1 11.0 %collective-permute-start.1 = (bf16[4,128,128]{2,1,0:T(8,128)(2,1)S(1)}, bf16[4,128,128]{2,1,0:T(8,128)(2,1)S(1)}, u32[]{:S(2)}, u32[]{:S(2)}) collective-permute-start(bf16[4,128,128]{2,1,0:T(8,128)(2,1)S(1)} %get-tuple-element.32), channel_id=1, source_target_pairs={{0,2},{4,6},{8,10},{12,14},{16,18},{20,22},{24,26},{28,30},{2,0},{... | collective-permute-start | bytes 393224 | tf_op jit(solution)/shard_map/ppermute | solution.py:426
  15.1 9.0 %collective-permute-start = (bf16[4,128,128]{2,1,0:T(8,128)(2,1)S(1)}, bf16[4,128,128]{2,1,0:T(8,128)(2,1)S(1)}, u32[]{:S(2)}, u32[]{:S(2)}) collective-permute-start(bf16[4,128,128]{2,1,0:T(8,128)(2,1)S(1)} %get-tuple-element.33), channel_id=1, source_target_pairs={{2,4},{6,8},{10,12},{14,16},{18,20},{22,24},{26,28},{4,2},{8,6},{1... | collective-permute-start | bytes 393224 | tf_op jit(solution)/shard_map/ppermute | solution.py:426
  29.1 3.9 %collective-permute-start.2 = (bf16[96,128]{1,0:T(8,128)(2,1)S(1)}, bf16[96,128]{1,0:T(8,128)(2,1)S(1)}, u32[]{:S(2)}, u32[]{:S(2)}) collective-permute-start(bf16[96,128]{1,0:T(8,128)(2,1)S(1)} %broadcast_select_fusion.2), channel_id=1, source_target_pairs={{0,1},{1,0},{2,3},{3,2},{4,5},{5,4},{6,7},{7,6},{8,9},{9,8},{10,11... | collective-permute-start | bytes 73736 | tf_op jit(solution)/shard_map/ppermute | solution.py:472
  33.8 4.4 %collective-permute-start.3 = (bf16[640,128]{1,0:T(8,128)(2,1)S(1)}, bf16[640,128]{1,0:T(8,128)(2,1)S(1)}, u32[]{:S(2)}, u32[]{:S(2)}) collective-permute-start(bf16[640,128]{1,0:T(8,128)(2,1)S(1)} %get-tuple-element.28), channel_id=1, source_target_pairs={{2,4},{6,8},{10,12},{14,16},{18,20},{22,24},{26,28},{4,2},{8,6},{1... | collective-permute-start | bytes 491528 | tf_op jit(solution)/shard_map/ppermute | solution.py:426
  34.5 10.2 %collective-permute-start.4 = (bf16[640,128]{1,0:T(8,128)(2,1)S(1)}, bf16[640,128]{1,0:T(8,128)(2,1)S(1)}, u32[]{:S(2)}, u32[]{:S(2)}) collective-permute-start(bf16[640,128]{1,0:T(8,128)(2,1)S(1)} %get-tuple-element.29), channel_id=1, source_target_pairs={{0,2},{4,6},{8,10},{12,14},{16,18},{20,22},{24,26},{28,30},{2,0},{... | collective-permute-start | bytes 491528 | tf_op jit(solution)/shard_map/ppermute | solution.py:426

commit v5 on v4

--- a/solution.py
+++ b/solution.py
@@ -269,11 +269,6 @@
     return step, steps * y, steps * y + steps * step
 
 
-def bricks_kernel(source, bricks):
-    for k in range(source.shape[0]):
-        bricks[:, k] = source[k]
-
-
 def coefficients_kernel(speed, imped, stiff, buoy):
     for i in range(speed.shape[0]):
         stiff[i], buoy[i] = coefficients(f32(speed[i]), f32(imped[i]))
@@ -290,7 +285,7 @@
 
 
 def edge_kernel(
-    steps, layers, gy_size, own, left, right, loads, fluxes, far, near, strips, whole, series, columns
+    steps, layers, gy_size, own, left, right, loads, fluxes, near, far, strips, whole, series, columns
 ):
     y, lanes = own.shape[2], loads.shape[1]
     rows = layers * EDGE
@@ -361,7 +356,7 @@
 
 
 def joined_kernel(
-    steps, layers, src, stiff, buoy, strips, far, near, coef_far, coef_near, pressure_out, velocity_out,
+    steps, layers, src, stiff, buoy, strips, near, far, coef_near, coef_far, pressure_out, velocity_out,
     pressure, velocity, series, columns, sems,
 ):
     y, lanes = stiff.shape[1:]
@@ -442,17 +437,7 @@
     even = is_even()
     coef_far, coef_near = jnp.where(even, below, above), jnp.where(even, above, below)
     coef_far, coef_near = swapped(coef_far, xs, 1), swapped(coef_near, xs, 0)
-    chunk = whole_x // 4
-    bricks = pl.pallas_call(
-        bricks_kernel,
-        grid=(4,),
-        in_specs=[pl.BlockSpec((steps, chunk, brick_y, lanes), lambda j: (0, j, 0, 0))],
-        out_specs=pl.BlockSpec((chunk, steps, brick_y, lanes), lambda j: (j, 0, 0, 0)),
-        out_shape=sds((whole_x, steps, brick_y, lanes), bf16),
-        compiler_params=pltpu.CompilerParams(vmem_limit_bytes=60 * 1024 * 1024),
-        name="bricks",
-    )(source)
-    relaid = lax.all_to_all(bricks, xs, split_axis=0, concat_axis=0, tiled=True)
+    relaid = lax.all_to_all(source.transpose(1, 0, 2, 3), xs, split_axis=0, concat_axis=0, tiled=True)
     relaid = relaid.reshape(whole_x // layers, layers, steps, brick_y, lanes)
     field = sds((layers, y, lanes), jnp.float32)
     stiff, buoy = pl.pallas_call(
@@ -482,15 +467,16 @@
     )
     _, _, extra = strip_layout(steps, y)
     message = sds((extra + 4 * STRIP * (y // 128), 128), bf16)
-    far, near, strips = call(
+    near, far, strips = call(
         functools.partial(edge_kernel, steps, layers, gy_size),
         (message, message, sds((steps + 2, layers * STRIP, y), jnp.float32)),
         [pltpu.VMEM((steps + 2, layers * WIDE, y), jnp.float32)] + series,
         own, left, right, loads, fluxes, name="edge",
     )
-    far, near = swapped(far, xs, 1), swapped(near, xs, 0)
-
-    args = relaid, stiff, buoy, strips, far, near, coef_far, coef_near
+    near = swapped(near, xs, 0)
+    far = swapped(far, xs, 1)
+
+    args = relaid, stiff, buoy, strips, near, far, coef_near, coef_far
     return pl.pallas_call(
         functools.partial(joined_kernel, steps, layers),
         in_specs=[pl.BlockSpec(memory_space=pltpu.VMEM)] * len(args),

time: 48.5 us -> 44.4 us (0.915)
  the two profiles are of different devices: /device:TPU:0 before, /device:TPU:8 now
where the time goes in v5:
time: 44.4 us; the launch traced here: 44.1 us
  waiting for transfers between devices  17.8 us (40%)
  starting transfers between devices  15.9 us (36%)
  Pallas kernels  5.8 us (13%)
  local copies, waits for them, and re-layouts  3.75 us (8%)
  between operations  0.71 us (2%)
    ppermute x4, waiting for transfers between devices, swapped(): return lax.ppermute(block, axis, pairs + [(j, i) for i, j in pairs])  14.5 us
    ppermute x4, starting transfers between devices, swapped(): return lax.ppermute(block, axis, pairs + [(j, i) for i, j in pairs])  8.07 us
    all_to_all x1, starting transfers between devices, on_device(): lax.all_to_all(source.transpose(1, 0, 2, 3), xs, split_axis=0, concat_axi...  6.3 us
    pallas_call x1, Pallas kernels, on_device(): pl.pallas_call(functools.partial(joined_kernel, steps, layers), in_specs=...  3.47 us
    unnamed x5, local copies, waits for them, and re-layouts  2.88 us
    pallas_call x3, Pallas kernels, call(): pl.pallas_call(kernel, out_shape=outs, scratch_shapes=scratch, compiler_p...  2.24 us
    all_to_all x1, waiting for transfers between devices, on_device(): lax.all_to_all(source.transpose(1, 0, 2, 3), xs, split_axis=0, concat_axi...  1.8 us
    ppermute x1, waiting for transfers between devices, on_device(): lax.ppermute(jnp.where(lax.axis_index('gy') == 0, high, low), 'gy', [(0,...  1.57 us
  transfers between devices with their start and end apart: 6, of which 6 were waited for; matrix products, arithmetic and copies ran while one was open for 0% of the time, Pallas kernels for 2%

profile of v5, /device:TPU:8, one launch (start us, length us, event | category | flops | bytes accessed | tf_op | source)
XLA Modules:
  0.0 44.1 jit_solution(6446838213360015241)
XLA Ops:
  0.6 1.9 %copy.8 = bf16[4,64,8,128]{3,2,0,1:T(8,128)(2,1)} copy(bf16[4,64,8,128]{3,2,1,0:T(8,128)(2,1)} %param.3) | data formatting | bytes 1048576 | tf_op args[0]
  2.6 6.3 %all-to-all-start = ((bf16[64,4,8,128]{3,2,1,0:T(8,128)(2,1)}), bf16[64,4,8,128]{3,2,1,0:T(8,128)(2,1)S(1)}, u32[]{:S(2)}, u32[]{:S(2)}) async-start(bf16[64,4,8,128]{3,2,1,0:T(8,128)(2,1)} %bitcast.3), calls=%async_computation | async-start | bytes 1048576 | tf_op jit(solution)/shard_map/all_to_all | solution.py:440
  8.8 0.0 copy-start
  8.9 0.0 copy-start.1
  8.9 0.9 %copy-done = bf16[4,128,128]{2,1,0:T(8,128)(2,1)S(1)} copy-done((bf16[4,128,128]{2,1,0:T(8,128)(2,1)S(1)}, bf16[4,128,128]{2,1,0:T(8,128)(2,1)}, u32[]{:S(2)}) %copy-start) | copy-done | bytes 131096
  9.8 0.1 copy-done.1
  9.8 0.0 slice-start
  9.8 0.0 slice-start.1
  9.8 0.8 %slice-done = bf16[2,128,128]{2,1,0:T(8,128)(2,1)S(1)} async-done(((bf16[4,128,128]{2,1,0:T(8,128)(2,1)}), bf16[2,128,128]{2,1,0:T(8,128)(2,1)S(1)}, s32[]{:S(2)}) %slice-start) | async-done | bytes 65560 | tf_op jit(solution)/shard_map/slice | solution.py:435
  10.7 0.0 slice-done.1
  10.7 1.5 %collective-permute-start.1 = (bf16[4,128,128]{2,1,0:T(8,128)(2,1)S(1)}, bf16[4,128,128]{2,1,0:T(8,128)(2,1)S(1)}, u32[]{:S(2)}, u32[]{:S(2)}) collective-permute-start(bf16[4,128,128]{2,1,0:T(8,128)(2,1)S(1)} %get-tuple-element.32), channel_id=1, source_target_pairs={{0,2},{4,6},{8,10},{12,14},{16,18},{20,22},{24,26},{28,30},{2,0},{... | collective-permute-start | bytes 393224 | tf_op jit(solution)/shard_map/ppermute | solution.py:421
  12.3 2.0 %collective-permute-start = (bf16[4,128,128]{2,1,0:T(8,128)(2,1)S(1)}, bf16[4,128,128]{2,1,0:T(8,128)(2,1)S(1)}, u32[]{:S(2)}, u32[]{:S(2)}) collective-permute-start(bf16[4,128,128]{2,1,0:T(8,128)(2,1)S(1)} %get-tuple-element.33), channel_id=1, source_target_pairs={{2,4},{6,8},{10,12},{14,16},{18,20},{22,24},{26,28},{4,2},{8,6},{1... | collective-permute-start | bytes 393224 | tf_op jit(solution)/shard_map/ppermute | solution.py:421
  14.3 0.1 coefficients.1
  14.4 3.5 %collective-permute-done.1.coef_near = bf16[4,128,128]{2,1,0:T(8,128)(2,1)S(1)} collective-permute-done((bf16[4,128,128]{2,1,0:T(8,128)(2,1)S(1)}, bf16[4,128,128]{2,1,0:T(8,128)(2,1)S(1)}, u32[]{:S(2)}, u32[]{:S(2)}) %collective-permute-start.1) | collective-permute-done | bytes 131104 | tf_op jit(solution)/shard_map/ppermute | solution.py:421
  17.9 5.4 %collective-permute-done.coef_far = bf16[4,128,128]{2,1,0:T(8,128)(2,1)S(1)} collective-permute-done((bf16[4,128,128]{2,1,0:T(8,128)(2,1)S(1)}, bf16[4,128,128]{2,1,0:T(8,128)(2,1)S(1)}, u32[]{:S(2)}, u32[]{:S(2)}) %collective-permute-start) | collective-permute-done | bytes 131104 | tf_op jit(solution)/shard_map/ppermute | solution.py:421
  23.3 1.8 %all-to-all-done = bf16[64,4,8,128]{3,2,1,0:T(8,128)(2,1)S(1)} async-done(((bf16[64,4,8,128]{3,2,1,0:T(8,128)(2,1)}), bf16[64,4,8,128]{3,2,1,0:T(8,128)(2,1)S(1)}, u32[]{:S(2)}, u32[]{:S(2)}) %all-to-all-start) | async-done | bytes 524320 | tf_op jit(solution)/shard_map/all_to_all | solution.py:440
  25.1 0.6 %pack.1 = (bf16[96,128]{1,0:T(8,128)(2,1)S(1)}, bf16[96,128]{1,0:T(8,128)(2,1)S(1)}, f32[6,128,128]{2,1,0:T(8,128)S(1)}) custom-call(bf16[16,4,4,8,128]{4,3,2,1,0:T(8,128)(2,1)S(1)} %bitcast.4, bf16[4,128,128]{2,1,0:T(8,128)(2,1)S(1)} %copy-done, bf16[4,128,128]{2,1,0:T(8,128)(2,1)S(1)} %copy-done.1), custom_call_target="tpu_custom_call" | custom-call | tf_op jit(solution)/shard_map/pack/pallas_call | solution.py:449
  25.7 1.6 %collective-permute-start.2 = (bf16[96,128]{1,0:T(8,128)(2,1)S(1)}, bf16[96,128]{1,0:T(8,128)(2,1)S(1)}, u32[]{:S(2)}, u32[]{:S(2)}) collective-permute-start(bf16[96,128]{1,0:T(8,128)(2,1)S(1)} %broadcast_select_fusion.2), channel_id=1, source_target_pairs={{0,1},{1,0},{2,3},{3,2},{4,5},{5,4},{6,7},{7,6},{8,9},{9,8},{10,11... | collective-permute-start | bytes 73736 | tf_op jit(solution)/shard_map/ppermute | solution.py:457
  27.3 0.8 %cut.1 = (bf16[512,128]{1,0:T(8,128)(2,1)S(1)}, bf16[512,128]{1,0:T(8,128)(2,1)S(1)}) custom-call(bf16[16,4,4,8,128]{4,3,2,1,0:T(8,128)(2,1)S(1)} %bitcast.5, f32[4,128,128]{2,1,0:T(8,128)S(1)} %get-tuple-element.20.stiff, f32[4,128,128]{2,1,0:T(8,128)S(1)} %get-tuple-element.21.buoy), custom_call_target="tpu_custom_call" | custom-call | tf_op jit(solution)/shard_map/cut/pallas_call | solution.py:449
  28.0 1.6 %collective-permute-done.2.left.right = bf16[96,128]{1,0:T(8,128)(2,1)S(1)} collective-permute-done((bf16[96,128]{1,0:T(8,128)(2,1)S(1)}, bf16[96,128]{1,0:T(8,128)(2,1)S(1)}, u32[]{:S(2)}, u32[]{:S(2)}) %collective-permute-start.2) | collective-permute-done | bytes 24608 | tf_op jit(solution)/shard_map/ppermute | solution.py:457
  29.6 0.9 %edge.1 = (bf16[640,128]{1,0:T(8,128)(2,1)S(1)}, bf16[640,128]{1,0:T(8,128)(2,1)S(1)}, f32[6,64,128]{2,1,0:T(8,128)S(1)}) custom-call(f32[6,128,128]{2,1,0:T(8,128)S(1)} %get-tuple-element.22.own, bf16[96,128]{1,0:T(8,128)(2,1)S(1)} %collective-permute-done.2.left.right, bf16[96,128]{1,0:T(8,128)(2,1)S(1)} %collective-permute-done.2.left.right, ...), custom_call_target="tpu_custom_call" | custom-call | tf_op jit(solution)/shard_map/edge/pallas_call | solution.py:449
  30.5 2.0 %collective-permute-start.3 = (bf16[640,128]{1,0:T(8,128)(2,1)S(1)}, bf16[640,128]{1,0:T(8,128)(2,1)S(1)}, u32[]{:S(2)}, u32[]{:S(2)}) collective-permute-start(bf16[640,128]{1,0:T(8,128)(2,1)S(1)} %get-tuple-element.28), channel_id=1, source_target_pairs={{0,2},{4,6},{8,10},{12,14},{16,18},{20,22},{24,26},{28,30},{2,0},{... | collective-permute-start | bytes 491528 | tf_op jit(solution)/shard_map/ppermute | solution.py:421
  32.5 2.5 %collective-permute-start.4 = (bf16[640,128]{1,0:T(8,128)(2,1)S(1)}, bf16[640,128]{1,0:T(8,128)(2,1)S(1)}, u32[]{:S(2)}, u32[]{:S(2)}) collective-permute-start(bf16[640,128]{1,0:T(8,128)(2,1)S(1)} %get-tuple-element.29), channel_id=1, source_target_pairs={{2,4},{6,8},{10,12},{14,16},{18,20},{22,24},{26,28},{4,2},{8,6},{1... | collective-permute-start | bytes 491528 | tf_op jit(solution)/shard_map/ppermute | solution.py:421
  35.0 3.9 %collective-permute-done.3.near = bf16[640,128]{1,0:T(8,128)(2,1)S(1)} collective-permute-done((bf16[640,128]{1,0:T(8,128)(2,1)S(1)}, bf16[640,128]{1,0:T(8,128)(2,1)S(1)}, u32[]{:S(2)}, u32[]{:S(2)}) %collective-permute-start.3) | collective-permute-done | bytes 163872 | tf_op jit(solution)/shard_map/ppermute | solution.py:421
  38.9 1.7 %collective-permute-done.4.far = bf16[640,128]{1,0:T(8,128)(2,1)S(1)} collective-permute-done((bf16[640,128]{1,0:T(8,128)(2,1)S(1)}, bf16[640,128]{1,0:T(8,128)(2,1)S(1)}, u32[]{:S(2)}, u32[]{:S(2)}) %collective-permute-start.4) | collective-permute-done | bytes 163872 | tf_op jit(solution)/shard_map/ppermute | solution.py:421
  40.6 3.5 %joined.1 = (f32[4,128,128]{2,1,0:T(8,128)}, f32[3,4,128,128]{3,2,1,0:T(8,128)}) custom-call(bf16[16,4,4,8,128]{4,3,2,1,0:T(8,128)(2,1)S(1)} %bitcast.6, f32[4,128,128]{2,1,0:T(8,128)S(1)} %get-tuple-element.20.stiff, f32[4,128,128]{2,1,0:T(8,128)S(1)} %get-tuple-element.21.buoy, f32[6,64,128]{2,1,0:T(8,128)S(1)} %get-tuple-element.27.strips, ...), custom_call_target="tpu_custom_call" | custom-call | tf_op jit(solution)/shard_map/joined/pallas_call | solution.py:480
  (3 shorter events, 0.1 us)
Async XLA Ops:
  2.6 22.5 %all-to-all-start = ((bf16[64,4,8,128]{3,2,1,0:T(8,128)(2,1)}), bf16[64,4,8,128]{3,2,1,0:T(8,128)(2,1)S(1)}, u32[]{:S(2)}, u32[]{:S(2)}) async-start(bf16[64,4,8,128]{3,2,1,0:T(8,128)(2,1)} %bitcast.3), calls=%async_computation | async-start | bytes 1048576 | tf_op jit(solution)/shard_map/all_to_all | solution.py:440
  8.8 0.9 %copy-start = (bf16[4,128,128]{2,1,0:T(8,128)(2,1)S(1)}, bf16[4,128,128]{2,1,0:T(8,128)(2,1)}, u32[]{:S(2)}) copy-start(bf16[4,128,128]{2,1,0:T(8,128)(2,1)} %speed.3) | copy-start | bytes 393220
  8.9 1.0 %copy-start.1 = (bf16[4,128,128]{2,1,0:T(8,128)(2,1)S(1)}, bf16[4,128,128]{2,1,0:T(8,128)(2,1)}, u32[]{:S(2)}) copy-start(bf16[4,128,128]{2,1,0:T(8,128)(2,1)} %imped.3) | copy-start | bytes 393220
  9.8 0.8 %slice-start = ((bf16[4,128,128]{2,1,0:T(8,128)(2,1)}), bf16[2,128,128]{2,1,0:T(8,128)(2,1)S(1)}, s32[]{:S(2)}) async-start(bf16[4,128,128]{2,1,0:T(8,128)(2,1)} %speed.3), calls=%async_computation.1 | async-start | bytes 131072 | tf_op jit(solution)/shard_map/slice | solution.py:435
  9.8 0.9 %slice-start.1 = ((bf16[4,128,128]{2,1,0:T(8,128)(2,1)}), bf16[2,128,128]{2,1,0:T(8,128)(2,1)S(1)}, s32[]{:S(2)}) async-start(bf16[4,128,128]{2,1,0:T(8,128)(2,1)} %imped.3), calls=%async_computation.2 | async-start | bytes 131072 | tf_op jit(solution)/shard_map/slice | solution.py:435
  10.7 7.2 %collective-permute-start.1 = (bf16[4,128,128]{2,1,0:T(8,128)(2,1)S(1)}, bf16[4,128,128]{2,1,0:T(8,128)(2,1)S(1)}, u32[]{:S(2)}, u32[]{:S(2)}) collective-permute-start(bf16[4,128,128]{2,1,0:T(8,128)(2,1)S(1)} %get-tuple-element.32), channel_id=1, source_target_pairs={{0,2},{4,6},{8,10},{12,14},{16,18},{20,22},{24,26},{28,30},{2,0},{... | collective-permute-start | bytes 393224 | tf_op jit(solution)/shard_map/ppermute | solution.py:421
  12.3 11.0 %collective-permute-start = (bf16[4,128,128]{2,1,0:T(8,128)(2,1)S(1)}, bf16[4,128,128]{2,1,0:T(8,128)(2,1)S(1)}, u32[]{:S(2)}, u32[]{:S(2)}) collective-permute-start(bf16[4,128,128]{2,1,0:T(8,128)(2,1)S(1)} %get-tuple-element.33), channel_id=1, source_target_pairs={{2,4},{6,8},{10,12},{14,16},{18,20},{22,24},{26,28},{4,2},{8,6},{1... | collective-permute-start | bytes 393224 | tf_op jit(solution)/shard_map/ppermute | solution.py:421
  25.7 3.9 %collective-permute-start.2 = (bf16[96,128]{1,0:T(8,128)(2,1)S(1)}, bf16[96,128]{1,0:T(8,128)(2,1)S(1)}, u32[]{:S(2)}, u32[]{:S(2)}) collective-permute-start(bf16[96,128]{1,0:T(8,128)(2,1)S(1)} %broadcast_select_fusion.2), channel_id=1, source_target_pairs={{0,1},{1,0},{2,3},{3,2},{4,5},{5,4},{6,7},{7,6},{8,9},{9,8},{10,11... | collective-permute-start | bytes 73736 | tf_op jit(solution)/shard_map/ppermute | solution.py:457
  30.5 8.4 %collective-permute-start.3 = (bf16[640,128]{1,0:T(8,128)(2,1)S(1)}, bf16[640,128]{1,0:T(8,128)(2,1)S(1)}, u32[]{:S(2)}, u32[]{:S(2)}) collective-permute-start(bf16[640,128]{1,0:T(8,128)(2,1)S(1)} %get-tuple-element.28), channel_id=1, source_target_pairs={{0,2},{4,6},{8,10},{12,14},{16,18},{20,22},{24,26},{28,30},{2,0},{... | collective-permute-start | bytes 491528 | tf_op jit(solution)/shard_map/ppermute | solution.py:421
  32.5 8.1 %collective-permute-start.4 = (bf16[640,128]{1,0:T(8,128)(2,1)S(1)}, bf16[640,128]{1,0:T(8,128)(2,1)S(1)}, u32[]{:S(2)}, u32[]{:S(2)}) collective-permute-start(bf16[640,128]{1,0:T(8,128)(2,1)S(1)} %get-tuple-element.29), channel_id=1, source_target_pairs={{2,4},{6,8},{10,12},{14,16},{18,20},{22,24},{26,28},{4,2},{8,6},{1... | collective-permute-start | bytes 491528 | tf_op jit(solution)/shard_map/ppermute | solution.py:421

commit v6 on v5

--- a/solution.py
+++ b/solution.py
@@ -198,7 +198,7 @@
         self.ref[i] = value
 
 
-def pack_kernel(steps, layers, src, speed, imped, low, high, own):
+def pack_kernel(steps, layers, src, speed, imped, coef_near, coef_far, low, high, own):
     lanes = src.shape[-1]
     rows = layers * EDGE
     row, lane = iota((rows, lanes), 0), iota((rows, lanes), 1)
@@ -207,7 +207,7 @@
     at_low = (wrow >= EDGE) & (wrow < half) & (wlane == wrow - EDGE)
     at_high = (wrow >= half) & (wrow < half + OWN) & (wlane == wrow + (lanes - OWN - half))
     wide = jnp.where(at_low | at_high, 1.0, 0.0)
-    for f in range(steps + 2):
+    for f in range(steps + 4):
         total = None
         for i in range(layers):
             mine = (row >> 2) == i
@@ -216,7 +216,7 @@
             if f < steps:
                 block = brick_block(src, f, i).astype(jnp.bfloat16)
             else:
-                block = (speed, imped)[f - steps][i]
+                block = (speed, imped, coef_near, coef_far)[f - steps][i]
             part = lax.dot_general(pick, block, (((1,), (1,)), ((), ())), preferred_element_type=jnp.float32)
             own[f, i * WIDE : (i + 1) * WIDE, :] = part[:WIDE]
             total = part[WIDE:] if total is None else total + part[WIDE:]
@@ -269,8 +269,15 @@
     return step, steps * y, steps * y + steps * step
 
 
-def coefficients_kernel(speed, imped, stiff, buoy):
-    for i in range(speed.shape[0]):
+def coefficients_kernel(speed, imped, stiff, buoy, near, far):
+    faces = Faces(far, near)
+    last = speed.shape[0] - 1
+    for j, ref in enumerate((speed, imped)):
+        for depth in range(2):
+            def write(out, value, at=2 * j + depth):
+                out[at] = value.astype(jnp.bfloat16)
+            faces.put(write, f32(ref[depth]), f32(ref[last - depth]))
+    for i in range(last + 1):
         stiff[i], buoy[i] = coefficients(f32(speed[i]), f32(imped[i]))
 
 
@@ -302,7 +309,7 @@
         half = STRIP // 2
         return jnp.concatenate([a[:half], a[WIDE - half :]], 0)
 
-    for f in range(steps + 2):
+    for f in range(steps + 4):
         parts = jnp.concatenate([a[f * rows : (f + 1) * rows, :] for a in (left, right)], 0)
         whole[f] = own[f] + jnp.dot(order, parts, preferred_element_type=jnp.float32)
         for i in range(layers):
@@ -312,13 +319,7 @@
         return whole[f, i * WIDE : (i + 1) * WIDE, :]
 
     faces = Faces(far, near)
-    step, base, extra = strip_layout(steps, y)
-    last = layers - 1
-    for j, (f, depth) in enumerate(((steps, 0), (steps, 1), (steps + 1, 0), (steps + 1, 1))):
-        faces.put(
-            lambda ref, value, at=extra + j * step: put_strip(ref, at, value),
-            narrow(strip(f, depth)), narrow(strip(f, last - depth)),
-        )
+    step, base, _ = strip_layout(steps, y)
     coef = [coefficients(strip(steps, i), strip(steps + 1, i)) for i in range(layers)]
     strip_loads, strip_fluxes = {}, {}
     run_cut(
@@ -365,7 +366,9 @@
         return strips[f, i * STRIP : (i + 1) * STRIP, :]
 
     faces = Faces(far, near)
-    step, base, extra = strip_layout(steps, y)
+    step, base, _ = strip_layout(steps, y)
+    held = Faces(coef_far, coef_near)
+    edge_held = Faces(steps + 3, steps + 2)
 
     def strip_at(at):
         return lambda ref: strip_rows(ref, at, y)
@@ -381,8 +384,8 @@
         Strip((STRIP, y), series), steps, layers, lambda k, i: strip(steps - 1 - k, i),
         lambda i: coef[i][0], lambda i: coef[i][1], {}, {},
         lambda k: faces.above(strip_at(base + k * step)), lambda k: faces.below(strip_at(base + k * step)),
-        beside(faces.above, lambda j: strip_at(extra + j * step)),
-        beside(faces.below, lambda j: strip_at(extra + j * step)),
+        beside(edge_held.above, lambda j: lambda f: strip(f, j)),
+        beside(edge_held.below, lambda j: lambda f: strip(f, j)),
     )
     columns[...] = series[...].T
 
@@ -396,7 +399,6 @@
         for copy in copies(i):
             copy.start()
 
-    held = Faces(coef_far, coef_near)
     read = rows_reader(y)
     run_joined(
         Block((y, lanes), columns), steps, layers, lambda k, i: brick_block(src, steps - 1 - k, i),
@@ -432,26 +434,23 @@
     sds = jax.ShapeDtypeStruct
 
     assert lax.axis_size("gx") % 2 == 0
-    below = jnp.concatenate([speed[:2], impedance[:2]], 0)
-    above = jnp.concatenate([speed[-1:], speed[-2:-1], impedance[-1:], impedance[-2:-1]], 0)
-    even = is_even()
-    coef_far, coef_near = jnp.where(even, below, above), jnp.where(even, above, below)
-    coef_far, coef_near = swapped(coef_far, xs, 1), swapped(coef_near, xs, 0)
+    field, coef = sds((layers, y, lanes), jnp.float32), sds((4, y, lanes), bf16)
+    stiff, buoy, coef_near, coef_far = pl.pallas_call(
+        coefficients_kernel, out_shape=(field, field, coef, coef), compiler_params=params, name="coefficients"
+    )(speed, impedance)
+    coef_near, coef_far = swapped(coef_near, xs, 0), swapped(coef_far, xs, 1)
     relaid = lax.all_to_all(source.transpose(1, 0, 2, 3), xs, split_axis=0, concat_axis=0, tiled=True)
     relaid = relaid.reshape(whole_x // layers, layers, steps, brick_y, lanes)
-    field = sds((layers, y, lanes), jnp.float32)
-    stiff, buoy = pl.pallas_call(
-        coefficients_kernel, out_shape=(field, field), compiler_params=params, name="coefficients"
-    )(speed, impedance)
-    relaid, coef_far, coef_near, stiff, buoy = lax.optimization_barrier((relaid, coef_far, coef_near, stiff, buoy))
+    relaid, coef_near, coef_far, stiff, buoy = lax.optimization_barrier((relaid, coef_near, coef_far, stiff, buoy))
 
     def call(kernel, outs, scratch, *args, name):
         return pl.pallas_call(kernel, out_shape=outs, scratch_shapes=scratch, compiler_params=params, name=name)(*args)
 
-    edge = sds(((steps + 2) * layers * EDGE, y), bf16)
+    edge = sds(((steps + 4) * layers * EDGE, y), bf16)
     low, high, own = call(
         functools.partial(pack_kernel, steps, layers),
-        (edge, edge, sds((steps + 2, layers * WIDE, y), jnp.float32)), [], relaid, speed, impedance, name="pack",
+        (edge, edge, sds((steps + 4, layers * WIDE, y), jnp.float32)), [],
+        relaid, speed, impedance, coef_near, coef_far, name="pack",
     )
     if gy_size == 2:
         left = right = lax.ppermute(jnp.where(lax.axis_index("gy") == 0, high, low), "gy", [(0, 1), (1, 0)])
@@ -465,12 +464,11 @@
     loads, fluxes = call(
         functools.partial(cut_kernel, steps, layers), (face, face), [whole, whole_velocity], relaid, stiff, buoy, name="cut"
     )
-    _, _, extra = strip_layout(steps, y)
-    message = sds((extra + 4 * STRIP * (y // 128), 128), bf16)
+    message = sds((strip_layout(steps, y)[2], 128), bf16)
     near, far, strips = call(
         functools.partial(edge_kernel, steps, layers, gy_size),
-        (message, message, sds((steps + 2, layers * STRIP, y), jnp.float32)),
-        [pltpu.VMEM((steps + 2, layers * WIDE, y), jnp.float32)] + series,
+        (message, message, sds((steps + 4, layers * STRIP, y), jnp.float32)),
+        [pltpu.VMEM((steps + 4, layers * WIDE, y), jnp.float32)] + series,
         own, left, right, loads, fluxes, name="edge",
     )
     near = swapped(near, xs, 0)

time: 44.4 us -> 44.6 us (level)
  local copies, waits for them, and re-layouts: 3.75 us -> 1.93 us
  waiting for transfers between devices: 17.8 us -> 19.6 us
    ppermute x4, waiting for transfers between devices: 14.5 us -> 16.1 us  [swapped(): return lax.ppermute(block, axis, pairs + [(j, i) for i, j in pairs])]
    unnamed x5, local copies, waits for them, and re-layouts: 2.88 us -> 1.93 us
    slice x5 -> x0, local copies, waits for them, and re-layouts: 0.87 us -> none  [the longest x4 0.86 us: on_device(): below = jnp.concatenate([speed[:2], impedance[:2]], 0)]
where the time goes in v6:
time: 44.6 us; the launch traced here: 44.3 us
  waiting for transfers between devices  19.6 us (44%)
  starting transfers between devices  16 us (36%)
  Pallas kernels  6.04 us (14%)
  local copies, waits for them, and re-layouts  1.93 us (4%)
  between operations  0.69 us (2%)
    ppermute x4, waiting for transfers between devices, swapped(): return lax.ppermute(block, axis, pairs + [(j, i) for i, j in pairs])  16.1 us
    ppermute x4, starting transfers between devices, swapped(): return lax.ppermute(block, axis, pairs + [(j, i) for i, j in pairs])  8.07 us
    all_to_all x1, starting transfers between devices, on_device(): lax.all_to_all(source.transpose(1, 0, 2, 3), xs, split_axis=0, concat_axi...  6.43 us
    pallas_call x1, Pallas kernels, on_device(): pl.pallas_call(functools.partial(joined_kernel, steps, layers), in_specs=...  3.46 us
    pallas_call x3, Pallas kernels, call(): pl.pallas_call(kernel, out_shape=outs, scratch_shapes=scratch, compiler_p...  2.42 us
    unnamed x5, local copies, waits for them, and re-layouts  1.93 us
    all_to_all x1, waiting for transfers between devices, on_device(): lax.all_to_all(source.transpose(1, 0, 2, 3), xs, split_axis=0, concat_axi...  1.8 us
    ppermute x1, waiting for transfers between devices, on_device(): lax.ppermute(jnp.where(lax.axis_index('gy') == 0, high, low), 'gy', [(0,...  1.66 us
  transfers between devices with their start and end apart: 6, of which 6 were waited for; matrix products, arithmetic and copies ran while one was open for 0% of the time, Pallas kernels for 2%

profile of v6, /device:TPU:8, one launch (start us, length us, event | category | flops | bytes accessed | tf_op | source)
XLA Modules:
  0.0 44.3 jit_solution(6479251748631293739)
XLA Ops:
  0.6 1.9 %copy.8 = bf16[4,64,8,128]{3,2,0,1:T(8,128)(2,1)} copy(bf16[4,64,8,128]{3,2,1,0:T(8,128)(2,1)} %param.3) | data formatting | bytes 1048576 | tf_op args[0]
  2.6 0.0 copy-start
  2.6 0.0 copy-start.1
  2.6 6.4 %all-to-all-start = ((bf16[64,4,8,128]{3,2,1,0:T(8,128)(2,1)}), bf16[64,4,8,128]{3,2,1,0:T(8,128)(2,1)S(1)}, u32[]{:S(2)}, u32[]{:S(2)}) async-start(bf16[64,4,8,128]{3,2,1,0:T(8,128)(2,1)} %bitcast.3), calls=%async_computation | async-start | bytes 1048576 | tf_op jit(solution)/shard_map/all_to_all | solution.py:442
  9.0 0.0 copy-done
  9.0 0.0 copy-done.1
  9.0 0.2 coefficients.1
  9.2 1.5 %collective-permute-start = (bf16[4,128,128]{2,1,0:T(8,128)(2,1)S(1)}, bf16[4,128,128]{2,1,0:T(8,128)(2,1)S(1)}, u32[]{:S(2)}, u32[]{:S(2)}) collective-permute-start(bf16[4,128,128]{2,1,0:T(8,128)(2,1)S(1)} %get-tuple-element.19), channel_id=1, source_target_pairs={{0,2},{4,6},{8,10},{12,14},{16,18},{20,22},{24,26},{28,30},{2,0},{... | collective-permute-start | bytes 393224 | tf_op jit(solution)/shard_map/ppermute | solution.py:423
  10.7 2.0 %collective-permute-start.1 = (bf16[4,128,128]{2,1,0:T(8,128)(2,1)S(1)}, bf16[4,128,128]{2,1,0:T(8,128)(2,1)S(1)}, u32[]{:S(2)}, u32[]{:S(2)}) collective-permute-start(bf16[4,128,128]{2,1,0:T(8,128)(2,1)S(1)} %get-tuple-element.20), channel_id=1, source_target_pairs={{2,4},{6,8},{10,12},{14,16},{18,20},{22,24},{26,28},{4,2},{8,6},{1... | collective-permute-start | bytes 393224 | tf_op jit(solution)/shard_map/ppermute | solution.py:423
  12.7 3.9 %collective-permute-done.coef_near = bf16[4,128,128]{2,1,0:T(8,128)(2,1)S(1)} collective-permute-done((bf16[4,128,128]{2,1,0:T(8,128)(2,1)S(1)}, bf16[4,128,128]{2,1,0:T(8,128)(2,1)S(1)}, u32[]{:S(2)}, u32[]{:S(2)}) %collective-permute-start) | collective-permute-done | bytes 131104 | tf_op jit(solution)/shard_map/ppermute | solution.py:423
  16.6 6.8 %collective-permute-done.1.coef_far = bf16[4,128,128]{2,1,0:T(8,128)(2,1)S(1)} collective-permute-done((bf16[4,128,128]{2,1,0:T(8,128)(2,1)S(1)}, bf16[4,128,128]{2,1,0:T(8,128)(2,1)S(1)}, u32[]{:S(2)}, u32[]{:S(2)}) %collective-permute-start.1) | collective-permute-done | bytes 131104 | tf_op jit(solution)/shard_map/ppermute | solution.py:423
  23.4 1.8 %all-to-all-done = bf16[64,4,8,128]{3,2,1,0:T(8,128)(2,1)S(1)} async-done(((bf16[64,4,8,128]{3,2,1,0:T(8,128)(2,1)}), bf16[64,4,8,128]{3,2,1,0:T(8,128)(2,1)S(1)}, u32[]{:S(2)}, u32[]{:S(2)}) %all-to-all-start) | async-done | bytes 524320 | tf_op jit(solution)/shard_map/all_to_all | solution.py:442
  25.2 0.8 %pack.1 = (bf16[128,128]{1,0:T(8,128)(2,1)S(1)}, bf16[128,128]{1,0:T(8,128)(2,1)S(1)}, f32[8,128,128]{2,1,0:T(8,128)S(1)}) custom-call(bf16[16,4,4,8,128]{4,3,2,1,0:T(8,128)(2,1)S(1)} %bitcast.4, bf16[4,128,128]{2,1,0:T(8,128)(2,1)S(1)} %copy-done, bf16[4,128,128]{2,1,0:T(8,128)(2,1)S(1)} %copy-done.1, ...), custom_call_target="tpu_custom_call" | custom-call | tf_op jit(solution)/shard_map/pack/pallas_call | solution.py:447
  26.0 1.6 %collective-permute-start.2 = (bf16[128,128]{1,0:T(8,128)(2,1)S(1)}, bf16[128,128]{1,0:T(8,128)(2,1)S(1)}, u32[]{:S(2)}, u32[]{:S(2)}) collective-permute-start(bf16[128,128]{1,0:T(8,128)(2,1)S(1)} %broadcast_select_fusion), channel_id=1, source_target_pairs={{0,1},{1,0},{2,3},{3,2},{4,5},{5,4},{6,7},{7,6},{8,9},{9,8},{10,11... | collective-permute-start | bytes 98312 | tf_op jit(solution)/shard_map/ppermute | solution.py:456
  27.6 0.8 %cut.1 = (bf16[512,128]{1,0:T(8,128)(2,1)S(1)}, bf16[512,128]{1,0:T(8,128)(2,1)S(1)}) custom-call(bf16[16,4,4,8,128]{4,3,2,1,0:T(8,128)(2,1)S(1)} %bitcast.5, f32[4,128,128]{2,1,0:T(8,128)S(1)} %get-tuple-element.24.stiff, f32[4,128,128]{2,1,0:T(8,128)S(1)} %get-tuple-element.25.buoy), custom_call_target="tpu_custom_call" | custom-call | tf_op jit(solution)/shard_map/cut/pallas_call | solution.py:447
  28.3 1.7 %collective-permute-done.2.left.right = bf16[128,128]{1,0:T(8,128)(2,1)S(1)} collective-permute-done((bf16[128,128]{1,0:T(8,128)(2,1)S(1)}, bf16[128,128]{1,0:T(8,128)(2,1)S(1)}, u32[]{:S(2)}, u32[]{:S(2)}) %collective-permute-start.2) | collective-permute-done | bytes 32800 | tf_op jit(solution)/shard_map/ppermute | solution.py:456
  30.0 0.9 %edge.1 = (bf16[576,128]{1,0:T(8,128)(2,1)S(1)}, bf16[576,128]{1,0:T(8,128)(2,1)S(1)}, f32[8,64,128]{2,1,0:T(8,128)S(1)}) custom-call(f32[8,128,128]{2,1,0:T(8,128)S(1)} %get-tuple-element.28.own, bf16[128,128]{1,0:T(8,128)(2,1)S(1)} %collective-permute-done.2.left.right, bf16[128,128]{1,0:T(8,128)(2,1)S(1)} %collective-permute-done.2.left.right, ...), custom_call_target="tpu_custom_call" | custom-call | tf_op jit(solution)/shard_map/edge/pallas_call | solution.py:447
  30.9 2.0 %collective-permute-start.3 = (bf16[576,128]{1,0:T(8,128)(2,1)S(1)}, bf16[576,128]{1,0:T(8,128)(2,1)S(1)}, u32[]{:S(2)}, u32[]{:S(2)}) collective-permute-start(bf16[576,128]{1,0:T(8,128)(2,1)S(1)} %get-tuple-element.34), channel_id=1, source_target_pairs={{0,2},{4,6},{8,10},{12,14},{16,18},{20,22},{24,26},{28,30},{2,0},{... | collective-permute-start | bytes 442376 | tf_op jit(solution)/shard_map/ppermute | solution.py:423
  32.9 2.5 %collective-permute-start.4 = (bf16[576,128]{1,0:T(8,128)(2,1)S(1)}, bf16[576,128]{1,0:T(8,128)(2,1)S(1)}, u32[]{:S(2)}, u32[]{:S(2)}) collective-permute-start(bf16[576,128]{1,0:T(8,128)(2,1)S(1)} %get-tuple-element.35), channel_id=1, source_target_pairs={{2,4},{6,8},{10,12},{14,16},{18,20},{22,24},{26,28},{4,2},{8,6},{1... | collective-permute-start | bytes 442376 | tf_op jit(solution)/shard_map/ppermute | solution.py:423
  35.4 3.4 %collective-permute-done.3.near = bf16[576,128]{1,0:T(8,128)(2,1)S(1)} collective-permute-done((bf16[576,128]{1,0:T(8,128)(2,1)S(1)}, bf16[576,128]{1,0:T(8,128)(2,1)S(1)}, u32[]{:S(2)}, u32[]{:S(2)}) %collective-permute-start.3) | collective-permute-done | bytes 147488 | tf_op jit(solution)/shard_map/ppermute | solution.py:423
  38.8 2.1 %collective-permute-done.4.far = bf16[576,128]{1,0:T(8,128)(2,1)S(1)} collective-permute-done((bf16[576,128]{1,0:T(8,128)(2,1)S(1)}, bf16[576,128]{1,0:T(8,128)(2,1)S(1)}, u32[]{:S(2)}, u32[]{:S(2)}) %collective-permute-start.4) | collective-permute-done | bytes 147488 | tf_op jit(solution)/shard_map/ppermute | solution.py:423
  40.8 3.5 %joined.1 = (f32[4,128,128]{2,1,0:T(8,128)}, f32[3,4,128,128]{3,2,1,0:T(8,128)}) custom-call(bf16[16,4,4,8,128]{4,3,2,1,0:T(8,128)(2,1)S(1)} %bitcast.6, f32[4,128,128]{2,1,0:T(8,128)S(1)} %get-tuple-element.24.stiff, f32[4,128,128]{2,1,0:T(8,128)S(1)} %get-tuple-element.25.buoy, f32[8,64,128]{2,1,0:T(8,128)S(1)} %get-tuple-element.33.strips, ...), custom_call_target="tpu_custom_call" | custom-call | tf_op jit(solution)/shard_map/joined/pallas_call | solution.py:478
  (1 shorter events, 0.0 us)
Async XLA Ops:
  2.6 6.4 %copy-start = (bf16[4,128,128]{2,1,0:T(8,128)(2,1)S(1)}, bf16[4,128,128]{2,1,0:T(8,128)(2,1)}, u32[]{:S(2)}) copy-start(bf16[4,128,128]{2,1,0:T(8,128)(2,1)} %speed.3) | copy-start | bytes 393220
  2.6 6.4 %copy-start.1 = (bf16[4,128,128]{2,1,0:T(8,128)(2,1)S(1)}, bf16[4,128,128]{2,1,0:T(8,128)(2,1)}, u32[]{:S(2)}) copy-start(bf16[4,128,128]{2,1,0:T(8,128)(2,1)} %imped.3) | copy-start | bytes 393220
  2.6 22.6 %all-to-all-start = ((bf16[64,4,8,128]{3,2,1,0:T(8,128)(2,1)}), bf16[64,4,8,128]{3,2,1,0:T(8,128)(2,1)S(1)}, u32[]{:S(2)}, u32[]{:S(2)}) async-start(bf16[64,4,8,128]{3,2,1,0:T(8,128)(2,1)} %bitcast.3), calls=%async_computation | async-start | bytes 1048576 | tf_op jit(solution)/shard_map/all_to_all | solution.py:442
  9.2 7.4 %collective-permute-start = (bf16[4,128,128]{2,1,0:T(8,128)(2,1)S(1)}, bf16[4,128,128]{2,1,0:T(8,128)(2,1)S(1)}, u32[]{:S(2)}, u32[]{:S(2)}) collective-permute-start(bf16[4,128,128]{2,1,0:T(8,128)(2,1)S(1)} %get-tuple-element.19), channel_id=1, source_target_pairs={{0,2},{4,6},{8,10},{12,14},{16,18},{20,22},{24,26},{28,30},{2,0},{... | collective-permute-start | bytes 393224 | tf_op jit(solution)/shard_map/ppermute | solution.py:423
  10.7 12.7 %collective-permute-start.1 = (bf16[4,128,128]{2,1,0:T(8,128)(2,1)S(1)}, bf16[4,128,128]{2,1,0:T(8,128)(2,1)S(1)}, u32[]{:S(2)}, u32[]{:S(2)}) collective-permute-start(bf16[4,128,128]{2,1,0:T(8,128)(2,1)S(1)} %get-tuple-element.20), channel_id=1, source_target_pairs={{2,4},{6,8},{10,12},{14,16},{18,20},{22,24},{26,28},{4,2},{8,6},{1... | collective-permute-start | bytes 393224 | tf_op jit(solution)/shard_map/ppermute | solution.py:423
  26.0 4.0 %collective-permute-start.2 = (bf16[128,128]{1,0:T(8,128)(2,1)S(1)}, bf16[128,128]{1,0:T(8,128)(2,1)S(1)}, u32[]{:S(2)}, u32[]{:S(2)}) collective-permute-start(bf16[128,128]{1,0:T(8,128)(2,1)S(1)} %broadcast_select_fusion), channel_id=1, source_target_pairs={{0,1},{1,0},{2,3},{3,2},{4,5},{5,4},{6,7},{7,6},{8,9},{9,8},{10,11... | collective-permute-start | bytes 98312 | tf_op jit(solution)/shard_map/ppermute | solution.py:456
  30.9 7.9 %collective-permute-start.3 = (bf16[576,128]{1,0:T(8,128)(2,1)S(1)}, bf16[576,128]{1,0:T(8,128)(2,1)S(1)}, u32[]{:S(2)}, u32[]{:S(2)}) collective-permute-start(bf16[576,128]{1,0:T(8,128)(2,1)S(1)} %get-tuple-element.34), channel_id=1, source_target_pairs={{0,2},{4,6},{8,10},{12,14},{16,18},{20,22},{24,26},{28,30},{2,0},{... | collective-permute-start | bytes 442376 | tf_op jit(solution)/shard_map/ppermute | solution.py:423
  32.9 7.9 %collective-permute-start.4 = (bf16[576,128]{1,0:T(8,128)(2,1)S(1)}, bf16[576,128]{1,0:T(8,128)(2,1)S(1)}, u32[]{:S(2)}, u32[]{:S(2)}) collective-permute-start(bf16[576,128]{1,0:T(8,128)(2,1)S(1)} %get-tuple-element.35), channel_id=1, source_target_pairs={{2,4},{6,8},{10,12},{14,16},{18,20},{22,24},{26,28},{4,2},{8,6},{1... | collective-permute-start | bytes 442376 | tf_op jit(solution)/shard_map/ppermute | solution.py:423

commit v7 on v6

--- a/solution.py
+++ b/solution.py
@@ -198,30 +198,42 @@
         self.ref[i] = value
 
 
-def pack_kernel(steps, layers, src, speed, imped, coef_near, coef_far, low, high, own):
+def field_block(steps, src, fields, f, i):
+    return brick_block(src, f, i).astype(jnp.bfloat16) if f < steps else fields[f - steps][i]
+
+
+def picked(pick, block):
+    return lax.dot_general(pick, block, (((1,), (1,)), ((), ())), preferred_element_type=jnp.float32)
+
+
+def pack_kernel(steps, layers, src, speed, imped, coef_near, coef_far, low, high):
     lanes = src.shape[-1]
     rows = layers * EDGE
     row, lane = iota((rows, lanes), 0), iota((rows, lanes), 1)
-    wrow, wlane = iota((WIDE, lanes), 0), iota((WIDE, lanes), 1)
-    half = WIDE // 2
-    at_low = (wrow >= EDGE) & (wrow < half) & (wlane == wrow - EDGE)
-    at_high = (wrow >= half) & (wrow < half + OWN) & (wlane == wrow + (lanes - OWN - half))
-    wide = jnp.where(at_low | at_high, 1.0, 0.0)
+    fields = speed, imped, coef_near, coef_far
     for f in range(steps + 4):
         total = None
         for i in range(layers):
             mine = (row >> 2) == i
             picks = [mine & (lane == base + (row & 3)) for base in (0, lanes - EDGE)]
-            pick = jnp.concatenate([wide] + [jnp.where(p, 1.0, 0.0) for p in picks], 0).astype(jnp.bfloat16)
-            if f < steps:
-                block = brick_block(src, f, i).astype(jnp.bfloat16)
-            else:
-                block = (speed, imped, coef_near, coef_far)[f - steps][i]
-            part = lax.dot_general(pick, block, (((1,), (1,)), ((), ())), preferred_element_type=jnp.float32)
-            own[f, i * WIDE : (i + 1) * WIDE, :] = part[:WIDE]
-            total = part[WIDE:] if total is None else total + part[WIDE:]
+            pick = jnp.concatenate([jnp.where(p, 1.0, 0.0) for p in picks], 0).astype(jnp.bfloat16)
+            part = picked(pick, field_block(steps, src, fields, f, i))
+            total = part if total is None else total + part
         low[f * rows : (f + 1) * rows, :] = total[:rows].astype(jnp.bfloat16)
         high[f * rows : (f + 1) * rows, :] = total[rows:].astype(jnp.bfloat16)
+
+
+def own_kernel(steps, layers, src, speed, imped, coef_near, coef_far, own):
+    lanes = src.shape[-1]
+    wrow, wlane = iota((WIDE, lanes), 0), iota((WIDE, lanes), 1)
+    half = WIDE // 2
+    at_low = (wrow >= EDGE) & (wrow < half) & (wlane == wrow - EDGE)
+    at_high = (wrow >= half) & (wrow < half + OWN) & (wlane == wrow + (lanes - OWN - half))
+    wide = jnp.where(at_low | at_high, 1.0, 0.0).astype(jnp.bfloat16)
+    fields = speed, imped, coef_near, coef_far
+    for f in range(steps + 4):
+        for i in range(layers):
+            own[f, i * WIDE : (i + 1) * WIDE, :] = picked(wide, field_block(steps, src, fields, f, i))
 
 
 def strip_rows(message, at, lanes):
@@ -447,16 +459,16 @@
         return pl.pallas_call(kernel, out_shape=outs, scratch_shapes=scratch, compiler_params=params, name=name)(*args)
 
     edge = sds(((steps + 4) * layers * EDGE, y), bf16)
-    low, high, own = call(
-        functools.partial(pack_kernel, steps, layers),
-        (edge, edge, sds((steps + 4, layers * WIDE, y), jnp.float32)), [],
-        relaid, speed, impedance, coef_near, coef_far, name="pack",
-    )
+    fields = relaid, speed, impedance, coef_near, coef_far
+    low, high = call(functools.partial(pack_kernel, steps, layers), (edge, edge), [], *fields, name="pack")
     if gy_size == 2:
         left = right = lax.ppermute(jnp.where(lax.axis_index("gy") == 0, high, low), "gy", [(0, 1), (1, 0)])
     else:
         left, right = shifted(high, "gy", 1), shifted(low, "gy", -1)
 
+    own = call(
+        functools.partial(own_kernel, steps, layers), sds((steps + 4, layers * WIDE, y), jnp.float32), [], *fields, name="own"
+    )
     whole = pltpu.VMEM((layers, y, lanes), jnp.float32)
     whole_velocity = pltpu.VMEM((3, layers, y, lanes), jnp.float32)
     series = [pltpu.VMEM((128, y), jnp.float32), pltpu.VMEM((y, 128), jnp.float32)]

time: 44.6 us -> 44.4 us (level)
  the two profiles are of different devices: /device:TPU:8 before, /device:TPU:10 now
where the time goes in v7:
time: 44.4 us; the launch traced here: 44.1 us
  waiting for transfers between devices  19.9 us (45%)
  starting transfers between devices  15.1 us (34%)
  Pallas kernels  6.54 us (15%)
  local copies, waits for them, and re-layouts  1.93 us (4%)
  between operations  0.7 us (2%)
    ppermute x4, waiting for transfers between devices, swapped(): return lax.ppermute(block, axis, pairs + [(j, i) for i, j in pairs])  16.1 us
    ppermute x4, starting transfers between devices, swapped(): return lax.ppermute(block, axis, pairs + [(j, i) for i, j in pairs])  8.06 us
    all_to_all x1, starting transfers between devices, on_device(): lax.all_to_all(source.transpose(1, 0, 2, 3), xs, split_axis=0, concat_axi...  6.43 us
    pallas_call x1, Pallas kernels, on_device(): pl.pallas_call(functools.partial(joined_kernel, steps, layers), in_specs=...  3.46 us
    pallas_call x4, Pallas kernels, call(): pl.pallas_call(kernel, out_shape=outs, scratch_shapes=scratch, compiler_p...  2.92 us
    ppermute x1, waiting for transfers between devices, on_device(): lax.ppermute(jnp.where(lax.axis_index('gy') == 0, high, low), 'gy', [(0,...  1.95 us
    unnamed x5, local copies, waits for them, and re-layouts  1.93 us
    all_to_all x1, waiting for transfers between devices, on_device(): lax.all_to_all(source.transpose(1, 0, 2, 3), xs, split_axis=0, concat_axi...  1.8 us
  transfers between devices with their start and end apart: 6, of which 6 were waited for; matrix products, arithmetic and copies ran while one was open for 0% of the time, Pallas kernels for 4%

profile of v7, /device:TPU:10, one launch (start us, length us, event | category | flops | bytes accessed | tf_op | source)
XLA Modules:
  0.0 44.1 jit_solution(4699221702369140759)
XLA Ops:
  0.6 1.9 %copy.8 = bf16[4,64,8,128]{3,2,0,1:T(8,128)(2,1)} copy(bf16[4,64,8,128]{3,2,1,0:T(8,128)(2,1)} %param.3) | data formatting | bytes 1048576 | tf_op args[0]
  2.6 0.0 copy-start
  2.6 0.0 copy-start.1
  2.6 6.4 %all-to-all-start = ((bf16[64,4,8,128]{3,2,1,0:T(8,128)(2,1)}), bf16[64,4,8,128]{3,2,1,0:T(8,128)(2,1)S(1)}, u32[]{:S(2)}, u32[]{:S(2)}) async-start(bf16[64,4,8,128]{3,2,1,0:T(8,128)(2,1)} %bitcast.3), calls=%async_computation | async-start | bytes 1048576 | tf_op jit(solution)/shard_map/all_to_all | solution.py:454
  9.0 0.0 copy-done
  9.0 0.0 copy-done.1
  9.0 0.2 coefficients.1
  9.2 1.5 %collective-permute-start = (bf16[4,128,128]{2,1,0:T(8,128)(2,1)S(1)}, bf16[4,128,128]{2,1,0:T(8,128)(2,1)S(1)}, u32[]{:S(2)}, u32[]{:S(2)}) collective-permute-start(bf16[4,128,128]{2,1,0:T(8,128)(2,1)S(1)} %get-tuple-element.18), channel_id=1, source_target_pairs={{0,2},{4,6},{8,10},{12,14},{16,18},{20,22},{24,26},{28,30},{2,0},{... | collective-permute-start | bytes 393224 | tf_op jit(solution)/shard_map/ppermute | solution.py:435
  10.7 2.0 %collective-permute-start.1 = (bf16[4,128,128]{2,1,0:T(8,128)(2,1)S(1)}, bf16[4,128,128]{2,1,0:T(8,128)(2,1)S(1)}, u32[]{:S(2)}, u32[]{:S(2)}) collective-permute-start(bf16[4,128,128]{2,1,0:T(8,128)(2,1)S(1)} %get-tuple-element.19), channel_id=1, source_target_pairs={{2,4},{6,8},{10,12},{14,16},{18,20},{22,24},{26,28},{4,2},{8,6},{1... | collective-permute-start | bytes 393224 | tf_op jit(solution)/shard_map/ppermute | solution.py:435
  12.7 3.9 %collective-permute-done.coef_near = bf16[4,128,128]{2,1,0:T(8,128)(2,1)S(1)} collective-permute-done((bf16[4,128,128]{2,1,0:T(8,128)(2,1)S(1)}, bf16[4,128,128]{2,1,0:T(8,128)(2,1)S(1)}, u32[]{:S(2)}, u32[]{:S(2)}) %collective-permute-start) | collective-permute-done | bytes 131104 | tf_op jit(solution)/shard_map/ppermute | solution.py:435
  16.6 6.8 %collective-permute-done.1.coef_far = bf16[4,128,128]{2,1,0:T(8,128)(2,1)S(1)} collective-permute-done((bf16[4,128,128]{2,1,0:T(8,128)(2,1)S(1)}, bf16[4,128,128]{2,1,0:T(8,128)(2,1)S(1)}, u32[]{:S(2)}, u32[]{:S(2)}) %collective-permute-start.1) | collective-permute-done | bytes 131104 | tf_op jit(solution)/shard_map/ppermute | solution.py:435
  23.4 1.8 %all-to-all-done = bf16[64,4,8,128]{3,2,1,0:T(8,128)(2,1)S(1)} async-done(((bf16[64,4,8,128]{3,2,1,0:T(8,128)(2,1)}), bf16[64,4,8,128]{3,2,1,0:T(8,128)(2,1)S(1)}, u32[]{:S(2)}, u32[]{:S(2)}) %all-to-all-start) | async-done | bytes 524320 | tf_op jit(solution)/shard_map/all_to_all | solution.py:454
  25.2 0.6 %pack.1 = (bf16[128,128]{1,0:T(8,128)(2,1)S(1)}, bf16[128,128]{1,0:T(8,128)(2,1)S(1)}) custom-call(bf16[16,4,4,8,128]{4,3,2,1,0:T(8,128)(2,1)S(1)} %bitcast.4, bf16[4,128,128]{2,1,0:T(8,128)(2,1)S(1)} %copy-done, bf16[4,128,128]{2,1,0:T(8,128)(2,1)S(1)} %copy-done.1, bf16[4,128,128]{2,1,0:T(8,128)(2,1)S(1)} %collective-permute-done.coef_near, ...), custom_call_target="tpu_custom_call" | custom-call | tf_op jit(solution)/shard_map/pack/pallas_call | solution.py:459
  25.9 0.6 %collective-permute-start.2 = (bf16[128,128]{1,0:T(8,128)(2,1)S(1)}, bf16[128,128]{1,0:T(8,128)(2,1)S(1)}, u32[]{:S(2)}, u32[]{:S(2)}) collective-permute-start(bf16[128,128]{1,0:T(8,128)(2,1)S(1)} %broadcast_select_fusion), channel_id=1, source_target_pairs={{0,1},{1,0},{2,3},{3,2},{4,5},{5,4},{6,7},{7,6},{8,9},{9,8},{10,11... | collective-permute-start | bytes 98312 | tf_op jit(solution)/shard_map/ppermute | solution.py:465
  26.5 0.6 %own.1 = f32[8,128,128]{2,1,0:T(8,128)S(1)} custom-call(bf16[16,4,4,8,128]{4,3,2,1,0:T(8,128)(2,1)S(1)} %bitcast.5, bf16[4,128,128]{2,1,0:T(8,128)(2,1)S(1)} %copy-done, bf16[4,128,128]{2,1,0:T(8,128)(2,1)S(1)} %copy-done.1, bf16[4,128,128]{2,1,0:T(8,128)(2,1)S(1)} %collective-permute-done.coef_near, bf16[4,128,128]{2,1,0:T(8,128)(2,1)S(1)} %collective-permute-done.1.coef_far), custom_call_target="tpu_custom_call" | custom-call | tf_op jit(solution)/shard_map/own/pallas_call | solution.py:459
  27.1 0.8 %cut.1 = (bf16[512,128]{1,0:T(8,128)(2,1)S(1)}, bf16[512,128]{1,0:T(8,128)(2,1)S(1)}) custom-call(bf16[16,4,4,8,128]{4,3,2,1,0:T(8,128)(2,1)S(1)} %bitcast.6, f32[4,128,128]{2,1,0:T(8,128)S(1)} %get-tuple-element.23.stiff, f32[4,128,128]{2,1,0:T(8,128)S(1)} %get-tuple-element.24.buoy), custom_call_target="tpu_custom_call" | custom-call | tf_op jit(solution)/shard_map/cut/pallas_call | solution.py:459
  27.9 1.9 %collective-permute-done.2.left.right = bf16[128,128]{1,0:T(8,128)(2,1)S(1)} collective-permute-done((bf16[128,128]{1,0:T(8,128)(2,1)S(1)}, bf16[128,128]{1,0:T(8,128)(2,1)S(1)}, u32[]{:S(2)}, u32[]{:S(2)}) %collective-permute-start.2) | collective-permute-done | bytes 32800 | tf_op jit(solution)/shard_map/ppermute | solution.py:465
  29.8 0.9 %edge.1 = (bf16[576,128]{1,0:T(8,128)(2,1)S(1)}, bf16[576,128]{1,0:T(8,128)(2,1)S(1)}, f32[8,64,128]{2,1,0:T(8,128)S(1)}) custom-call(f32[8,128,128]{2,1,0:T(8,128)S(1)} %own.1, bf16[128,128]{1,0:T(8,128)(2,1)S(1)} %collective-permute-done.2.left.right, bf16[128,128]{1,0:T(8,128)(2,1)S(1)} %collective-permute-done.2.left.right, ...), custom_call_target="tpu_custom_call" | custom-call | tf_op jit(solution)/shard_map/edge/pallas_call | solution.py:459
  30.7 2.0 %collective-permute-start.3 = (bf16[576,128]{1,0:T(8,128)(2,1)S(1)}, bf16[576,128]{1,0:T(8,128)(2,1)S(1)}, u32[]{:S(2)}, u32[]{:S(2)}) collective-permute-start(bf16[576,128]{1,0:T(8,128)(2,1)S(1)} %get-tuple-element.32), channel_id=1, source_target_pairs={{0,2},{4,6},{8,10},{12,14},{16,18},{20,22},{24,26},{28,30},{2,0},{... | collective-permute-start | bytes 442376 | tf_op jit(solution)/shard_map/ppermute | solution.py:435
  32.7 2.5 %collective-permute-start.4 = (bf16[576,128]{1,0:T(8,128)(2,1)S(1)}, bf16[576,128]{1,0:T(8,128)(2,1)S(1)}, u32[]{:S(2)}, u32[]{:S(2)}) collective-permute-start(bf16[576,128]{1,0:T(8,128)(2,1)S(1)} %get-tuple-element.33), channel_id=1, source_target_pairs={{2,4},{6,8},{10,12},{14,16},{18,20},{22,24},{26,28},{4,2},{8,6},{1... | collective-permute-start | bytes 442376 | tf_op jit(solution)/shard_map/ppermute | solution.py:435
  35.2 3.4 %collective-permute-done.3.near = bf16[576,128]{1,0:T(8,128)(2,1)S(1)} collective-permute-done((bf16[576,128]{1,0:T(8,128)(2,1)S(1)}, bf16[576,128]{1,0:T(8,128)(2,1)S(1)}, u32[]{:S(2)}, u32[]{:S(2)}) %collective-permute-start.3) | collective-permute-done | bytes 147488 | tf_op jit(solution)/shard_map/ppermute | solution.py:435
  38.6 2.1 %collective-permute-done.4.far = bf16[576,128]{1,0:T(8,128)(2,1)S(1)} collective-permute-done((bf16[576,128]{1,0:T(8,128)(2,1)S(1)}, bf16[576,128]{1,0:T(8,128)(2,1)S(1)}, u32[]{:S(2)}, u32[]{:S(2)}) %collective-permute-start.4) | collective-permute-done | bytes 147488 | tf_op jit(solution)/shard_map/ppermute | solution.py:435
  40.7 3.5 %joined.1 = (f32[4,128,128]{2,1,0:T(8,128)}, f32[3,4,128,128]{3,2,1,0:T(8,128)}) custom-call(bf16[16,4,4,8,128]{4,3,2,1,0:T(8,128)(2,1)S(1)} %bitcast.7, f32[4,128,128]{2,1,0:T(8,128)S(1)} %get-tuple-element.23.stiff, f32[4,128,128]{2,1,0:T(8,128)S(1)} %get-tuple-element.24.buoy, f32[8,64,128]{2,1,0:T(8,128)S(1)} %get-tuple-element.31.strips, ...), custom_call_target="tpu_custom_call" | custom-call | tf_op jit(solution)/shard_map/joined/pallas_call | solution.py:490
  (1 shorter events, 0.0 us)
Async XLA Ops:
  2.6 6.4 %copy-start = (bf16[4,128,128]{2,1,0:T(8,128)(2,1)S(1)}, bf16[4,128,128]{2,1,0:T(8,128)(2,1)}, u32[]{:S(2)}) copy-start(bf16[4,128,128]{2,1,0:T(8,128)(2,1)} %speed.5) | copy-start | bytes 393220
  2.6 6.4 %copy-start.1 = (bf16[4,128,128]{2,1,0:T(8,128)(2,1)S(1)}, bf16[4,128,128]{2,1,0:T(8,128)(2,1)}, u32[]{:S(2)}) copy-start(bf16[4,128,128]{2,1,0:T(8,128)(2,1)} %imped.5) | copy-start | bytes 393220
  2.6 22.6 %all-to-all-start = ((bf16[64,4,8,128]{3,2,1,0:T(8,128)(2,1)}), bf16[64,4,8,128]{3,2,1,0:T(8,128)(2,1)S(1)}, u32[]{:S(2)}, u32[]{:S(2)}) async-start(bf16[64,4,8,128]{3,2,1,0:T(8,128)(2,1)} %bitcast.3), calls=%async_computation | async-start | bytes 1048576 | tf_op jit(solution)/shard_map/all_to_all | solution.py:454
  9.2 7.4 %collective-permute-start = (bf16[4,128,128]{2,1,0:T(8,128)(2,1)S(1)}, bf16[4,128,128]{2,1,0:T(8,128)(2,1)S(1)}, u32[]{:S(2)}, u32[]{:S(2)}) collective-permute-start(bf16[4,128,128]{2,1,0:T(8,128)(2,1)S(1)} %get-tuple-element.18), channel_id=1, source_target_pairs={{0,2},{4,6},{8,10},{12,14},{16,18},{20,22},{24,26},{28,30},{2,0},{... | collective-permute-start | bytes 393224 | tf_op jit(solution)/shard_map/ppermute | solution.py:435
  10.7 12.7 %collective-permute-start.1 = (bf16[4,128,128]{2,1,0:T(8,128)(2,1)S(1)}, bf16[4,128,128]{2,1,0:T(8,128)(2,1)S(1)}, u32[]{:S(2)}, u32[]{:S(2)}) collective-permute-start(bf16[4,128,128]{2,1,0:T(8,128)(2,1)S(1)} %get-tuple-element.19), channel_id=1, source_target_pairs={{2,4},{6,8},{10,12},{14,16},{18,20},{22,24},{26,28},{4,2},{8,6},{1... | collective-permute-start | bytes 393224 | tf_op jit(solution)/shard_map/ppermute | solution.py:435
  25.9 4.0 %collective-permute-start.2 = (bf16[128,128]{1,0:T(8,128)(2,1)S(1)}, bf16[128,128]{1,0:T(8,128)(2,1)S(1)}, u32[]{:S(2)}, u32[]{:S(2)}) collective-permute-start(bf16[128,128]{1,0:T(8,128)(2,1)S(1)} %broadcast_select_fusion), channel_id=1, source_target_pairs={{0,1},{1,0},{2,3},{3,2},{4,5},{5,4},{6,7},{7,6},{8,9},{9,8},{10,11... | collective-permute-start | bytes 98312 | tf_op jit(solution)/shard_map/ppermute | solution.py:465
  30.7 7.9 %collective-permute-start.3 = (bf16[576,128]{1,0:T(8,128)(2,1)S(1)}, bf16[576,128]{1,0:T(8,128)(2,1)S(1)}, u32[]{:S(2)}, u32[]{:S(2)}) collective-permute-start(bf16[576,128]{1,0:T(8,128)(2,1)S(1)} %get-tuple-element.32), channel_id=1, source_target_pairs={{0,2},{4,6},{8,10},{12,14},{16,18},{20,22},{24,26},{28,30},{2,0},{... | collective-permute-start | bytes 442376 | tf_op jit(solution)/shard_map/ppermute | solution.py:435
  32.7 7.9 %collective-permute-start.4 = (bf16[576,128]{1,0:T(8,128)(2,1)S(1)}, bf16[576,128]{1,0:T(8,128)(2,1)S(1)}, u32[]{:S(2)}, u32[]{:S(2)}) collective-permute-start(bf16[576,128]{1,0:T(8,128)(2,1)S(1)} %get-tuple-element.33), channel_id=1, source_target_pairs={{2,4},{6,8},{10,12},{14,16},{18,20},{22,24},{26,28},{4,2},{8,6},{1... | collective-permute-start | bytes 442376 | tf_op jit(solution)/shard_map/ppermute | solution.py:435
